TPU v7x, 32 devices: a whole 2x2x4 slice. The times are simulated.
32 devices in a mesh: section: 2 (over core), dp: 16 (over z, y, x).
Axes of the slice: x: 2, y: 2, z: 4, core: 2. Of those that a mesh axis runs over, the one named last changes fastest.
Arguments:
- patches: bfloat16 [12800, 1024], P('dp'), may hold values from -6 to 6
- live: int32 [256], P('dp'), may hold values 0 or 1
- cotangent: bfloat16 [12800, 1024], P('dp'), may hold values from -6 to 6
- w_qkv: float32 [2, 1024, 3072], P('section', 'dp'), may hold values from -0.25 to 0.25
- w_proj: float32 [2, 1024, 1024], P('section', 'dp'), may hold values from -0.5 to 0.5
- w_in: float32 [2, 1024, 4096], P('section', 'dp'), may hold values from -0.1875 to 0.1875
- w_out: float32 [2, 4096, 1024], P('section', 'dp'), may hold values from -0.125 to 0.125
- vectors: float32 [2, 12, 1024], P('section', None, 'dp'), may hold values from -1.2 to 2.4, as said below
- first_qkv: float32 [2, 1024, 3072], P('section', 'dp'), may hold values from -0.0001454472 to 0.0001454472
- first_proj: float32 [2, 1024, 1024], P('section', 'dp'), may hold values from -7.571223e-05 to 7.571223e-05
- first_in: float32 [2, 1024, 4096], P('section', 'dp'), may hold values from -0.00013349262 to 0.00013349262
- first_out: float32 [2, 4096, 1024], P('section', 'dp'), may hold values from -0.00011356835 to 0.00011356835
- first_vectors: float32 [2, 12, 1024], P('section', None, 'dp'), may hold values from -0.00018529574 to 0.00018529574
- second_qkv: float32 [2, 1024, 3072], P('section', 'dp'), may hold values from 2.5406504e-09 to 1.0162601e-08
- second_proj: float32 [2, 1024, 1024], P('section', 'dp'), may hold values from 6.748603e-10 to 2.6994411e-09
- second_in: float32 [2, 1024, 4096], P('section', 'dp'), may hold values from 2.103976e-09 to 8.415904e-09
- second_out: float32 [2, 4096, 1024], P('section', 'dp'), may hold values from 1.5085112e-09 to 6.034045e-09
- second_vectors: float32 [2, 12, 1024], P('section', None, 'dp'), may hold values from 4.1682546e-09 to 1.6673019e-08
Outputs:
- blocks: bfloat16 [2, 12800, 1024], P('section', 'dp')
- input_grad: bfloat16 [2, 12800, 1024], P('section', 'dp')
- grad_qkv: float32 [2, 1024, 3072], P('section', 'dp')
- grad_proj: float32 [2, 1024, 1024], P('section', 'dp')
- grad_in: float32 [2, 1024, 4096], P('section', 'dp')
- grad_out: float32 [2, 4096, 1024], P('section', 'dp')
- grad_vectors: float32 [2, 12, 1024], P('section', None, 'dp')
- grad_norm: float32 [], replicated
- new_qkv: float32 [2, 1024, 3072], P('section', 'dp')
- new_proj: float32 [2, 1024, 1024], P('section', 'dp')
- new_in: float32 [2, 1024, 4096], P('section', 'dp')
- new_out: float32 [2, 4096, 1024], P('section', 'dp')
- new_vectors: float32 [2, 12, 1024], P('section', None, 'dp')
- lowered_qkv: bfloat16 [2, 1024, 3072], P('section', 'dp')
- lowered_proj: bfloat16 [2, 1024, 1024], P('section', 'dp')
- lowered_in: bfloat16 [2, 1024, 4096], P('section', 'dp')
- lowered_out: bfloat16 [2, 4096, 1024], P('section', 'dp')
- lowered_vectors: bfloat16 [2, 12, 1024], P('section', None, 'dp')
- momentum_qkv: float32 [2, 1024, 3072], P('section', 'dp')
- momentum_proj: float32 [2, 1024, 1024], P('section', 'dp')
- momentum_in: float32 [2, 1024, 4096], P('section', 'dp')
- momentum_out: float32 [2, 4096, 1024], P('section', 'dp')
- momentum_vectors: float32 [2, 12, 1024], P('section', None, 'dp')
- variance_qkv: float32 [2, 1024, 3072], P('section', 'dp')
- variance_proj: float32 [2, 1024, 1024], P('section', 'dp')
- variance_in: float32 [2, 1024, 4096], P('section', 'dp')
- variance_out: float32 [2, 4096, 1024], P('section', 'dp')
- variance_vectors: float32 [2, 12, 1024], P('section', None, 'dp')
Inputs may be any that keep to these rules, and one draw needn't show every extreme that they name: `vectors`: rows 0 and 5 of each layer are positive gains.
All inputs are finite; a program needn't handle non-finite values. No bound on the sum of `live` on one device may be relied on, other than what follows from the above.
Results may differ from a plain program's by a relative error of at most 0.03.
Values may be sent and summed in bfloat16 or wider, within the bound.
No kernel may reach another device: no remote copies, remote signals or barrier semaphores. Data moves between devices by JAX's collectives and lax.ppermute only.
A program may use at most 320 MiB of HBM per device.

v0:
```python
import jax
import jax.numpy as jnp
from jax import lax
from jax.sharding import PartitionSpec as P

HEADS = 16
HEAD = 64
SEQ = 50
MICRO = 4
STEP = 10


norm_epsilon = 1e-06
clip_norm = 1.0
beta_one = 0.9
beta_two = 0.95
rate_matrix = 0.05
rate_vector = 1.0
decay_matrix = 0.1
epsilon = 1e-08


def from_behind(x, axis, by):
    count = lax.axis_size(axis)
    pairs = [(i, i + by) for i in range(count) if 0 <= i + by < count]
    return lax.ppermute(x, axis, pairs)


def normalize(inputs):
    centered = inputs - jnp.mean(inputs, axis=-1, keepdims=True)
    inverse = lax.rsqrt(jnp.mean(centered * centered, axis=-1, keepdims=True) + norm_epsilon)
    return (centered * inverse, inverse)


def normalize_back(upstream, scaled, inverse):
    return inverse * (
        upstream
        - jnp.mean(upstream, axis=-1, keepdims=True)
        - scaled * jnp.mean(upstream * scaled, axis=-1, keepdims=True)
    )


def layer_forward(inputs, params):
    w_qkv, w_proj, w_in, w_out, vectors = params
    rows_all = vectors.astype(jnp.float32)
    count_rows = inputs.shape[0]
    model_width = inputs.shape[1]
    count_images = count_rows // SEQ
    scaled_one, inverse_one = normalize(inputs)
    hidden = (scaled_one * rows_all[0] + rows_all[1]).astype(jnp.bfloat16)
    bias_all = jnp.concatenate([rows_all[2], jnp.zeros_like(rows_all[2]), rows_all[3]])
    packed = (jnp.dot(hidden, w_qkv, preferred_element_type=jnp.float32) + bias_all).astype(
        jnp.bfloat16
    )
    shaped = packed.reshape(count_images, SEQ, 3, HEADS, HEAD)
    queries = shaped[:, :, 0]
    key_part = shaped[:, :, 1]
    values = shaped[:, :, 2]
    scaling = HEAD ** (-0.5)
    scores = (
        jnp.einsum("ishd,ithd->ihst", queries, key_part, preferred_element_type=jnp.float32)
        * scaling
    )
    raised = jnp.exp(scores - jnp.max(scores, axis=-1, keepdims=True))
    attention = raised / jnp.sum(raised, axis=-1, keepdims=True)
    attention_low = attention.astype(jnp.bfloat16)
    mixed_low = jnp.einsum(
        "ihst,ithd->ishd", attention_low, values, preferred_element_type=jnp.float32
    )
    mixed_low = mixed_low.reshape(count_rows, model_width).astype(jnp.bfloat16)
    middle = inputs + (jnp.dot(mixed_low, w_proj, preferred_element_type=jnp.float32) + rows_all[4])
    scaled_two, inverse_two = normalize(middle)
    hidden_two = (scaled_two * rows_all[5] + rows_all[6]).astype(jnp.bfloat16)
    pre_act = jnp.dot(hidden_two, w_in, preferred_element_type=jnp.float32) + rows_all[
        8:12
    ].reshape(-1)
    active_low = jax.nn.gelu(pre_act, approximate=False).astype(jnp.bfloat16)
    output = middle + (jnp.dot(active_low, w_out, preferred_element_type=jnp.float32) + rows_all[7])
    remembered = (
        scaled_one,
        inverse_one,
        hidden,
        queries,
        key_part,
        values,
        attention,
        attention_low,
        mixed_low,
        scaled_two,
        inverse_two,
        hidden_two,
        pre_act,
        active_low,
    )
    return (output, remembered)


def layer_backward(inputs, upstream, params, early_hook=None):
    w_qkv, w_proj, w_in, w_out, vectors = params
    rows_all = vectors.astype(jnp.float32)
    remembered = layer_forward(inputs, params)[1]
    (
        scaled_one,
        inverse_one,
        hidden,
        queries,
        key_part,
        values,
        attention,
        attention_low,
        mixed_low,
        scaled_two,
        inverse_two,
        hidden_two,
        pre_act,
        active_low,
    ) = remembered
    count_rows = inputs.shape[0]
    model_width = inputs.shape[1]
    count_images = count_rows // SEQ
    scaling = HEAD ** (-0.5)
    grad_out_low = upstream.astype(jnp.bfloat16)
    grad_w_out = jnp.einsum(
        "nf,nd->fd", active_low, grad_out_low, preferred_element_type=jnp.float32
    )
    grad_b_out = jnp.sum(grad_out_low.astype(jnp.float32), axis=0)
    grad_active = jnp.einsum("nd,fd->nf", grad_out_low, w_out, preferred_element_type=jnp.float32)
    normal_cdf = 0.5 * (1.0 + lax.erf(pre_act * 0.7071067811865476))
    density = jnp.exp(-0.5 * pre_act * pre_act) * 0.3989422804014327
    grad_pre_low = (grad_active * (normal_cdf + pre_act * density)).astype(jnp.bfloat16)
    grad_w_in = jnp.einsum(
        "nd,nf->df", hidden_two, grad_pre_low, preferred_element_type=jnp.float32
    )
    grad_b_in = jnp.sum(grad_pre_low.astype(jnp.float32), axis=0)
    grad_hidden_two = jnp.einsum(
        "nf,df->nd", grad_pre_low, w_in, preferred_element_type=jnp.float32
    )
    grad_gain_two = jnp.sum(grad_hidden_two * scaled_two, axis=0)
    grad_shift_two = jnp.sum(grad_hidden_two, axis=0)
    grad_middle = upstream + normalize_back(grad_hidden_two * rows_all[5], scaled_two, inverse_two)
    grad_branch_low = grad_middle.astype(jnp.bfloat16)
    grad_w_proj = jnp.einsum(
        "nd,ne->de", mixed_low, grad_branch_low, preferred_element_type=jnp.float32
    )
    grad_b_proj = jnp.sum(grad_branch_low.astype(jnp.float32), axis=0)
    grad_mixed = jnp.einsum(
        "ne,de->nd", grad_branch_low, w_proj, preferred_element_type=jnp.float32
    )
    grad_mixed_low = grad_mixed.astype(jnp.bfloat16).reshape(count_images, SEQ, HEADS, HEAD)
    grad_attention = jnp.einsum(
        "ishd,ithd->ihst", grad_mixed_low, values, preferred_element_type=jnp.float32
    )
    grad_values = jnp.einsum(
        "ihst,ishd->ithd", attention_low, grad_mixed_low, preferred_element_type=jnp.float32
    )
    grad_scores_low = (
        attention * (grad_attention - jnp.sum(attention * grad_attention, axis=-1, keepdims=True))
    ).astype(jnp.bfloat16)
    grad_queries = (
        jnp.einsum("ihst,ithd->ishd", grad_scores_low, key_part, preferred_element_type=jnp.float32)
        * scaling
    )
    grad_keys = (
        jnp.einsum("ihst,ishd->ithd", grad_scores_low, queries, preferred_element_type=jnp.float32)
        * scaling
    )
    grad_packed_low = (
        jnp.stack([grad_queries, grad_keys, grad_values], axis=2)
        .reshape(count_rows, 3 * model_width)
        .astype(jnp.bfloat16)
    )
    grad_w_qkv = jnp.einsum(
        "nd,ne->de", hidden, grad_packed_low, preferred_element_type=jnp.float32
    )
    column_sums = jnp.sum(grad_packed_low.astype(jnp.float32), axis=0)
    grad_hidden = jnp.einsum(
        "ne,de->nd", grad_packed_low, w_qkv, preferred_element_type=jnp.float32
    )
    grad_gain_one = jnp.sum(grad_hidden * scaled_one, axis=0)
    grad_shift_one = jnp.sum(grad_hidden, axis=0)
    grad_entry = grad_middle + normalize_back(grad_hidden * rows_all[0], scaled_one, inverse_one)
    grad_rows = jnp.stack(
        [
            grad_gain_one,
            grad_shift_one,
            column_sums[:model_width],
            column_sums[2 * model_width :],
            grad_b_proj,
            grad_gain_two,
            grad_shift_two,
            grad_b_out,
        ]
    )
    grad_vectors = jnp.concatenate([grad_rows, grad_b_in.reshape(4, model_width)], axis=0)
    return (grad_entry, (grad_w_qkv, grad_w_proj, grad_w_in, grad_w_out, grad_vectors))


def adam_update(weight, grad, first, second, factor, rate, decay):
    clipped = grad * factor
    momentum = beta_one * first + (1.0 - beta_one) * clipped
    variance = beta_two * second + (1.0 - beta_two) * clipped * clipped
    corrected_m = momentum / (1.0 - beta_one**STEP)
    corrected_v = variance / (1.0 - beta_two**STEP)
    updated = weight - rate * (corrected_m / (jnp.sqrt(corrected_v) + epsilon) + decay * weight)
    return (updated, momentum, variance)


def body(
    patches,
    live,
    cotangent,
    w_qkv,
    w_proj,
    w_in,
    w_out,
    vectors,
    first_qkv,
    first_proj,
    first_in,
    first_out,
    first_vectors,
    second_qkv,
    second_proj,
    second_in,
    second_out,
    second_vectors,
):
    section_index = lax.axis_index("section")
    at_first = section_index == 0
    masters = (w_qkv[0], w_proj[0], w_in[0], w_out[0], vectors[0])
    lowered = tuple((m.astype(jnp.bfloat16) for m in masters))
    params = (
        lax.all_gather(lowered[0], "dp", axis=0, tiled=True),
        lax.all_gather(lowered[1], "dp", axis=0, tiled=True),
        lax.all_gather(lowered[2], "dp", axis=0, tiled=True),
        lax.all_gather(lowered[3], "dp", axis=0, tiled=True),
        lax.all_gather(lowered[4], "dp", axis=1, tiled=True),
    )
    tokens_mb = patches.shape[0] // MICRO
    images_mb = live.shape[0] // MICRO
    model_width = patches.shape[1]
    inputs_mb = patches.reshape(MICRO, tokens_mb, model_width)
    weighting = live.astype(jnp.float32).reshape(MICRO, images_mb, 1, 1)
    targets = (
        cotangent.astype(jnp.float32).reshape(MICRO, images_mb, SEQ, model_width) * weighting
    ).reshape(MICRO, tokens_mb, model_width)
    carried = jnp.zeros((tokens_mb, model_width), jnp.bfloat16)
    kept_inputs = []
    produced = []
    for tick_index in range(MICRO + 1):
        own_rows = inputs_mb[tick_index] if tick_index < MICRO else jnp.zeros_like(carried)
        entry_rows = jnp.where(at_first, own_rows, carried)
        kept_inputs.append(entry_rows)
        result = layer_forward(entry_rows.astype(jnp.float32), params)[0].astype(jnp.bfloat16)
        produced.append(result)
        if tick_index < MICRO:
            carried = from_behind(result, "section", 1)
    blocks = jnp.where(
        at_first, jnp.concatenate(produced[:MICRO], axis=0), jnp.concatenate(produced[1:], axis=0)
    )
    back_params = (
        lax.all_gather(lowered[0], "dp", axis=0, tiled=True),
        lax.all_gather(lowered[1], "dp", axis=0, tiled=True),
        lax.all_gather(lowered[2], "dp", axis=0, tiled=True),
        lax.all_gather(lowered[3], "dp", axis=0, tiled=True),
        lax.all_gather(lowered[4], "dp", axis=1, tiled=True),
    )
    totals = tuple((jnp.zeros(p.shape, jnp.float32) for p in back_params))
    returned = jnp.zeros((tokens_mb, model_width), jnp.bfloat16)
    grads_entry = []
    for tick_index in range(MICRO + 1):
        own_target = (
            targets[MICRO - 1 - tick_index]
            if tick_index < MICRO
            else jnp.zeros((tokens_mb, model_width), jnp.float32)
        )
        incoming = jnp.where(at_first, returned.astype(jnp.float32), own_target)
        entry_rows = kept_inputs[MICRO - tick_index].astype(jnp.float32)
        grad_entry, terms = layer_backward(entry_rows, incoming, back_params)
        totals = tuple((a + b for a, b in zip(totals, terms)))
        grad_low = grad_entry.astype(jnp.bfloat16)
        grads_entry.append(grad_low)
        if tick_index < MICRO:
            returned = from_behind(grad_low, "section", -1)
    shards = (
        lax.psum_scatter(totals[0], "dp", scatter_dimension=0, tiled=True),
        lax.psum_scatter(totals[1], "dp", scatter_dimension=0, tiled=True),
        lax.psum_scatter(totals[2], "dp", scatter_dimension=0, tiled=True),
        lax.psum_scatter(totals[3], "dp", scatter_dimension=0, tiled=True),
        lax.psum_scatter(totals[4], "dp", scatter_dimension=1, tiled=True),
    )
    first_grads = jnp.concatenate([grads_entry[MICRO - k] for k in range(MICRO)], axis=0)
    second_grads = jnp.concatenate([grads_entry[MICRO - 1 - k] for k in range(MICRO)], axis=0)
    input_grad = jnp.where(at_first, first_grads, second_grads)
    local_sum = sum((jnp.sum(s * s) for s in shards))
    global_sum = lax.psum(local_sum, ("section", "dp"))
    grad_norm = jnp.sqrt(global_sum)
    factor = clip_norm / jnp.maximum(grad_norm, clip_norm)
    firsts = (first_qkv[0], first_proj[0], first_in[0], first_out[0], first_vectors[0])
    seconds = (second_qkv[0], second_proj[0], second_in[0], second_out[0], second_vectors[0])
    rates = (rate_matrix, rate_matrix, rate_matrix, rate_matrix, rate_vector)
    decays = (decay_matrix, decay_matrix, decay_matrix, decay_matrix, 0.0)
    results = [
        adam_update(w, g, f, s, factor, r, d)
        for w, g, f, s, r, d in zip(masters, shards, firsts, seconds, rates, decays)
    ]
    news = tuple((item[0][None] for item in results))
    momenta = tuple((item[1][None] for item in results))
    variances = tuple((item[2][None] for item in results))
    copies = tuple((n.astype(jnp.bfloat16) for n in news))
    grads_out = tuple((s[None] for s in shards))
    return (
        blocks[None],
        input_grad[None],
        grads_out[0],
        grads_out[1],
        grads_out[2],
        grads_out[3],
        grads_out[4],
        grad_norm,
        news[0],
        news[1],
        news[2],
        news[3],
        news[4],
        copies[0],
        copies[1],
        copies[2],
        copies[3],
        copies[4],
        momenta[0],
        momenta[1],
        momenta[2],
        momenta[3],
        momenta[4],
        variances[0],
        variances[1],
        variances[2],
        variances[3],
        variances[4],
    )


def solution(mesh):
    in_specs = (
        P("dp", None),
        P("dp"),
        P("dp", None),
        P("section", "dp", None),
        P("section", "dp", None),
        P("section", "dp", None),
        P("section", "dp", None),
        P("section", None, "dp"),
        P("section", "dp", None),
        P("section", "dp", None),
        P("section", "dp", None),
        P("section", "dp", None),
        P("section", None, "dp"),
        P("section", "dp", None),
        P("section", "dp", None),
        P("section", "dp", None),
        P("section", "dp", None),
        P("section", None, "dp"),
    )
    out_specs = (
        P("section", "dp", None),
        P("section", "dp", None),
        P("section", "dp", None),
        P("section", "dp", None),
        P("section", "dp", None),
        P("section", "dp", None),
        P("section", None, "dp"),
        P(),
        P("section", "dp", None),
        P("section", "dp", None),
        P("section", "dp", None),
        P("section", "dp", None),
        P("section", None, "dp"),
        P("section", "dp", None),
        P("section", "dp", None),
        P("section", "dp", None),
        P("section", "dp", None),
        P("section", None, "dp"),
        P("section", "dp", None),
        P("section", "dp", None),
        P("section", "dp", None),
        P("section", "dp", None),
        P("section", None, "dp"),
        P("section", "dp", None),
        P("section", "dp", None),
        P("section", "dp", None),
        P("section", "dp", None),
        P("section", None, "dp"),
    )
    return jax.shard_map(body, mesh=mesh, in_specs=in_specs, out_specs=out_specs, check_vma=False)
```

profile of v0, /device:TPU:0, one launch (start us, length us, event | category | flops | bytes accessed | tf_op | source)
XLA Modules:
  0.0 1972.1 jit_solution(16947912519660905992)
XLA Ops:
  14.3 43.3 %all-gather = bf16[16,64,12]{1,2,0:T(8,128)(2,1)S(1)} all-gather(bf16[1,64,12]{1,2,0:T(8,128)(2,1)S(1)} %bitcast.657), channel_id=1, replica_groups=mesh['section'=2,'dp'=16] {'dp'}, dimensions={0}, use_global_device_ids=true | all-gather | bytes 26112 | tf_op jit(solution)/shard_map/all_gather | solution.py:237
  58.8 50.0 %all-gather.6.cloned.1.call-done = bf16[1024,3072]{1,0:T(8,128)(2,1)} async-done(((bf16[64,3072]{1,0:T(8,128)(2,1)}), bf16[1024,3072]{1,0:T(8,128)(2,1)}) %all-gather.6.cloned.1.call-update) | async-done | bytes 6291472 | tf_op jit(solution)/shard_map/all_gather | solution.py:233
  123.6 47.5 %all-gather.8.cloned.1.call-done = bf16[1024,1024]{1,0:T(8,128)(2,1)} async-done(((bf16[64,1024]{1,0:T(8,128)(2,1)}), bf16[1024,1024]{1,0:T(8,128)(2,1)}) %all-gather.8.cloned.1.call-update) | async-done | bytes 2097168 | tf_op jit(solution)/shard_map/all_gather | solution.py:234
  173.8 112.2 %all-gather.10.cloned.1.call-done = bf16[1024,4096]{1,0:T(8,128)(2,1)} async-done(((bf16[64,4096]{1,0:T(8,128)(2,1)}), bf16[1024,4096]{1,0:T(8,128)(2,1)}) %all-gather.10.cloned.1.call-update) | async-done | bytes 8388624 | tf_op jit(solution)/shard_map/all_gather | solution.py:235
  286.0 7.0 convolution_add_fusion.4
  293.0 107.2 %all-gather.12.cloned.1.call-done = bf16[4096,1024]{1,0:T(8,128)(2,1)} async-done(((bf16[256,1024]{1,0:T(8,128)(2,1)}), bf16[4096,1024]{1,0:T(8,128)(2,1)}) %all-gather.12.cloned.1.call-update) | async-done | bytes 8388624 | tf_op jit(solution)/shard_map/all_gather | solution.py:236
  400.3 11.6 fusion.109
  435.5 13.3 fusion.20
  477.2 13.1 fusion.23
  525.5 12.7 fusion.26
  580.5 12.2 fusion.29
  599.0 7.0 multiply_reduce_fusion.16
  719.6 7.1 convert_reduce_fusion.6
  804.6 7.0 fusion.215
  813.6 9.2 add_add_fusion.3
  824.1 6.6 fusion.289
  837.3 6.6 fusion.283
  850.5 22.4 %add_add_fusion.2 = f32[1024,3072]{1,0:T(8,128)} fusion(f32[1024,3072]{1,0:T(8,128)} %fusion.280, f32[1024,3072]{1,0:T(8,128)} %fusion.283, f32[1024,3072]{1,0:T(8,128)} %fusion.289, f32[1024,3072]{1,0:T(8,128)} %fusion.286, bf16[200,3072]{1,0:T(8,128)(2,1)S(1)} %copy-done.42, f32[1024]{0:T(1024)S(1)} %bitcast.628, f32[1024]{0:T(1024)S(1)} %bitcast.616, ...), kind=kOutput, calls=%fused_computation.7 | convolution fusion | flops 1272307712 | bytes 64562752 | tf_op jit(solution)/shard_map/nd,ne->de/dot_general | solution.py:172
  874.1 9.9 fusion.297
  884.0 8.3 fusion.296
  892.3 8.3 fusion.295
  900.7 8.3 fusion.294
  909.0 29.4 %add_add_fusion.1 = f32[1024,4096]{1,0:T(8,128)} fusion(f32[1024,4096]{1,0:T(8,128)} %fusion.294, f32[1024,4096]{1,0:T(8,128)} %fusion.295, f32[1024,4096]{1,0:T(8,128)} %fusion.297, f32[1024,4096]{1,0:T(8,128)} %fusion.296, bf16[200,4096]{1,0:T(8,128)(2,1)} %copy-done.95, f32[200,1024]{1,0:T(8,128)S(1)} %copy-done.35, f32[1024]{0:T(1024)S(1)} %bitcast.597, ...), kind=kOutput, calls=%fused_computation.6 | convolution fusion | flops 1695522816 | bytes 86353472 | tf_op jit(solution)/shard_map/nd,nf->df/dot_general | solution.py:131
  939.6 9.7 fusion.248
  949.3 8.2 fusion.325
  957.5 8.2 fusion.326
  965.7 8.3 fusion.327
  974.0 31.8 %add_add_fusion = f32[4096,1024]{1,0:T(8,128)} fusion(f32[4096,1024]{1,0:T(8,128)} %fusion.327, f32[4096,1024]{1,0:T(8,128)} %fusion.326, f32[4096,1024]{1,0:T(8,128)} %fusion.248, f32[4096,1024]{1,0:T(8,128)} %fusion.325, bf16[200,1024]{1,0:T(8,128)(2,1)} %collective-permute-done.7, pred[]{:T(512)S(6)} %eq.3, f32[200,4096]{1,0:T(8,128)} %convolution_add_fusion.4), kind=kOutput, calls=%fused_computation.5 | convolution fusion | flops 1748361216 | bytes 87572480 | tf_op jit(solution)/shard_map/nf,nd->fd/dot_general | solution.py:123
  1023.4 174.8 %reduce-scatter.8.cloned.1.call-done = f32[64,3072]{1,0:T(8,128)} async-done(((f32[1024,3072]{1,0:T(8,128)}), f32[64,3072]{1,0:T(8,128)}) %reduce-scatter.8.cloned.1.call-update) | async-done | bytes 786448 | tf_op jit(solution)/shard_map/reduce_scatter | solution.py:286
  1201.5 345.6 %reduce-scatter.12.cloned.1.call-done = f32[64,4096]{1,0:T(8,128)} async-done(((f32[1024,4096]{1,0:T(8,128)}), f32[64,4096]{1,0:T(8,128)}) %reduce-scatter.12.cloned.1.call-update) | async-done | bytes 1048592 | tf_op jit(solution)/shard_map/reduce_scatter | solution.py:288
  1549.8 352.2 %reduce-scatter.14.cloned.1.call-done = f32[256,1024]{1,0:T(8,128)} async-done(((f32[4096,1024]{1,0:T(8,128)}), f32[256,1024]{1,0:T(8,128)}) %reduce-scatter.14.cloned.1.call-update) | async-done | bytes 1048592 | tf_op jit(solution)/shard_map/reduce_scatter | solution.py:289
  1906.0 44.4 %psum.7 = f32[]{:T(128)} all-reduce(f32[]{:T(128)S(6)} %add.751), channel_id=1, replica_groups=mesh['section'=2,'dp'=16] {'section','dp'}, use_global_device_ids=true, to_apply=%region_105.106 | all-reduce | flops 1 | bytes 8 | tf_op jit(solution)/shard_map/psum | solution.py:296
  (698 shorter events, 406.7 us)
Async XLA Ops:
  7.2 101.5 %all-gather.6.cloned.1.call-start = ((), (), s32[]{:S(2)}) async-start(), calls=%async_computation.5 | async-start | bytes 6684672 | tf_op jit(solution)/shard_map/all_gather | solution.py:233
  9.4 161.8 %all-gather.8.cloned.1.call-start = ((), (), s32[]{:S(2)}) async-start(), calls=%async_computation.6 | async-start | bytes 2228224 | tf_op jit(solution)/shard_map/all_gather | solution.py:234
  11.1 274.9 %all-gather.10.cloned.1.call-start = ((), (), s32[]{:S(2)}) async-start(), calls=%async_computation.7 | async-start | bytes 8912896 | tf_op jit(solution)/shard_map/all_gather | solution.py:235
  13.2 387.0 %all-gather.12.cloned.1.call-start = ((), (), s32[]{:S(2)}) async-start(), calls=%async_computation.8 | async-start | bytes 8912896 | tf_op jit(solution)/shard_map/all_gather | solution.py:236
  14.2 1006.0 %reduce-scatter.16.cloned.1.call-start = ((), (), s32[]{:S(2)}) async-start(), calls=%async_computation.13 | async-start | bytes 557056
  58.3 497.4 %copy-start.96 = (f32[1,1024]{1,0:T(1,128)}, f32[1,1024]{1,0:T(1,128)S(1)}, u32[]{:S(2)}) copy-start(f32[1,1024]{1,0:T(1,128)S(1)} %get-tuple-element.203) | copy-start | bytes 12292
  58.3 522.1 %copy-start.68 = (f32[1,1024]{1,0:T(1,128)}, f32[1,1024]{1,0:T(1,128)S(1)}, u32[]{:S(2)}) copy-start(f32[1,1024]{1,0:T(1,128)S(1)} %get-tuple-element.199) | copy-start | bytes 12292
  173.5 226.8 %copy-start.33 = (f32[200,1024]{1,0:T(8,128)}, f32[200,1024]{1,0:T(8,128)S(1)}, u32[]{:S(2)}) copy-start(f32[200,1024]{1,0:T(8,128)S(1)} %get-tuple-element.220) | copy-start | bytes 2457604
  411.8 2.7 collective-permute-start
  451.4 3.6 collective-permute-start.1
  493.1 6.0 collective-permute-start.2
  500.3 171.5 %copy-start.23 = (bf16[200,1024]{1,0:T(8,128)(2,1)}, bf16[200,1024]{1,0:T(8,128)(2,1)S(1)}, u32[]{:S(2)}) copy-start(bf16[200,1024]{1,0:T(8,128)(2,1)S(1)} %get-tuple-element.163) | copy-start | bytes 1228804
  500.3 171.5 %copy-start.145 = (f32[200]{0:T(256)}, f32[200]{0:T(256)S(1)}, u32[]{:S(2)}) copy-start(f32[200]{0:T(256)S(1)} %broadcast_multiply_fusion.24) | copy-start | bytes 2404
  500.6 171.2 %copy-start.167 = (f32[200]{0:T(256)}, f32[200]{0:T(256)S(1)}, u32[]{:S(2)}) copy-start(f32[200]{0:T(256)S(1)} %add_rsqrt_fusion.3) | copy-start | bytes 2404
  541.8 13.5 collective-permute-start.3
  631.3 5.9 collective-permute-start.4
  672.9 5.5 collective-permute-start.5
  711.7 6.2 collective-permute-start.6
  756.9 11.1 collective-permute-start.7
  813.6 208.1 %reduce-scatter.10.cloned.1.call-start = ((), (), s32[]{:S(2)}) async-start(), calls=%async_computation.10 | async-start | bytes 4456448 | tf_op jit(solution)/shard_map/reduce_scatter | solution.py:287
  822.9 375.3 %reduce-scatter.8.cloned.1.call-start = ((), (), s32[]{:S(2)}) async-start(), calls=%async_computation.9 | async-start | bytes 13369344 | tf_op jit(solution)/shard_map/reduce_scatter | solution.py:286
  873.0 674.0 %reduce-scatter.12.cloned.1.call-start = ((), (), s32[]{:S(2)}) async-start(), calls=%async_computation.11 | async-start | bytes 17825792 | tf_op jit(solution)/shard_map/reduce_scatter | solution.py:288
  938.5 963.5 %reduce-scatter.14.cloned.1.call-start = ((), (), s32[]{:S(2)}) async-start(), calls=%async_computation.12 | async-start | bytes 17825792 | tf_op jit(solution)/shard_map/reduce_scatter | solution.py:289
  1017.0 934.1 %copy-start.160 = (f32[1,12,64]{2,0,1:T(1,128)S(1)}, f32[1,12,64]{2,0,1:T(1,128)}, u32[]{:S(2)}) copy-start(f32[1,12,64]{2,0,1:T(1,128)} %param.25) | copy-start | bytes 9220
  1017.0 934.1 %copy-start.182 = (f32[1,12,64]{2,0,1:T(1,128)S(1)}, f32[1,12,64]{2,0,1:T(1,128)}, u32[]{:S(2)}) copy-start(f32[1,12,64]{2,0,1:T(1,128)} %param.35) | copy-start | bytes 9220
  1017.0 934.1 %copy-start.183 = (f32[1,12,64]{2,0,1:T(1,128)S(1)}, f32[1,12,64]{2,0,1:T(1,128)}, u32[]{:S(2)}) copy-start(f32[1,12,64]{2,0,1:T(1,128)} %param.30) | copy-start | bytes 9220
  1017.0 936.5 %copy-start.102 = (f32[1,64,1024]{2,1,0:T(8,128)S(1)}, f32[1,64,1024]{2,1,0:T(8,128)}, u32[]{:S(2)}) copy-start(f32[1,64,1024]{2,1,0:T(8,128)} %param.22) | copy-start | bytes 786436
  1017.1 936.5 %copy-start.121 = (f32[1,64,1024]{2,1,0:T(8,128)S(1)}, f32[1,64,1024]{2,1,0:T(8,128)}, u32[]{:S(2)}) copy-start(f32[1,64,1024]{2,1,0:T(8,128)} %param.32) | copy-start | bytes 786436
  1017.1 936.5 %copy-start.122 = (f32[1,64,1024]{2,1,0:T(8,128)S(1)}, f32[1,64,1024]{2,1,0:T(8,128)}, u32[]{:S(2)}) copy-start(f32[1,64,1024]{2,1,0:T(8,128)} %param.27) | copy-start | bytes 786436
  1020.2 934.6 %copy-start.66 = (f32[1,64,3072]{2,1,0:T(8,128)S(1)}, f32[1,64,3072]{2,1,0:T(8,128)}, u32[]{:S(2)}) copy-start(f32[1,64,3072]{2,1,0:T(8,128)} %param.21) | copy-start | bytes 2359300
  1021.7 931.9 %copy-start.103 = (f32[64,1024]{1,0:T(8,128)S(1)}, f32[64,1024]{1,0:T(8,128)}, u32[]{:S(2)}) copy-start(f32[64,1024]{1,0:T(8,128)} %reduce-scatter.10.cloned.1.call-done) | copy-start | bytes 786436
  1198.2 756.6 %copy-start.67 = (f32[64,3072]{1,0:T(8,128)S(1)}, f32[64,3072]{1,0:T(8,128)}, u32[]{:S(2)}) copy-start(f32[64,3072]{1,0:T(8,128)} %reduce-scatter.8.cloned.1.call-done) | copy-start | bytes 2359300
  (190 other events, 2245.1 us)
Sparse Core Ops, SparseCore 0:
  11.4 97.3 all-gather.5
  112.1 58.9 all-gather.7
  174.5 111.4 all-gather.9
  289.2 111.0 all-gather.11
  813.7 79.2 reduce-scatter.15
  895.8 91.5 reduce-scatter.9
  994.5 203.6 reduce-scatter.7
  1201.0 345.9 reduce-scatter.11
  1549.9 352.0 reduce-scatter.13
where the time goes:
time: 1980 us; the launch traced here: 1970 us
  waiting for transfers between devices  1190 us (60%)
  matrix products  463 us (23%)
  local copies, waits for them, and re-layouts  126 us (6%)
  blocking collectives  87.7 us (4%)
  other arithmetic  67.8 us (3%)
  between operations  22.1 us (1%)
    reduce_scatter x1, waiting for transfers between devices, body(): lax.psum_scatter(totals[3], 'dp', scatter_dimension=0, tiled=True)  352 us
    reduce_scatter x1, waiting for transfers between devices, body(): lax.psum_scatter(totals[2], 'dp', scatter_dimension=0, tiled=True)  346 us
    reduce_scatter x1, waiting for transfers between devices, body(): lax.psum_scatter(totals[0], 'dp', scatter_dimension=0, tiled=True)  175 us
    all_gather x1, waiting for transfers between devices, body(): lax.all_gather(lowered[2], 'dp', axis=0, tiled=True)  112 us
    all_gather x1, waiting for transfers between devices, body(): lax.all_gather(lowered[3], 'dp', axis=0, tiled=True)  107 us
    dot_general x5, matrix products, layer_backward(): jnp.einsum('nf,nd->fd', active_low, grad_out_low, preferred_element_type=...  66.1 us
    dot_general x5, matrix products, layer_backward(): jnp.einsum('nd,nf->df', hidden_two, grad_pre_low, preferred_element_type=...  64.2 us
    dot_general x5, matrix products, layer_forward(): jnp.dot(hidden_two, w_in, preferred_element_type=jnp.float32)  58.3 us
  transfers between devices with their start and end apart: 17, of which 9 were waited for; matrix products, arithmetic and copies ran while one was open for 14% of the time, Pallas kernels for 0%

commit v1 on v0

v1 whole, which is shorter than its diff:
```python
import functools
import jax
import jax.numpy as jnp
from jax import lax
from jax.experimental import pallas as pl
from jax.experimental.pallas import tpu as pltpu
from jax.sharding import PartitionSpec as P

HEADS = 16
HEAD = 64
SEQ = 50
STEP = 10
SIDE = 4
LEVELS = 4

norm_epsilon = 1e-06
clip_norm = 1.0
beta_one = 0.9
beta_two = 0.95
rate_matrix = 0.05
rate_vector = 1.0
decay_matrix = 0.1
epsilon = 1e-08
PAD = 128
low_type = jnp.bfloat16
wide = jnp.float32


def swap_cores(x):
    return lax.ppermute(x, "section", [(0, 1), (1, 0)])


def flip(x, bit):
    count = lax.axis_size("dp")
    return lax.ppermute(x, "dp", [(i, i ^ bit) for i in range(count)])


def shift(x, levels, by):
    pairs = [
        (level * SIDE + q, (level + by) * SIDE + q) for level in levels for q in range(SIDE)
    ]
    return lax.ppermute(x, "dp", pairs)


def split_halves(own, first):
    rows = own.shape[0] // 2
    below, above = own[:rows], own[rows:]
    keep = jnp.where(first, below, above)
    got = swap_cores(jnp.where(first, above, below))
    return jnp.where(first, keep, got), jnp.where(first, got, keep)


def join_halves(part_zero, part_one, first):
    got = swap_cores(jnp.where(first, part_one, part_zero))
    mine = jnp.where(first, part_zero, part_one)
    return jnp.where(
        first, jnp.concatenate([mine, got], axis=0), jnp.concatenate([got, mine], axis=0)
    )


def gather_column(part, level):
    ups, downs = [], []
    up = down = part
    for step in range(1, LEVELS):
        up = shift(up, range(step - 1, LEVELS - 1), 1)
        down = shift(down, range(1, LEVELS + 1 - step), -1)
        ups.append(up)
        downs.append(down)
    line = jnp.stack(ups[::-1] + [part] + downs)
    return lax.dynamic_slice_in_dim(line, LEVELS - 1 - level, LEVELS, axis=0)


def gather_pieces(part, level):
    column = gather_column(part, level)
    across = flip(column, 1)
    along = flip(column, 2)
    half = LEVELS // 2
    corner_low = flip(along[:half], 1)
    corner_high = flip(across[half:], 2)
    mine = [column, across, along, corner_low, corner_high]
    return mine, [swap_cores(piece) for piece in mine]


def assemble_kernel(cuts, rows, place_ref, *refs):
    pieces, outs, sems = refs[:10], refs[10:-1], refs[-1]
    me, core = place_ref[0], place_ref[1]
    half = LEVELS // 2
    copies = []
    for side in range(2):
        owner = lax.rem(core + side, 2)
        for slot in range(5):
            relative = min(slot, 3)
            first_level = half if slot == 4 else 0
            levels = LEVELS if slot < 3 else half
            chip = jnp.bitwise_xor(me, relative)
            for j in range(levels):
                row = ((first_level + j) * SIDE + chip) * 2 + owner
                for k, (start, width) in enumerate(cuts):
                    copies.append(
                        pltpu.make_async_copy(
                            pieces[side * 5 + slot].at[j, :, pl.ds(start, width)],
                            outs[k].at[pl.ds(pl.multiple_of(row * rows, rows), rows)],
                            sems.at[len(copies)],
                        )
                    )
    for copy in copies:
        copy.start()
    for copy in copies:
        copy.wait()


def assemble(mine, theirs, place, cuts):
    rows, columns = mine[0].shape[1:]
    total = LEVELS * SIDE * 2 * rows
    count = 2 * (3 * LEVELS + LEVELS) * len(cuts)
    size = total * sum(width for _, width in cuts) * 2
    outs = pl.pallas_call(
        functools.partial(assemble_kernel, cuts, rows),
        out_shape=[jax.ShapeDtypeStruct((total, width), low_type) for _, width in cuts],
        in_specs=[pl.BlockSpec(memory_space=pltpu.SMEM)] + [pl.BlockSpec(memory_space=pl.ANY)] * 10,
        out_specs=[pl.BlockSpec(memory_space=pl.ANY)] * len(cuts),
        scratch_shapes=[pltpu.SemaphoreType.DMA((count,))],
        cost_estimate=pl.CostEstimate(flops=0, bytes_accessed=2 * size, transcendentals=0),
        name="assemble",
    )(place, *mine, *theirs)
    return outs


def scatter_pieces(grad, core, me, level):
    columns = grad.shape[1]
    rows = grad.shape[0] // (LEVELS * SIDE * 2)
    shaped = grad.reshape(LEVELS * SIDE, 2, rows, columns)
    other = lax.dynamic_index_in_dim(shaped, 1 - core, 1, keepdims=False)
    mine = lax.dynamic_index_in_dim(shaped, core, 1, keepdims=False)
    got = swap_cores(other)
    chip = (mine.astype(wide) + got.astype(wide)).astype(low_type)
    chip = chip.reshape(LEVELS, SIDE, rows, columns)
    half = LEVELS // 2

    def toward(relative):
        return lax.dynamic_index_in_dim(chip, jnp.bitwise_xor(me, relative), 1, keepdims=False)

    corner = toward(3)
    from_across = flip(corner[:half], 1)
    from_along = flip(corner[half:], 2)
    along, across = toward(2), toward(1)
    along = jnp.concatenate(
        [(along[:half].astype(wide) + from_across.astype(wide)).astype(low_type), along[half:]]
    )
    across = jnp.concatenate(
        [across[:half], (across[half:].astype(wide) + from_along.astype(wide)).astype(low_type)]
    )
    got_across = flip(across, 1)
    got_along = flip(along, 2)
    line = toward(0).astype(wide) + got_across.astype(wide) + got_along.astype(wide)

    def pick(target):
        return lax.dynamic_index_in_dim(line, jnp.clip(target, 0, LEVELS - 1), 0, keepdims=False)

    up = down = 0.0
    for step in range(1, LEVELS):
        far = LEVELS - step
        up = shift((pick(level + far) + up).astype(low_type), range(0, step), 1).astype(wide)
        down = shift(
            (pick(level - far) + down).astype(low_type), range(LEVELS - step, LEVELS), -1
        ).astype(wide)
    return pick(level) + up + down


def total_of(value):
    value = value + swap_cores(value)
    across, along, corner = flip(value, 1), flip(value, 2), flip(value, 3)
    value = (value + across) + (along + corner)
    count = lax.axis_size("dp")

    def turn(by):
        pairs = [(i, (i + by * SIDE) % count) for i in range(count)]
        return lax.ppermute(value, "dp", pairs)

    one, two, three = turn(1), turn(2), turn(3)
    return (value + two) + (one + three)


def normalize(inputs):
    centered = inputs - jnp.mean(inputs, axis=-1, keepdims=True)
    inverse = lax.rsqrt(jnp.mean(centered * centered, axis=-1, keepdims=True) + norm_epsilon)
    return (centered * inverse, inverse)


def normalize_back(upstream, scaled, inverse):
    return inverse * (
        upstream
        - jnp.mean(upstream, axis=-1, keepdims=True)
        - scaled * jnp.mean(upstream * scaled, axis=-1, keepdims=True)
    )


def dot_nt(left, right):
    return lax.dot_general(left, right, (((1,), (1,)), ((), ())), preferred_element_type=wide)


def dot_nn(left, right):
    return lax.dot_general(left, right, (((1,), (0,)), ((), ())), preferred_element_type=wide)


def dot_tn(left, right):
    return lax.dot_general(left, right, (((0,), (0,)), ((), ())), preferred_element_type=wide)


def same_image(rows):
    image_row = lax.broadcasted_iota(jnp.int32, (rows, rows), 0) // SEQ
    image_col = lax.broadcasted_iota(jnp.int32, (rows, rows), 1) // SEQ
    return image_row == image_col


def attend_kernel(q_ref, k_ref, v_ref, o_ref):
    rows = q_ref.shape[0]
    mask = same_image(rows)
    lane = lax.broadcasted_iota(jnp.int32, (rows, 2 * HEAD), 1)
    queries, keys, values = q_ref[...], k_ref[...], v_ref[...]
    mixed = []
    for head in range(2):
        inside = (lane >= head * HEAD) & (lane < (head + 1) * HEAD)
        own = jnp.where(inside, queries, jnp.zeros_like(queries))
        scores = jnp.where(mask, dot_nt(own, keys) * HEAD ** (-0.5), -jnp.inf)
        raised = jnp.exp(scores - jnp.max(scores, axis=1, keepdims=True))
        weights = raised / jnp.sum(raised, axis=1, keepdims=True)
        mixed.append(dot_nn(weights.astype(low_type), values))
    o_ref[...] = jnp.where(lane < HEAD, mixed[0], mixed[1]).astype(low_type)


def attend(packed):
    rows, columns = packed.shape
    blocks = columns // 3 // (2 * HEAD)
    width = 2 * HEAD

    def at(third):
        return pl.BlockSpec((rows, width), lambda j: (0, third * blocks + j))

    return pl.pallas_call(
        attend_kernel,
        grid=(blocks,),
        in_specs=[at(0), at(1), at(2)],
        out_specs=at(0),
        out_shape=jax.ShapeDtypeStruct((rows, columns // 3), low_type),
        cost_estimate=pl.CostEstimate(
            flops=8 * rows * rows * columns // 3,
            bytes_accessed=8 * rows * columns // 3,
            transcendentals=rows * rows * HEADS,
        ),
        compiler_params=pltpu.CompilerParams(vmem_limit_bytes=32 * 1024 * 1024),
        name="attend",
    )(packed, packed, packed)


def attend_back_kernel(q_ref, k_ref, v_ref, g_ref, dq_ref, dk_ref, dv_ref):
    rows = q_ref.shape[0]
    mask = same_image(rows)
    lane = lax.broadcasted_iota(jnp.int32, (rows, 2 * HEAD), 1)
    queries, keys, values, upstream = q_ref[...], k_ref[...], v_ref[...], g_ref[...]
    scaling = HEAD ** (-0.5)
    to_queries, to_keys, to_values = [], [], []
    for head in range(2):
        inside = (lane >= head * HEAD) & (lane < (head + 1) * HEAD)
        zero = jnp.zeros_like(queries)
        own_queries = jnp.where(inside, queries, zero)
        own_upstream = jnp.where(inside, upstream, zero)
        scores = jnp.where(mask, dot_nt(keys, own_queries) * scaling, -jnp.inf)
        raised = jnp.exp(scores - jnp.max(scores, axis=0, keepdims=True))
        weights = raised / jnp.sum(raised, axis=0, keepdims=True)
        to_values.append(dot_nn(weights.astype(low_type), upstream))
        slope = dot_nt(values, own_upstream)
        inner = jnp.sum(weights * slope, axis=0, keepdims=True)
        change = (weights * (slope - inner)).astype(low_type)
        to_keys.append(dot_nn(change, queries))
        to_queries.append(dot_tn(keys, change))
    lower = lane < HEAD
    dv_ref[...] = jnp.where(lower, to_values[0], to_values[1]).astype(low_type)
    dk_ref[...] = (jnp.where(lower, to_keys[0], to_keys[1]) * scaling).astype(low_type)
    turned = jnp.concatenate([to_queries[0][:HEAD], to_queries[1][HEAD:]], axis=0)
    dq_ref[...] = (turned.T * scaling).astype(low_type)


def attend_back(packed, upstream):
    rows, columns = packed.shape
    blocks = columns // 3 // (2 * HEAD)
    width = 2 * HEAD

    def at(third):
        return pl.BlockSpec((rows, width), lambda j: (0, third * blocks + j))

    shape = jax.ShapeDtypeStruct((rows, columns // 3), low_type)
    return pl.pallas_call(
        attend_back_kernel,
        grid=(blocks,),
        in_specs=[at(0), at(1), at(2), at(0)],
        out_specs=[at(0)] * 3,
        out_shape=[shape] * 3,
        cost_estimate=pl.CostEstimate(
            flops=20 * rows * rows * columns // 3,
            bytes_accessed=14 * rows * columns // 3,
            transcendentals=rows * rows * HEADS,
        ),
        compiler_params=pltpu.CompilerParams(vmem_limit_bytes=48 * 1024 * 1024),
        name="attend_back",
    )(packed, packed, packed, upstream)


def dot(left, right):
    return jnp.dot(left, right, preferred_element_type=wide)


def back_dot(left, right):
    return jnp.einsum("nf,df->nd", left, right, preferred_element_type=wide)


def weight_dot(left, right):
    return jnp.einsum("nd,nf->df", left, right, preferred_element_type=wide).astype(low_type)


def layer_forward(inputs, weights, rows_all):
    w_qkv, w_proj, w_in, w_out = weights
    scaled_one, inverse_one = normalize(inputs)
    hidden = (scaled_one * rows_all[0] + rows_all[1]).astype(low_type)
    bias_all = jnp.concatenate([rows_all[2], jnp.zeros_like(rows_all[2]), rows_all[3]])
    packed = (dot(hidden, w_qkv) + bias_all).astype(low_type)
    mixed_low = attend(packed)
    middle = inputs + (dot(mixed_low, w_proj) + rows_all[4])
    scaled_two, inverse_two = normalize(middle)
    hidden_two = (scaled_two * rows_all[5] + rows_all[6]).astype(low_type)
    pre_act = dot(hidden_two, w_in) + rows_all[8:12].reshape(-1)
    active_low = jax.nn.gelu(pre_act, approximate=False).astype(low_type)
    output = middle + (dot(active_low, w_out) + rows_all[7])
    kept = (inputs, hidden, packed, mixed_low, middle, hidden_two, pre_act, active_low)
    return output, kept


def layer_backward(upstream, weights, rows_all, kept):
    w_qkv, w_proj, w_in, w_out = weights
    inputs, hidden, packed, mixed_low, middle, hidden_two, pre_act, active_low = kept
    scaled_one, inverse_one = normalize(inputs)
    scaled_two, inverse_two = normalize(middle)
    model_width = inputs.shape[1]
    grad_out_low = upstream.astype(low_type)
    grad_w_out = weight_dot(active_low, grad_out_low)
    grad_b_out = jnp.sum(grad_out_low.astype(wide), axis=0)
    grad_active = back_dot(grad_out_low, w_out)
    normal_cdf = 0.5 * (1.0 + lax.erf(pre_act * 0.7071067811865476))
    density = jnp.exp(-0.5 * pre_act * pre_act) * 0.3989422804014327
    grad_pre_low = (grad_active * (normal_cdf + pre_act * density)).astype(low_type)
    grad_w_in = weight_dot(hidden_two, grad_pre_low)
    grad_b_in = jnp.sum(grad_pre_low.astype(wide), axis=0)
    grad_hidden_two = back_dot(grad_pre_low, w_in)
    grad_gain_two = jnp.sum(grad_hidden_two * scaled_two, axis=0)
    grad_shift_two = jnp.sum(grad_hidden_two, axis=0)
    grad_middle = upstream + normalize_back(grad_hidden_two * rows_all[5], scaled_two, inverse_two)
    grad_branch_low = grad_middle.astype(low_type)
    grad_w_proj = weight_dot(mixed_low, grad_branch_low)
    grad_b_proj = jnp.sum(grad_branch_low.astype(wide), axis=0)
    grad_mixed_low = back_dot(grad_branch_low, w_proj).astype(low_type)
    grad_packed_low = jnp.concatenate(attend_back(packed, grad_mixed_low), axis=1)
    grad_w_qkv = weight_dot(hidden, grad_packed_low)
    column_sums = jnp.sum(grad_packed_low.astype(wide), axis=0)
    grad_hidden = back_dot(grad_packed_low, w_qkv)
    grad_gain_one = jnp.sum(grad_hidden * scaled_one, axis=0)
    grad_shift_one = jnp.sum(grad_hidden, axis=0)
    grad_entry = grad_middle + normalize_back(grad_hidden * rows_all[0], scaled_one, inverse_one)
    grad_rows = jnp.stack(
        [
            grad_gain_one,
            grad_shift_one,
            column_sums[:model_width],
            column_sums[2 * model_width :],
            grad_b_proj,
            grad_gain_two,
            grad_shift_two,
            grad_b_out,
        ]
    )
    grad_vectors = jnp.concatenate([grad_rows, grad_b_in.reshape(4, model_width)], axis=0)
    turned = jnp.pad(grad_vectors.T, ((0, 0), (0, PAD - grad_vectors.shape[0]))).astype(low_type)
    first_group = jnp.concatenate([grad_w_qkv, grad_w_proj, turned], axis=1)
    return grad_entry, (first_group, grad_w_in, grad_w_out)


def adam_update(weight, grad, first, second, factor, rate, decay):
    clipped = grad * factor
    momentum = beta_one * first + (1.0 - beta_one) * clipped
    variance = beta_two * second + (1.0 - beta_two) * clipped * clipped
    corrected_m = momentum / (1.0 - beta_one**STEP)
    corrected_v = variance / (1.0 - beta_two**STEP)
    updated = weight - rate * (corrected_m / (jnp.sqrt(corrected_v) + epsilon) + decay * weight)
    return (updated, momentum, variance)


def body(
    patches,
    live,
    cotangent,
    w_qkv,
    w_proj,
    w_in,
    w_out,
    vectors,
    first_qkv,
    first_proj,
    first_in,
    first_out,
    first_vectors,
    second_qkv,
    second_proj,
    second_in,
    second_out,
    second_vectors,
):
    core = lax.axis_index("section")
    first = core == 0
    chip = lax.axis_index("dp")
    count_dp = lax.axis_size("dp")
    tuned = count_dp == LEVELS * SIDE
    level = chip // SIDE
    me = chip % SIDE
    place = jnp.stack([me, core]).astype(jnp.int32)
    masters = (w_qkv[0], w_proj[0], w_in[0], w_out[0], vectors[0])
    count_vectors = vectors.shape[1]
    width = patches.shape[1]
    wide_qkv, wide_proj = w_qkv.shape[2], w_proj.shape[2]
    wide_first = wide_qkv + wide_proj + PAD
    turned = jnp.pad(vectors[0].T, ((0, 0), (0, PAD - count_vectors)))
    packs = (
        jnp.concatenate(
            [w_qkv[0].astype(low_type), w_proj[0].astype(low_type), turned.astype(low_type)], axis=1
        ),
        w_in[0].astype(low_type),
        w_out[0].astype(low_type),
    )
    cuts = (
        ((0, wide_qkv), (wide_qkv, wide_proj), (wide_qkv + wide_proj, PAD)),
        ((0, w_in.shape[2]),),
        ((0, w_out.shape[2]),),
    )

    gathered = [[], []]
    if tuned:
        parts = [split_halves(pack, first) for pack in packs]
        for layer in range(2):
            for part, cut in zip(parts, cuts):
                mine, theirs = gather_pieces(part[layer], level)
                gathered[layer].extend(assemble(mine, theirs, place, cut))
    else:
        for pack, cut in zip(packs, cuts):
            own = lax.all_gather(pack, "dp", axis=0, tiled=True)
            other = swap_cores(own)
            for layer in range(2):
                full = jnp.where(core == layer, own, other)
                gathered[layer].extend(full[:, start : start + size] for start, size in cut)

    layers = []
    for layer in range(2):
        g_qkv, g_proj, g_turned, g_in, g_out = gathered[layer]
        rows_all = g_turned[:, :count_vectors].T.astype(wide)
        layers.append(((g_qkv, g_proj, g_in, g_out), rows_all))

    tokens = patches.shape[0] // 2
    images = live.shape[0] // 2
    entry = lax.dynamic_slice_in_dim(patches, core * tokens, tokens, axis=0).astype(wide)
    weighting = lax.dynamic_slice_in_dim(live, core * images, images, axis=0).astype(wide)
    target = lax.dynamic_slice_in_dim(cotangent, core * tokens, tokens, axis=0).astype(wide)
    target = (
        target.reshape(images, SEQ, width) * weighting.reshape(images, 1, 1)
    ).reshape(tokens, width)

    output_zero, kept_zero = layer_forward(entry, *layers[0])
    block_zero = output_zero.astype(low_type)
    output_one, kept_one = layer_forward(block_zero.astype(wide), *layers[1])
    block_one = output_one.astype(low_type)

    def reduce_group(grad):
        if tuned:
            return scatter_pieces(grad, core, me, level)
        return grad

    entry_one, terms_one = layer_backward(target, *layers[1], kept_one)
    entry_one = entry_one.astype(low_type)
    halves_one = [reduce_group(term) for term in terms_one[::-1]][::-1]
    entry_zero, terms_zero = layer_backward(entry_one.astype(wide), *layers[0], kept_zero)
    entry_zero = entry_zero.astype(low_type)
    halves_zero = [reduce_group(term) for term in terms_zero[::-1]][::-1]

    if tuned:
        sums = [join_halves(a, b, first) for a, b in zip(halves_zero, halves_one)]
    else:
        sums = []
        for a, b in zip(terms_zero, terms_one):
            got = swap_cores(jnp.where(first, b, a))
            own = jnp.where(first, a, b).astype(wide) + got.astype(wide)
            sums.append(lax.psum_scatter(own, "dp", scatter_dimension=0, tiled=True))
    blocks = join_halves(block_zero, block_one, first)
    input_grad = join_halves(entry_zero, entry_one, first)

    shards = (
        sums[0][:, :wide_qkv],
        sums[0][:, wide_qkv : wide_qkv + wide_proj],
        sums[1],
        sums[2],
        sums[0][:, wide_qkv + wide_proj : wide_qkv + wide_proj + count_vectors].T,
    )
    local_sum = sum((jnp.sum(s * s) for s in shards))
    if tuned:
        global_sum = total_of(local_sum)
    else:
        global_sum = lax.psum(local_sum, ("section", "dp"))
    grad_norm = jnp.sqrt(global_sum)
    factor = clip_norm / jnp.maximum(grad_norm, clip_norm)
    firsts = (first_qkv[0], first_proj[0], first_in[0], first_out[0], first_vectors[0])
    seconds = (second_qkv[0], second_proj[0], second_in[0], second_out[0], second_vectors[0])
    rates = (rate_matrix, rate_matrix, rate_matrix, rate_matrix, rate_vector)
    decays = (decay_matrix, decay_matrix, decay_matrix, decay_matrix, 0.0)
    results = [
        adam_update(w, g, f, s, factor, r, d)
        for w, g, f, s, r, d in zip(masters, shards, firsts, seconds, rates, decays)
    ]
    news = tuple((item[0][None] for item in results))
    momenta = tuple((item[1][None] for item in results))
    variances = tuple((item[2][None] for item in results))
    copies = tuple((n.astype(low_type) for n in news))
    grads_out = tuple((s[None] for s in shards))
    return (
        blocks[None],
        input_grad[None],
        *grads_out,
        grad_norm,
        *news,
        *copies,
        *momenta,
        *variances,
    )


def solution(mesh):
    in_specs = (
        P("dp", None),
        P("dp"),
        P("dp", None),
        P("section", "dp", None),
        P("section", "dp", None),
        P("section", "dp", None),
        P("section", "dp", None),
        P("section", None, "dp"),
        P("section", "dp", None),
        P("section", "dp", None),
        P("section", "dp", None),
        P("section", "dp", None),
        P("section", None, "dp"),
        P("section", "dp", None),
        P("section", "dp", None),
        P("section", "dp", None),
        P("section", "dp", None),
        P("section", None, "dp"),
    )
    out_specs = (
        P("section", "dp", None),
        P("section", "dp", None),
        P("section", "dp", None),
        P("section", "dp", None),
        P("section", "dp", None),
        P("section", "dp", None),
        P("section", None, "dp"),
        P(),
        P("section", "dp", None),
        P("section", "dp", None),
        P("section", "dp", None),
        P("section", "dp", None),
        P("section", None, "dp"),
        P("section", "dp", None),
        P("section", "dp", None),
        P("section", "dp", None),
        P("section", "dp", None),
        P("section", None, "dp"),
        P("section", "dp", None),
        P("section", "dp", None),
        P("section", "dp", None),
        P("section", "dp", None),
        P("section", None, "dp"),
        P("section", "dp", None),
        P("section", "dp", None),
        P("section", "dp", None),
        P("section", "dp", None),
        P("section", None, "dp"),
    )
    return jax.shard_map(body, mesh=mesh, in_specs=in_specs, out_specs=out_specs, check_vma=False)
```

time: 1980 us -> 2690 us (1.36)
  Pallas kernels: 0 us -> 1610 us
  waiting for transfers between devices: 1190 us -> 441 us
  matrix products: 463 us -> 154 us
  starting transfers between devices: 13.6 us -> 308 us
  blocking collectives: 87.7 us -> 0 us
  local copies, waits for them, and re-layouts: 126 us -> 59.3 us
  other arithmetic: 67.8 us -> 96.1 us
    pallas_call x0 -> x10, Pallas kernels: none -> 1610 us  [the longest x6 1550 us: assemble(): pl.pallas_call(functools.partial(assemble_kernel, cuts, rows), out_shape=...]
    reduce_scatter x4 -> x0, waiting for transfers between devices: 873 us -> none  [the longest x1 352 us: body(): lax.psum_scatter(totals[3], 'dp', scatter_dimension=0, tiled=True)]
    ppermute x8 -> x171, waiting for transfers between devices: 2.67 us -> 441 us  [the longest x51 319 us: flip(): return lax.ppermute(x, 'dp', [(i, i ^ bit) for i in range(count)])]
    all_gather x4 -> x0, waiting for transfers between devices: 317 us -> none  [the longest x1 112 us: body(): lax.all_gather(lowered[2], 'dp', axis=0, tiled=True)]
    ppermute x8 -> x171, starting transfers between devices: 13.3 us -> 308 us  [the longest x72 206 us: shift(): return lax.ppermute(x, 'dp', pairs)]
    dot_general x85 -> x24, matrix products: 446 us -> 154 us  [the longest x8 64.4 us: dot(): return jnp.dot(left, right, preferred_element_type=wide)]
    convert_element_type x21 -> x6, local copies, waits for them, and re-layouts: 45.9 us -> 0.41 us  [scatter_pieces(): (pick(level + far) + up).astype(low_type)]
    psum x1 -> x0, blocking collectives: 44.4 us -> none  [body(): global_sum = lax.psum(local_sum, ('section', 'dp'))]
  transfers between devices with their start and end apart: 17 -> 171, of which waited for: 9 -> 77; matrix products, arithmetic and copies ran while one was open for 14% -> 4% of each run, Pallas kernels for 0% -> 48%
where the time goes in v1:
time: 2690 us; the launch traced here: 2680 us
  Pallas kernels  1610 us (60%)
  waiting for transfers between devices  441 us (16%)
  starting transfers between devices  308 us (11%)
  matrix products  154 us (6%)
  other arithmetic  96.1 us (4%)
  local copies, waits for them, and re-layouts  59.3 us (2%)
    pallas_call x6, Pallas kernels, assemble(): pl.pallas_call(functools.partial(assemble_kernel, cuts, rows), out_shape=...  1550 us
    ppermute x51, waiting for transfers between devices, flip(): return lax.ppermute(x, 'dp', [(i, i ^ bit) for i in range(count)])  319 us
    ppermute x72, starting transfers between devices, shift(): return lax.ppermute(x, 'dp', pairs)  206 us
    ppermute x72, waiting for transfers between devices, shift(): return lax.ppermute(x, 'dp', pairs)  101 us
    ppermute x51, starting transfers between devices, flip(): return lax.ppermute(x, 'dp', [(i, i ^ bit) for i in range(count)])  73.3 us
    dot_general x8, matrix products, dot(): return jnp.dot(left, right, preferred_element_type=wide)  64.4 us
  transfers between devices with their start and end apart: 171, of which 77 were waited for; matrix products, arithmetic and copies ran while one was open for 4% of the time, Pallas kernels for 48%

profile of v1, /device:TPU:0, one launch (start us, length us, event | category | flops | bytes accessed | tf_op | source)
XLA Modules:
  0.0 2678.4 jit_solution(18394249782186147009)
XLA Ops:
  21.9 12.1 collective-permute-start.81
  35.5 12.2 collective-permute-start.78
  61.0 15.8 collective-permute-done.21
  113.6 15.2 collective-permute-start.82
  181.0 12.0 collective-permute-done.40.refs_2_
  196.8 18.7 collective-permute-done.85.refs_2_
  220.3 17.7 collective-permute-done.24.refs_2_
  241.8 18.6 collective-permute-done.70.refs_2_
  264.4 19.3 collective-permute-done.8.refs_2_
  290.4 16.3 collective-permute-done.55.refs_2_
  342.9 21.5 collective-permute-done.71.refs_3_
  367.2 10.8 collective-permute-done.56.refs_3_
  406.1 256.2 %assemble.8 = bf16[4096,1024]{1,0:T(8,128)(2,1)} custom-call(s32[2]{0:T(128)} %pad_add_fusion.place_ref, bf16[4,128,1024]{2,1,0:T(8,128)(2,1)} %copy-done.29, bf16[4,128,1024]{2,1,0:T(8,128)(2,1)} %copy-done.46, bf16[4,128,1024]{2,1,0:T(8,128)(2,1)} %copy-done.45, bf16[2,128,1024]{2,1,0:T(8,128)(2,1)} %copy-done.88, bf16[2,128,1024]{2,1,0:T(8,128)(2,1)} %copy-done.90, ...), custom_call_target="tpu_custom_call" | custom-call | bytes 16777216 | tf_op jit(solution)/shard_map/assemble/pallas_call | solution.py:117
  662.3 256.2 %assemble.11 = bf16[4096,1024]{1,0:T(8,128)(2,1)} custom-call(s32[2]{0:T(128)} %pad_add_fusion.place_ref, bf16[4,128,1024]{2,1,0:T(8,128)(2,1)} %copy-done.30, bf16[4,128,1024]{2,1,0:T(8,128)(2,1)} %copy-done.48, bf16[4,128,1024]{2,1,0:T(8,128)(2,1)} %copy-done.47, bf16[2,128,1024]{2,1,0:T(8,128)(2,1)} %copy-done.89, bf16[2,128,1024]{2,1,0:T(8,128)(2,1)} %copy-done.92, ...), custom_call_target="tpu_custom_call" | custom-call | bytes 16777216 | tf_op jit(solution)/shard_map/assemble/pallas_call | solution.py:117
  918.5 256.2 %assemble.7 = bf16[1024,4096]{1,0:T(8,128)(2,1)} custom-call(s32[2]{0:T(128)} %pad_add_fusion.place_ref, bf16[4,32,4096]{2,1,0:T(8,128)(2,1)} %copy-done.27, bf16[4,32,4096]{2,1,0:T(8,128)(2,1)} %copy-done.50, bf16[4,32,4096]{2,1,0:T(8,128)(2,1)} %copy-done.49, bf16[2,32,4096]{2,1,0:T(8,128)(2,1)} %copy-done.91, bf16[2,32,4096]{2,1,0:T(8,128)(2,1)} %copy-done.93, ...), custom_call_target="tpu_custom_call" | custom-call | bytes 16777216 | tf_op jit(solution)/shard_map/assemble/pallas_call | solution.py:117
  1174.7 256.2 %assemble.10 = bf16[1024,4096]{1,0:T(8,128)(2,1)} custom-call(s32[2]{0:T(128)} %pad_add_fusion.place_ref, bf16[4,32,4096]{2,1,0:T(8,128)(2,1)} %copy-done.28, bf16[4,32,4096]{2,1,0:T(8,128)(2,1)} %copy-done.52, bf16[4,32,4096]{2,1,0:T(8,128)(2,1)} %copy-done.51, bf16[2,32,4096]{2,1,0:T(8,128)(2,1)} %collective-permute-done.71.refs_3_, ...), custom_call_target="tpu_custom_call" | custom-call | bytes 16777216 | tf_op jit(solution)/shard_map/assemble/pallas_call | solution.py:117
  1430.9 264.7 %assemble.6 = (bf16[1024,3072]{1,0:T(8,128)(2,1)}, bf16[1024,1024]{1,0:T(8,128)(2,1)}, bf16[1024,128]{1,0:T(8,128)(2,1)}) custom-call(s32[2]{0:T(128)} %pad_add_fusion.place_ref, bf16[4,32,4224]{2,1,0:T(8,128)(2,1)} %copy-done.26, bf16[4,32,4224]{2,1,0:T(8,128)(2,1)} %collective-permute-done.7.refs_1_, bf16[4,32,4224]{2,1,0:T(8,128)(2,1)} %collective-permute-done.8.refs_2_, ...), custom_call_target="tpu_custom_call" | custom-call | bytes 17301504 | tf_op jit(solution)/shard_map/assemble/pallas_call | solution.py:117
  1699.0 264.7 %assemble.9 = (bf16[1024,3072]{1,0:T(8,128)(2,1)}, bf16[1024,1024]{1,0:T(8,128)(2,1)}, bf16[1024,128]{1,0:T(8,128)(2,1)}) custom-call(s32[2]{0:T(128)} %pad_add_fusion.place_ref, bf16[4,32,4224]{2,1,0:T(8,128)(2,1)} %copy-done.25, bf16[4,32,4224]{2,1,0:T(8,128)(2,1)} %copy-done.44, bf16[4,32,4224]{2,1,0:T(8,128)(2,1)} %copy-done.43, ...), custom_call_target="tpu_custom_call" | custom-call | bytes 17301504 | tf_op jit(solution)/shard_map/assemble/pallas_call | solution.py:117
  1973.6 10.2 attend.2
  1985.3 22.4 fusion.12
  2015.4 10.2 attend.3
  2027.2 22.8 fusion.15
  2073.0 15.8 attend_back.2
  2119.5 16.0 attend_back.3
  2326.6 15.2 collective-permute-done.122
  2349.0 15.2 collective-permute-done.145
  2371.6 15.1 collective-permute-done.133
  2395.3 13.9 collective-permute-done.156
  2416.9 15.5 collective-permute-done.110
  2438.8 14.6 collective-permute-done.99
  2528.7 11.3 collective-permute-start.161
  2544.4 22.2 collective-permute-start.148
  (897 shorter events, 699.9 us)
Async XLA Ops:
  21.9 86.2 %collective-permute-start.81 = (bf16[128,1024]{1,0:T(8,128)(2,1)S(1)}, bf16[128,1024]{1,0:T(8,128)(2,1)S(1)}, u32[]{:S(2)}, u32[]{:S(2)}) collective-permute-start(bf16[128,1024]{1,0:T(8,128)(2,1)S(1)} %get-tuple-element.273), channel_id=1, source_target_pairs={{4,0},{5,1},{6,2},{7,3},{8,4},{9,5},{10,6},{11,7},{12,8},{13,9},{1... | collective-permute-start | bytes 786440 | tf_op jit(solution)/shard_map/ppermute | solution.py:42
  35.5 56.1 %collective-permute-start.78 = (bf16[128,1024]{1,0:T(8,128)(2,1)S(1)}, bf16[128,1024]{1,0:T(8,128)(2,1)S(1)}, u32[]{:S(2)}, u32[]{:S(2)}) collective-permute-start(bf16[128,1024]{1,0:T(8,128)(2,1)S(1)} %get-tuple-element.273), channel_id=1, source_target_pairs={{0,4},{1,5},{2,6},{3,7},{4,8},{5,9},{6,10},{7,11},{8,12},{9,13},{1... | collective-permute-start | bytes 786440 | tf_op jit(solution)/shard_map/ppermute | solution.py:42
  48.6 65.0 %collective-permute-start.36 = (bf16[128,1024]{1,0:T(8,128)(2,1)S(1)}, bf16[128,1024]{1,0:T(8,128)(2,1)S(1)}, u32[]{:S(2)}, u32[]{:S(2)}) collective-permute-start(bf16[128,1024]{1,0:T(8,128)(2,1)S(1)} %get-tuple-element.274), channel_id=1, source_target_pairs={{4,0},{5,1},{6,2},{7,3},{8,4},{9,5},{10,6},{11,7},{12,8},{13,9},{1... | collective-permute-start | bytes 786440 | tf_op jit(solution)/shard_map/ppermute | solution.py:42
  194.7 43.2 %collective-permute-start.24 = (bf16[4,32,4096]{2,1,0:T(8,128)(2,1)S(1)}, bf16[4,32,4096]{2,1,0:T(8,128)(2,1)S(1)}, u32[]{:S(2)}, u32[]{:S(2)}) collective-permute-start(bf16[4,32,4096]{2,1,0:T(8,128)(2,1)S(1)} %constant_dynamic-slice_fusion.4.refs_0_), channel_id=1, source_target_pairs={{0,2},{1,3},{2,0},{3,1},{4,6},{5,7},{6,4},{7,5},{8,10},{9,11},{10,... | collective-permute-start | bytes 3145736 | tf_op jit(solution)/shard_map/ppermute | solution.py:35
  195.3 44.4 %collective-permute-start.23 = (bf16[4,32,4096]{2,1,0:T(8,128)(2,1)S(1)}, bf16[4,32,4096]{2,1,0:T(8,128)(2,1)S(1)}, u32[]{:S(2)}, u32[]{:S(2)}) collective-permute-start(bf16[4,32,4096]{2,1,0:T(8,128)(2,1)S(1)} %constant_dynamic-slice_fusion.4.refs_0_), channel_id=1, source_target_pairs={{0,1},{1,0},{2,3},{3,2},{4,5},{5,4},{6,7},{7,6},{8,9},{9,8},{10,11... | collective-permute-start | bytes 3145736 | tf_op jit(solution)/shard_map/ppermute | solution.py:35
  218.8 43.4 %collective-permute-start.69 = (bf16[4,32,4096]{2,1,0:T(8,128)(2,1)S(1)}, bf16[4,32,4096]{2,1,0:T(8,128)(2,1)S(1)}, u32[]{:S(2)}, u32[]{:S(2)}) collective-permute-start(bf16[4,32,4096]{2,1,0:T(8,128)(2,1)S(1)} %constant_dynamic-slice_fusion.1.refs_0_), channel_id=1, source_target_pairs={{0,1},{1,0},{2,3},{3,2},{4,5},{5,4},{6,7},{7,6},{8,9},{9,8},{10,11... | collective-permute-start | bytes 3145736 | tf_op jit(solution)/shard_map/ppermute | solution.py:35
  239.7 44.0 %collective-permute-start.8 = (bf16[4,32,4224]{2,1,0:T(8,128)(2,1)S(1)}, bf16[4,32,4224]{2,1,0:T(8,128)(2,1)}, u32[]{:S(2)}, u32[]{:S(2)}) collective-permute-start(bf16[4,32,4224]{2,1,0:T(8,128)(2,1)S(1)} %constant_dynamic-slice_fusion.5.refs_0_), channel_id=1, source_target_pairs={{0,2},{1,3},{2,0},{3,1},{4,6},{5,7},{6,4},{7,5},{8,10},{9,11},{10,... | collective-permute-start | bytes 3244040 | tf_op jit(solution)/shard_map/ppermute | solution.py:35
  240.2 45.2 %collective-permute-start.7 = (bf16[4,32,4224]{2,1,0:T(8,128)(2,1)S(1)}, bf16[4,32,4224]{2,1,0:T(8,128)(2,1)}, u32[]{:S(2)}, u32[]{:S(2)}) collective-permute-start(bf16[4,32,4224]{2,1,0:T(8,128)(2,1)S(1)} %constant_dynamic-slice_fusion.5.refs_0_), channel_id=1, source_target_pairs={{0,1},{1,0},{2,3},{3,2},{4,5},{5,4},{6,7},{7,6},{8,9},{9,8},{10,11... | collective-permute-start | bytes 3244040 | tf_op jit(solution)/shard_map/ppermute | solution.py:35
  260.4 46.3 %collective-permute-start.55 = (bf16[4,32,4224]{2,1,0:T(8,128)(2,1)S(1)}, bf16[4,32,4224]{2,1,0:T(8,128)(2,1)S(1)}, u32[]{:S(2)}, u32[]{:S(2)}) collective-permute-start(bf16[4,32,4224]{2,1,0:T(8,128)(2,1)S(1)} %constant_dynamic-slice_fusion.2.refs_0_), channel_id=1, source_target_pairs={{0,2},{1,3},{2,0},{3,1},{4,6},{5,7},{6,4},{7,5},{8,10},{9,11},{10,... | collective-permute-start | bytes 3244040 | tf_op jit(solution)/shard_map/ppermute | solution.py:35
  262.1 46.3 %collective-permute-start.54 = (bf16[4,32,4224]{2,1,0:T(8,128)(2,1)S(1)}, bf16[4,32,4224]{2,1,0:T(8,128)(2,1)S(1)}, u32[]{:S(2)}, u32[]{:S(2)}) collective-permute-start(bf16[4,32,4224]{2,1,0:T(8,128)(2,1)S(1)} %constant_dynamic-slice_fusion.2.refs_0_), channel_id=1, source_target_pairs={{0,1},{1,0},{2,3},{3,2},{4,5},{5,4},{6,7},{7,6},{8,9},{9,8},{10,11... | collective-permute-start | bytes 3244040 | tf_op jit(solution)/shard_map/ppermute | solution.py:35
  263.7 56.1 %collective-permute-start.41 = (bf16[2,128,1024]{2,1,0:T(8,128)(2,1)S(1)}, bf16[2,128,1024]{2,1,0:T(8,128)(2,1)S(1)}, u32[]{:S(2)}, u32[]{:S(2)}) collective-permute-start(bf16[2,128,1024]{2,1,0:T(8,128)(2,1)S(1)} %slice.462), channel_id=1, source_target_pairs={{0,1},{1,0},{2,3},{3,2},{4,5},{5,4},{6,7},{7,6},{8,9},{9,8},{10,11... | collective-permute-start | bytes 1572872 | tf_op jit(solution)/shard_map/ppermute | solution.py:35
  285.4 45.5 %collective-permute-start.86 = (bf16[2,128,1024]{2,1,0:T(8,128)(2,1)S(1)}, bf16[2,128,1024]{2,1,0:T(8,128)(2,1)S(1)}, u32[]{:S(2)}, u32[]{:S(2)}) collective-permute-start(bf16[2,128,1024]{2,1,0:T(8,128)(2,1)S(1)} %slice.477), channel_id=1, source_target_pairs={{0,1},{1,0},{2,3},{3,2},{4,5},{5,4},{6,7},{7,6},{8,9},{9,8},{10,11... | collective-permute-start | bytes 1572872 | tf_op jit(solution)/shard_map/ppermute | solution.py:35
  321.4 44.4 %collective-permute-start.9 = (bf16[2,32,4224]{2,1,0:T(8,128)(2,1)S(1)}, bf16[2,32,4224]{2,1,0:T(8,128)(2,1)S(1)}, u32[]{:S(2)}, u32[]{:S(2)}) collective-permute-start(bf16[2,32,4224]{2,1,0:T(8,128)(2,1)S(1)} %slice.446), channel_id=1, source_target_pairs={{0,1},{1,0},{2,3},{3,2},{4,5},{5,4},{6,7},{7,6},{8,9},{9,8},{10,11... | collective-permute-start | bytes 1622024 | tf_op jit(solution)/shard_map/ppermute | solution.py:35
  396.1 1302.8 %collective-permute-start.58 = (bf16[4,32,4224]{2,1,0:T(8,128)(2,1)S(1)}, bf16[4,32,4224]{2,1,0:T(8,128)(2,1)}, u32[]{:S(2)}, u32[]{:S(2)}) collective-permute-start(bf16[4,32,4224]{2,1,0:T(8,128)(2,1)S(1)} %constant_dynamic-slice_fusion.2.refs_0_), channel_id=1, source_target_pairs={{0,16},{16,0},{1,17},{17,1},{2,18},{18,2},{3,19},{19,3},{4,20},{20... | collective-permute-start | bytes 3244040 | tf_op jit(solution)/shard_map/ppermute | solution.py:30
  396.7 1302.2 %collective-permute-start.60 = (bf16[4,32,4224]{2,1,0:T(8,128)(2,1)}, bf16[4,32,4224]{2,1,0:T(8,128)(2,1)}, u32[]{:S(2)}, u32[]{:S(2)}) collective-permute-start(bf16[4,32,4224]{2,1,0:T(8,128)(2,1)} %copy-done.43), channel_id=1, source_target_pairs={{0,16},{16,0},{1,17},{17,1},{2,18},{18,2},{3,19},{19,3},{4,20},{20... | collective-permute-start | bytes 3244040 | tf_op jit(solution)/shard_map/ppermute | solution.py:30
  396.9 1302.1 %collective-permute-start.59 = (bf16[4,32,4224]{2,1,0:T(8,128)(2,1)}, bf16[4,32,4224]{2,1,0:T(8,128)(2,1)}, u32[]{:S(2)}, u32[]{:S(2)}) collective-permute-start(bf16[4,32,4224]{2,1,0:T(8,128)(2,1)} %copy-done.44), channel_id=1, source_target_pairs={{0,16},{16,0},{1,17},{17,1},{2,18},{18,2},{3,19},{19,3},{4,20},{20... | collective-permute-start | bytes 3244040 | tf_op jit(solution)/shard_map/ppermute | solution.py:30
  404.2 1294.7 %collective-permute-start.61 = (bf16[2,32,4224]{2,1,0:T(8,128)(2,1)}, bf16[2,32,4224]{2,1,0:T(8,128)(2,1)}, u32[]{:S(2)}, u32[]{:S(2)}) collective-permute-start(bf16[2,32,4224]{2,1,0:T(8,128)(2,1)} %copy-done.86), channel_id=1, source_target_pairs={{0,16},{16,0},{1,17},{17,1},{2,18},{18,2},{3,19},{19,3},{4,20},{20... | collective-permute-start | bytes 1622024 | tf_op jit(solution)/shard_map/ppermute | solution.py:30
  404.4 1294.6 %collective-permute-start.62 = (bf16[2,32,4224]{2,1,0:T(8,128)(2,1)}, bf16[2,32,4224]{2,1,0:T(8,128)(2,1)}, u32[]{:S(2)}, u32[]{:S(2)}) collective-permute-start(bf16[2,32,4224]{2,1,0:T(8,128)(2,1)} %collective-permute-done.57.refs_4_), channel_id=1, source_target_pairs={{0,16},{16,0},{1,17},{17,1},{2,18},{18,2},{3,19},{19,3},{4,20},{20... | collective-permute-start | bytes 1622024 | tf_op jit(solution)/shard_map/ppermute | solution.py:30
  2185.9 416.2 %collective-permute-start.93 = (bf16[400,1024]{1,0:T(8,128)(2,1)}, bf16[400,1024]{1,0:T(8,128)(2,1)}, u32[]{:S(2)}, u32[]{:S(2)}) collective-permute-start(bf16[400,1024]{1,0:T(8,128)(2,1)} %get-tuple-element.269), channel_id=1, source_target_pairs={{0,16},{16,0},{1,17},{17,1},{2,18},{18,2},{3,19},{19,3},{4,20},{20... | collective-permute-start | bytes 2457608 | tf_op jit(solution)/shard_map/ppermute | solution.py:30
  2196.6 51.2 %collective-permute-start.129 = (bf16[16,32,4096]{2,1,0:T(8,128)(2,1)}, bf16[16,32,4096]{2,1,0:T(8,128)(2,1)}, u32[]{:S(2)}, u32[]{:S(2)}) collective-permute-start(bf16[16,32,4096]{2,1,0:T(8,128)(2,1)} %dynamic-slice_bitcast_fusion.4), channel_id=1, source_target_pairs={{0,16},{16,0},{1,17},{17,1},{2,18},{18,2},{3,19},{19,3},{4,20},{20... | collective-permute-start | bytes 12582920 | tf_op jit(solution)/shard_map/ppermute | solution.py:30
  2319.3 44.9 %collective-permute-start.145 = (bf16[4,128,1024]{2,1,0:T(8,128)(2,1)S(1)}, bf16[4,128,1024]{2,1,0:T(8,128)(2,1)S(1)}, u32[]{:S(2)}, u32[]{:S(2)}) collective-permute-start(bf16[4,128,1024]{2,1,0:T(8,128)(2,1)S(1)} %pad_maximum_fusion.9), channel_id=1, source_target_pairs={{0,2},{1,3},{2,0},{3,1},{4,6},{5,7},{6,4},{7,5},{8,10},{9,11},{10,... | collective-permute-start | bytes 3145736 | tf_op jit(solution)/shard_map/ppermute | solution.py:35
  2324.6 44.9 %collective-permute-start.143 = (bf16[4,128,1024]{2,1,0:T(8,128)(2,1)S(1)}, bf16[4,128,1024]{2,1,0:T(8,128)(2,1)S(1)}, u32[]{:S(2)}, u32[]{:S(2)}) collective-permute-start(bf16[4,128,1024]{2,1,0:T(8,128)(2,1)S(1)} %pad_maximum_fusion.8), channel_id=1, source_target_pairs={{0,1},{1,0},{2,3},{3,2},{4,5},{5,4},{6,7},{7,6},{8,9},{9,8},{10,11... | collective-permute-start | bytes 3145736 | tf_op jit(solution)/shard_map/ppermute | solution.py:35
  2341.8 44.9 %collective-permute-start.133 = (bf16[4,32,4096]{2,1,0:T(8,128)(2,1)S(1)}, bf16[4,32,4096]{2,1,0:T(8,128)(2,1)S(1)}, u32[]{:S(2)}, u32[]{:S(2)}) collective-permute-start(bf16[4,32,4096]{2,1,0:T(8,128)(2,1)S(1)} %pad_maximum_fusion.7), channel_id=1, source_target_pairs={{0,2},{1,3},{2,0},{3,1},{4,6},{5,7},{6,4},{7,5},{8,10},{9,11},{10,... | collective-permute-start | bytes 3145736 | tf_op jit(solution)/shard_map/ppermute | solution.py:35
  2347.1 45.0 %collective-permute-start.131 = (bf16[4,32,4096]{2,1,0:T(8,128)(2,1)S(1)}, bf16[4,32,4096]{2,1,0:T(8,128)(2,1)}, u32[]{:S(2)}, u32[]{:S(2)}) collective-permute-start(bf16[4,32,4096]{2,1,0:T(8,128)(2,1)S(1)} %pad_maximum_fusion.6), channel_id=1, source_target_pairs={{0,1},{1,0},{2,3},{3,2},{4,5},{5,4},{6,7},{7,6},{8,9},{9,8},{10,11... | collective-permute-start | bytes 3145736 | tf_op jit(solution)/shard_map/ppermute | solution.py:35
  2364.2 44.9 %collective-permute-start.156 = (bf16[4,128,1024]{2,1,0:T(8,128)(2,1)S(1)}, bf16[4,128,1024]{2,1,0:T(8,128)(2,1)S(1)}, u32[]{:S(2)}, u32[]{:S(2)}) collective-permute-start(bf16[4,128,1024]{2,1,0:T(8,128)(2,1)S(1)} %pad_maximum_fusion.11), channel_id=1, source_target_pairs={{0,2},{1,3},{2,0},{3,1},{4,6},{5,7},{6,4},{7,5},{8,10},{9,11},{10,... | collective-permute-start | bytes 3145736 | tf_op jit(solution)/shard_map/ppermute | solution.py:35
  2369.6 44.9 %collective-permute-start.154 = (bf16[4,128,1024]{2,1,0:T(8,128)(2,1)S(1)}, bf16[4,128,1024]{2,1,0:T(8,128)(2,1)S(1)}, u32[]{:S(2)}, u32[]{:S(2)}) collective-permute-start(bf16[4,128,1024]{2,1,0:T(8,128)(2,1)S(1)} %pad_maximum_fusion.10), channel_id=1, source_target_pairs={{0,1},{1,0},{2,3},{3,2},{4,5},{5,4},{6,7},{7,6},{8,9},{9,8},{10,11... | collective-permute-start | bytes 3145736 | tf_op jit(solution)/shard_map/ppermute | solution.py:35
  2386.7 45.6 %collective-permute-start.110 = (bf16[4,32,4224]{2,1,0:T(8,128)(2,1)S(1)}, bf16[4,32,4224]{2,1,0:T(8,128)(2,1)S(1)}, u32[]{:S(2)}, u32[]{:S(2)}) collective-permute-start(bf16[4,32,4224]{2,1,0:T(8,128)(2,1)S(1)} %pad_maximum_fusion.3), channel_id=1, source_target_pairs={{0,2},{1,3},{2,0},{3,1},{4,6},{5,7},{6,4},{7,5},{8,10},{9,11},{10,... | collective-permute-start | bytes 3244040 | tf_op jit(solution)/shard_map/ppermute | solution.py:35
  2392.1 45.5 %collective-permute-start.108 = (bf16[4,32,4224]{2,1,0:T(8,128)(2,1)S(1)}, bf16[4,32,4224]{2,1,0:T(8,128)(2,1)S(1)}, u32[]{:S(2)}, u32[]{:S(2)}) collective-permute-start(bf16[4,32,4224]{2,1,0:T(8,128)(2,1)S(1)} %pad_maximum_fusion.2), channel_id=1, source_target_pairs={{0,1},{1,0},{2,3},{3,2},{4,5},{5,4},{6,7},{7,6},{8,9},{9,8},{10,11... | collective-permute-start | bytes 3244040 | tf_op jit(solution)/shard_map/ppermute | solution.py:35
  2409.2 44.3 %collective-permute-start.99 = (bf16[4,32,4224]{2,1,0:T(8,128)(2,1)S(1)}, bf16[4,32,4224]{2,1,0:T(8,128)(2,1)S(1)}, u32[]{:S(2)}, u32[]{:S(2)}) collective-permute-start(bf16[4,32,4224]{2,1,0:T(8,128)(2,1)S(1)} %pad_maximum_fusion.1), channel_id=1, source_target_pairs={{0,2},{1,3},{2,0},{3,1},{4,6},{5,7},{6,4},{7,5},{8,10},{9,11},{10,... | collective-permute-start | bytes 3244040 | tf_op jit(solution)/shard_map/ppermute | solution.py:35
  2414.5 43.9 %collective-permute-start.97 = (bf16[4,32,4224]{2,1,0:T(8,128)(2,1)S(1)}, bf16[4,32,4224]{2,1,0:T(8,128)(2,1)S(1)}, u32[]{:S(2)}, u32[]{:S(2)}) collective-permute-start(bf16[4,32,4224]{2,1,0:T(8,128)(2,1)S(1)} %pad_maximum_fusion), channel_id=1, source_target_pairs={{0,1},{1,0},{2,3},{3,2},{4,5},{5,4},{6,7},{7,6},{8,9},{9,8},{10,11... | collective-permute-start | bytes 3244040 | tf_op jit(solution)/shard_map/ppermute | solution.py:35
  2437.7 51.2 %collective-permute-start.126 = (bf16[32,4096]{1,0:T(8,128)(2,1)S(1)}, bf16[32,4096]{1,0:T(8,128)(2,1)S(1)}, u32[]{:S(2)}, u32[]{:S(2)}) collective-permute-start(bf16[32,4096]{1,0:T(8,128)(2,1)S(1)} %get-tuple-element.257), channel_id=1, source_target_pairs={{12,8},{13,9},{14,10},{15,11},{28,24},{29,25},{30,26},{31,27}} | collective-permute-start | bytes 786440 | tf_op jit(solution)/shard_map/ppermute | solution.py:42
  2522.9 43.7 %collective-permute-start.136 = (bf16[32,4096]{1,0:T(8,128)(2,1)S(1)}, bf16[32,4096]{1,0:T(8,128)(2,1)S(1)}, u32[]{:S(2)}, u32[]{:S(2)}) collective-permute-start(bf16[32,4096]{1,0:T(8,128)(2,1)S(1)} %get-tuple-element.250), channel_id=1, source_target_pairs={{0,4},{1,5},{2,6},{3,7},{4,8},{5,9},{6,10},{7,11},{8,12},{9,13},{1... | collective-permute-start | bytes 786440 | tf_op jit(solution)/shard_map/ppermute | solution.py:42
  (292 other events, 10079.5 us)

commit v2 on v1

v2 whole, which is shorter than its diff:
```python
import functools
import jax
import jax.numpy as jnp
from jax import lax
from jax.experimental import pallas as pl
from jax.experimental.pallas import tpu as pltpu
from jax.sharding import PartitionSpec as P

HEADS = 16
HEAD = 64
SEQ = 50
STEP = 10
SIDE = 4
LEVELS = 4
GROUP = 200

norm_epsilon = 1e-06
clip_norm = 1.0
beta_one = 0.9
beta_two = 0.95
rate_matrix = 0.05
rate_vector = 1.0
decay_matrix = 0.1
epsilon = 1e-08
PAD = 128
LATE = ("G30", "H30",)
ORDER = (
    "G10", "G20", "G30", "G10", "G31", "G20", "G30", "G10", "G21", "G20", "G10", "G31", "G11",
    "G21", "G31", "G20", "G11", "G21", "G30", "G10", "G20", "G11", "G10", "G21", "G30", "G20",
    "G10", "F10", "F20", "G11", "G30", "G20", "F30", "G11", "G30", "G21", "G11", "G30", "G31",
    "F40", "G21", "G11", "F11", "F21", "G21", "F31", "G31", "H31", "G31", "H31", "G31", "B21",
    "B31", "B41", "H31", "B51", "H30", "B20", "H21", "H30", "H11", "H21", "H20", "H11", "H30",
    "H21", "B30", "B40", "H11", "H30", "B50", "H10", "H20", "H21", "H10", "H21", "H31", "H20",
    "H11", "H21", "F41", "H31", "H11", "H10", "H21", "H31", "H20", "H11", "H31", "H30", "H20",
    "H11", "H10", "H30", "H20", "H10", "H30", "H20", "H10", "H10",
)
low_type = jnp.bfloat16
wide = jnp.float32


def swap_cores(x):
    return lax.ppermute(x, "section", [(0, 1), (1, 0)])


def flip(x, bit):
    count = lax.axis_size("dp")
    return lax.ppermute(x, "dp", [(i, i ^ bit) for i in range(count)])


def shift(x, levels, by):
    pairs = [
        (level * SIDE + q, (level + by) * SIDE + q) for level in levels for q in range(SIDE)
    ]
    return lax.ppermute(x, "dp", pairs)


class Line:
    def __init__(self):
        self.token = jnp.zeros((), wide)

    def sync(self, *values):
        fenced = lax.optimization_barrier((self.token, *values))
        self.token = fenced[0]
        return fenced[1:]


def swap_halves(here, there, first):
    got = swap_cores(there)
    return jnp.where(first, here, got), jnp.where(first, got, here)


def place_blocks(blocks, me, axis):
    shape = list(blocks[0].shape)
    shape.insert(axis, SIDE)
    full = jnp.zeros(shape, blocks[0].dtype)
    for relative, block in enumerate(blocks):
        start = [0] * len(shape)
        start[axis] = jnp.bitwise_xor(me, relative)
        full = lax.dynamic_update_slice(full, jnp.expand_dims(block, axis), start)
    return full


def gather_flow(line, part, level, me, key, state):
    half = LEVELS // 2
    (part,) = line.sync(part)
    ups, downs = [], []
    up = down = part
    for step in range(1, LEVELS):
        up = shift(up, range(step - 1, LEVELS - 1), 1)
        down = shift(down, range(1, LEVELS + 1 - step), -1)
        yield
        up, down = line.sync(up, down)
        ups.append(up)
        downs.append(down)
    chain = jnp.stack(ups[::-1] + [part] + downs)
    column = lax.dynamic_slice_in_dim(chain, LEVELS - 1 - level, LEVELS, axis=0)
    across = flip(column, 1)
    along = flip(column, 2)
    yield
    across, along, column = line.sync(across, along, column)
    corner_low = flip(along[:half], 1)
    corner_high = flip(across[half:], 2)
    full = place_blocks([column, across, along], me, 1)
    yield
    corner_low, corner_high, full = line.sync(corner_low, corner_high, full)
    corner = jnp.bitwise_xor(me, 3)
    full = lax.dynamic_update_slice(full, corner_low[:, None], (0, corner, 0, 0))
    full = lax.dynamic_update_slice(full, corner_high[:, None], (half, corner, 0, 0))
    mine = full.reshape(-1, part.shape[1])
    theirs = swap_cores(mine)
    yield
    state[key] = line.sync(mine, theirs)
    yield


def gather_flow_late(line, part, level, me, key, state):
    rows = part.shape[0]
    half = rows // 2
    (part,) = line.sync(part)
    across = flip(part, 1)
    along = flip(part, 2)
    yield
    across, along = line.sync(across, along)
    corner_low = flip(along[:half], 1)
    corner_high = flip(across[half:], 2)
    yield
    corner_low, corner_high = line.sync(corner_low, corner_high)
    block = place_blocks([part, across, along, jnp.concatenate([corner_low, corner_high])], me, 0)
    ups, downs = [], []
    up = down = block
    for step in range(1, LEVELS):
        up = shift(up, range(step - 1, LEVELS - 1), 1)
        down = shift(down, range(1, LEVELS + 1 - step), -1)
        yield
        up, down = line.sync(up, down)
        ups.append(up)
        downs.append(down)
    chain = jnp.stack(ups[::-1] + [block] + downs)
    full = lax.dynamic_slice_in_dim(chain, LEVELS - 1 - level, LEVELS, axis=0)
    mine = full.reshape(-1, part.shape[1])
    theirs = swap_cores(mine)
    yield
    state[key] = line.sync(mine, theirs)
    yield


def add_low(left, right):
    return (left.astype(wide) + right.astype(wide)).astype(low_type)


def pick(array, index, axis):
    last = array.shape[axis] - 1
    return lax.dynamic_index_in_dim(array, jnp.clip(index, 0, last), axis, keepdims=False)


def chip_sum(line, make_there, make_here):
    there = make_there()
    got = swap_cores(there)
    yield
    (got,) = line.sync(got)
    total = make_here(got)
    return total.reshape(LEVELS, SIDE, total.shape[0] // (LEVELS * SIDE), total.shape[1])


def scatter_flow(line, make_there, make_here, level, me, key, state):
    half = LEVELS // 2
    chip = yield from chip_sum(line, make_there, make_here)
    corner = pick(chip, jnp.bitwise_xor(me, 3), 1)
    from_across = flip(corner[:half], 1)
    from_along = flip(corner[half:], 2)
    yield
    from_across, from_along, chip = line.sync(from_across, from_along, chip)
    along = pick(chip, jnp.bitwise_xor(me, 2), 1)
    across = pick(chip, jnp.bitwise_xor(me, 1), 1)
    along = jnp.concatenate([add_low(along[:half], from_across), along[half:]])
    across = jnp.concatenate([across[:half], add_low(across[half:], from_along)])
    got_across = flip(across, 1)
    got_along = flip(along, 2)
    own = pick(chip, me, 1)
    yield
    got_across, got_along, own = line.sync(got_across, got_along, own)
    column = own.astype(wide) + got_across.astype(wide) + got_along.astype(wide)
    up = down = jnp.zeros((), wide)
    for step in range(1, LEVELS):
        far = LEVELS - step
        up = shift((pick(column, level + far, 0) + up).astype(low_type), range(0, step), 1)
        down = shift(
            (pick(column, level - far, 0) + down).astype(low_type),
            range(LEVELS - step, LEVELS),
            -1,
        )
        yield
        up, down, column = line.sync(up, down, column)
        up, down = up.astype(wide), down.astype(wide)
    state[key] = line.sync(pick(column, level, 0) + up + down)[0]
    yield


def scatter_flow_late(line, make_there, make_here, level, me, key, state):
    chip = yield from chip_sum(line, make_there, make_here)
    half = chip.shape[2] // 2
    up = down = jnp.zeros((), wide)
    for step in range(1, LEVELS):
        far = LEVELS - step
        up = shift((pick(chip, level + far, 0) + up).astype(low_type), range(0, step), 1)
        down = shift(
            (pick(chip, level - far, 0) + down).astype(low_type), range(LEVELS - step, LEVELS), -1
        )
        yield
        up, down, chip = line.sync(up, down, chip)
        up, down = up.astype(wide), down.astype(wide)
    block = pick(chip, level, 0).astype(wide) + up + down
    corner = pick(block, jnp.bitwise_xor(me, 3), 0).astype(low_type)
    from_across = flip(corner[:half], 1)
    from_along = flip(corner[half:], 2)
    yield
    from_across, from_along, block = line.sync(from_across, from_along, block)
    along = pick(block, jnp.bitwise_xor(me, 2), 0)
    across = pick(block, jnp.bitwise_xor(me, 1), 0)
    along = jnp.concatenate([along[:half] + from_across.astype(wide), along[half:]])
    across = jnp.concatenate([across[:half], across[half:] + from_along.astype(wide)])
    got_across = flip(across.astype(low_type), 1)
    got_along = flip(along.astype(low_type), 2)
    yield
    got_across, got_along, block = line.sync(got_across, got_along, block)
    total = pick(block, me, 0) + got_across.astype(wide) + got_along.astype(wide)
    state[key] = line.sync(total)[0]
    yield


def gather_plain(line, part, key, state):
    (part,) = line.sync(part)
    mine = lax.all_gather(part, "dp", axis=0, tiled=True)
    state[key] = line.sync(mine, swap_cores(mine))
    yield


def scatter_plain(line, make_there, make_here, key, state):
    (got,) = line.sync(swap_cores(make_there()))
    total = make_here(got).astype(wide)
    state[key] = line.sync(lax.psum_scatter(total, "dp", scatter_dimension=0, tiled=True))[0]
    yield


def total_of(value):
    value = value + swap_cores(value)
    across, along, corner = flip(value, 1), flip(value, 2), flip(value, 3)
    value = (value + across) + (along + corner)
    count = lax.axis_size("dp")

    def turn(by):
        pairs = [(i, (i + by * SIDE) % count) for i in range(count)]
        return lax.ppermute(value, "dp", pairs)

    one, two, three = turn(1), turn(2), turn(3)
    return (value + two) + (one + three)


def normalize(inputs):
    centered = inputs - jnp.mean(inputs, axis=-1, keepdims=True)
    inverse = lax.rsqrt(jnp.mean(centered * centered, axis=-1, keepdims=True) + norm_epsilon)
    return (centered * inverse, inverse)


def normalize_back(upstream, scaled, inverse):
    return inverse * (
        upstream
        - jnp.mean(upstream, axis=-1, keepdims=True)
        - scaled * jnp.mean(upstream * scaled, axis=-1, keepdims=True)
    )


def dot_nt(left, right):
    return lax.dot_general(left, right, (((1,), (1,)), ((), ())), preferred_element_type=wide)


def dot_nn(left, right):
    return lax.dot_general(left, right, (((1,), (0,)), ((), ())), preferred_element_type=wide)


def dot_tn(left, right):
    return lax.dot_general(left, right, (((0,), (0,)), ((), ())), preferred_element_type=wide)


def same_image(rows):
    image_row = lax.broadcasted_iota(jnp.int32, (rows, rows), 0) // SEQ
    image_col = lax.broadcasted_iota(jnp.int32, (rows, rows), 1) // SEQ
    return image_row == image_col


def attend_kernel(q_ref, k_ref, v_ref, o_ref):
    rows = q_ref.shape[1]
    mask = same_image(rows)
    lane = lax.broadcasted_iota(jnp.int32, (rows, 2 * HEAD), 1)
    queries, keys, values = q_ref[0], k_ref[0], v_ref[0]
    queries = queries * jnp.asarray(HEAD ** (-0.5), low_type)
    mixed = []
    for head in range(2):
        inside = (lane >= head * HEAD) & (lane < (head + 1) * HEAD)
        own = jnp.where(inside, queries, jnp.zeros_like(queries))
        scores = jnp.where(mask, dot_nt(own, keys), -jnp.inf)
        raised = jnp.exp(scores - jnp.max(scores, axis=1, keepdims=True))
        weights = raised * (1.0 / jnp.sum(raised, axis=1, keepdims=True))
        mixed.append(dot_nn(weights.astype(low_type), values))
    o_ref[0] = jnp.where(lane < HEAD, mixed[0], mixed[1]).astype(low_type)


def block_at(third, blocks, rows):
    return pl.BlockSpec((1, rows, 2 * HEAD), lambda i, j: (i, 0, third * blocks + j))


def attend(packed):
    rows, columns = packed.shape
    blocks = columns // 3 // (2 * HEAD)
    groups = rows // GROUP
    packed = packed.reshape(groups, GROUP, columns)
    mixed = pl.pallas_call(
        attend_kernel,
        grid=(groups, blocks),
        in_specs=[block_at(third, blocks, GROUP) for third in range(3)],
        out_specs=block_at(0, blocks, GROUP),
        out_shape=jax.ShapeDtypeStruct((groups, GROUP, columns // 3), low_type),
        cost_estimate=pl.CostEstimate(
            flops=8 * rows * GROUP * columns // 3,
            bytes_accessed=8 * rows * columns // 3,
            transcendentals=rows * GROUP * columns // 3 // HEAD,
        ),
        compiler_params=pltpu.CompilerParams(vmem_limit_bytes=32 * 1024 * 1024),
        name="attend",
    )(packed, packed, packed)
    return mixed.reshape(rows, columns // 3)


def attend_back_kernel(q_ref, k_ref, v_ref, g_ref, dq_ref, dk_ref, dv_ref):
    rows = q_ref.shape[1]
    mask = same_image(rows)
    lane = lax.broadcasted_iota(jnp.int32, (rows, 2 * HEAD), 1)
    queries, keys, values, upstream = q_ref[0], k_ref[0], v_ref[0], g_ref[0]
    scaling = HEAD ** (-0.5)
    queries = queries * jnp.asarray(scaling, low_type)
    to_queries, to_keys, to_values = [], [], []
    for head in range(2):
        inside = (lane >= head * HEAD) & (lane < (head + 1) * HEAD)
        zero = jnp.zeros_like(queries)
        own_queries = jnp.where(inside, queries, zero)
        own_upstream = jnp.where(inside, upstream, zero)
        scores = jnp.where(mask, dot_nt(keys, own_queries), -jnp.inf)
        raised = jnp.exp(scores - jnp.max(scores, axis=0, keepdims=True))
        weights = raised * (1.0 / jnp.sum(raised, axis=0, keepdims=True))
        to_values.append(dot_nn(weights.astype(low_type), upstream))
        slope = dot_nt(values, own_upstream)
        inner = jnp.sum(weights * slope, axis=0, keepdims=True)
        change = (weights * (slope - inner)).astype(low_type)
        to_keys.append(dot_nn(change, queries))
        to_queries.append(dot_tn(keys, change))
    lower = lane < HEAD
    dv_ref[0] = jnp.where(lower, to_values[0], to_values[1]).astype(low_type)
    dk_ref[0] = jnp.where(lower, to_keys[0], to_keys[1]).astype(low_type)
    turned = jnp.concatenate([to_queries[0][:HEAD], to_queries[1][HEAD:]], axis=0)
    dq_ref[0] = (turned.T * scaling).astype(low_type)


def attend_back(packed, upstream):
    rows, columns = packed.shape
    blocks = columns // 3 // (2 * HEAD)
    groups = rows // GROUP
    packed = packed.reshape(groups, GROUP, columns)
    upstream = upstream.reshape(groups, GROUP, columns // 3)
    shape = jax.ShapeDtypeStruct((groups, GROUP, columns // 3), low_type)
    slopes = pl.pallas_call(
        attend_back_kernel,
        grid=(groups, blocks),
        in_specs=[block_at(third, blocks, GROUP) for third in (0, 1, 2, 0)],
        out_specs=[block_at(0, blocks, GROUP)] * 3,
        out_shape=[shape] * 3,
        cost_estimate=pl.CostEstimate(
            flops=20 * rows * GROUP * columns // 3,
            bytes_accessed=14 * rows * columns // 3,
            transcendentals=rows * GROUP * columns // 3 // HEAD,
        ),
        compiler_params=pltpu.CompilerParams(vmem_limit_bytes=32 * 1024 * 1024),
        name="attend_back",
    )(packed, packed, packed, upstream)
    return jnp.concatenate([part.reshape(rows, columns // 3) for part in slopes], axis=1)


def dot(left, right):
    return jnp.dot(left, right, preferred_element_type=wide)


def back_dot(left, right):
    return jnp.einsum("nf,df->nd", left, right, preferred_element_type=wide)


def weight_dot(left, right):
    return jnp.einsum("nd,nf->df", left, right, preferred_element_type=wide)


def adam_update(weight, grad, first, second, factor, rate, decay):
    clipped = grad * factor
    momentum = beta_one * first + (1.0 - beta_one) * clipped
    variance = beta_two * second + (1.0 - beta_two) * clipped * clipped
    corrected_m = momentum / (1.0 - beta_one**STEP)
    corrected_v = variance / (1.0 - beta_two**STEP)
    updated = weight - rate * (corrected_m / (jnp.sqrt(corrected_v) + epsilon) + decay * weight)
    return (updated, momentum, variance)


def body(
    patches,
    live,
    cotangent,
    w_qkv,
    w_proj,
    w_in,
    w_out,
    vectors,
    first_qkv,
    first_proj,
    first_in,
    first_out,
    first_vectors,
    second_qkv,
    second_proj,
    second_in,
    second_out,
    second_vectors,
):
    core = lax.axis_index("section")
    first = core == 0
    chip = lax.axis_index("dp")
    count_dp = lax.axis_size("dp")
    tuned = count_dp == LEVELS * SIDE
    level = chip // SIDE
    me = chip % SIDE
    masters = (w_qkv[0], w_proj[0], w_in[0], w_out[0], vectors[0])
    width = patches.shape[1]
    half_width = width // 2
    hidden_width = w_in.shape[2]
    half_vectors = vectors.shape[1] // 2
    half_qkv = w_qkv.shape[2] // 2
    stripe = hidden_width // (2 * count_dp)
    tokens = patches.shape[0] // 2
    images = live.shape[0] // 2
    line = Line()
    state = {}

    def halves_of(array, groups):
        rows = array.shape[0]
        shaped = array.reshape(rows, groups, 2, -1)
        return tuple(shaped[:, :, side].reshape(rows, -1) for side in range(2))

    def choose(pair):
        return jnp.where(first, pair[0], pair[1]), jnp.where(first, pair[1], pair[0])

    def join(here, there):
        return jnp.where(
            first,
            jnp.concatenate([here, there], axis=-1),
            jnp.concatenate([there, here], axis=-1),
        )

    def prepare():
        lowered = [m.astype(low_type) for m in masters]
        qkv, proj = halves_of(lowered[0], 3), halves_of(lowered[1], 1)
        turned = lowered[4].T
        pad = jnp.zeros((turned.shape[0], PAD - half_vectors), low_type)
        packs = [
            tuple(
                jnp.concatenate(
                    [
                        qkv[side],
                        proj[side],
                        turned[:, side * half_vectors : (side + 1) * half_vectors],
                        pad,
                    ],
                    axis=1,
                )
                for side in range(2)
            ),
            halves_of(lowered[2], count_dp),
            tuple(jnp.split(lowered[3], 2, axis=0)),
        ]
        for number, pack in enumerate(packs):
            here, there = choose(pack)
            parts = swap_halves(here, there, first)
            for layer in range(2):
                state[f"part{number + 1}{layer}"] = parts[layer]
        entry = lax.dynamic_slice_in_dim(patches, core * tokens, tokens, axis=0)
        state["x0"] = entry.astype(wide)
        weighting = lax.dynamic_slice_in_dim(live, core * images, images, axis=0).astype(wide)
        target = lax.dynamic_slice_in_dim(cotangent, core * tokens, tokens, axis=0).astype(wide)
        target = target.reshape(images, SEQ, width) * weighting.reshape(images, 1, 1)
        state["dy1"] = target.reshape(tokens, width)

    def take(*names):
        values = line.sync(*[state[name] for name in names])
        state.update(zip(names, values))
        return values

    def give(**values):
        state.update(zip(values, line.sync(*values.values())))

    def two(name):
        return [f"{name}_here", f"{name}_there"]

    def split_first(layer):
        halves = state[f"G1{layer}"]
        qkv = [h[:, :half_qkv] for h in halves]
        proj = [h[:, half_qkv : half_qkv + half_width] for h in halves]
        start = half_qkv + half_width
        rows = join(*[h[:, start : start + half_vectors] for h in halves]).T.astype(wide)
        return qkv, proj, rows

    def forward_one(layer):
        (inputs,) = take(f"x{layer}")
        qkv, proj, rows = split_first(layer)
        scaled, _ = normalize(inputs)
        hidden = (scaled * rows[0] + rows[1]).astype(low_type)
        biases = [halves_of(rows[i : i + 1], 1) for i in (2, 3)]
        query_bias, value_bias = [choose(pair) for pair in biases]
        packed = []
        for side in range(2):
            zero = jnp.zeros_like(query_bias[side])
            bias = jnp.concatenate([query_bias[side], zero, value_bias[side]], axis=1)
            packed.append((dot(hidden, qkv[side]) + bias).astype(low_type))
        give(
            **{
                f"rows{layer}": rows,
                f"hidden{layer}": hidden,
                f"packed_here{layer}": packed[0],
                f"packed_there{layer}": packed[1],
            }
        )

    def forward_two(layer):
        here, there, rows, inputs = take(
            f"packed_here{layer}", f"packed_there{layer}", f"rows{layer}", f"x{layer}"
        )
        _, proj, _ = split_first(layer)
        mixed = join(attend(here), attend(there))
        branch = join(*[dot(mixed, w) for w in proj])
        middle = inputs + (branch + rows[4])
        scaled, _ = normalize(middle)
        hidden = (scaled * rows[5] + rows[6]).astype(low_type)
        give(**{f"mixed{layer}": mixed, f"middle{layer}": middle, f"hidden_two{layer}": hidden})

    def forward_three(layer):
        hidden, rows = take(f"hidden_two{layer}", f"rows{layer}")
        bias = choose(halves_of(rows[8:12].reshape(1, -1), count_dp))
        out = {}
        for side, name in enumerate(("here", "there")):
            pre_act = dot(hidden, state[f"G2{layer}"][side]) + bias[side]
            cdf = 0.5 * (1.0 + lax.erf(pre_act * 0.7071067811865476))
            density = jnp.exp(-0.5 * pre_act * pre_act) * 0.3989422804014327
            out[f"active_{name}{layer}"] = (pre_act * cdf).astype(low_type)
            out[f"slope_{name}{layer}"] = (cdf + pre_act * density).astype(low_type)
        give(**out)

    def forward_four(layer):
        here, there, middle, rows = take(
            f"active_here{layer}", f"active_there{layer}", f"middle{layer}", f"rows{layer}"
        )
        weights = state[f"G3{layer}"]
        output = middle + (dot(here, weights[0]) + dot(there, weights[1]) + rows[7])
        output = output.astype(low_type)
        give(**{f"block{layer}": output, f"x{layer + 1}": output.astype(wide)})

    def out_grad(layer, side):
        def make(got=None):
            name = "here" if side == 0 else "there"
            active, upstream = take(f"active_{name}{layer}", f"dy{layer}")
            grad = weight_dot(active, upstream.astype(low_type))
            return finish(grad, got)

        return make

    def finish(grad, got):
        if got is not None:
            grad = grad + got.astype(wide)
        return line.sync(grad.astype(low_type))[0]

    def in_grad(layer, side):
        def make(got=None):
            name = "here" if side == 0 else "there"
            hidden, grad_pre = take(f"hidden_two{layer}", f"grad_pre_{name}{layer}")
            return finish(weight_dot(hidden, grad_pre), got)

        return make

    def first_grad(layer, side):
        def make(got=None):
            name = "here" if side == 0 else "there"
            hidden, grad_packed, mixed, branch, rows = take(
                f"hidden{layer}",
                f"grad_packed_{name}{layer}",
                f"mixed{layer}",
                f"grad_branch_{name}{layer}",
                f"grad_rows{layer}",
            )
            parts = jnp.split(rows, 2, axis=0)
            turned = choose(parts)[side].T
            turned = jnp.pad(turned, ((0, 0), (0, PAD - half_vectors)))
            grads = [weight_dot(hidden, grad_packed), weight_dot(mixed, branch), turned]
            if got is not None:
                start = half_qkv + half_width
                cuts = (got[:, :half_qkv], got[:, half_qkv:start], got[:, start:])
                grads = [a + b.astype(wide) for a, b in zip(grads, cuts)]
            return line.sync(jnp.concatenate([g.astype(low_type) for g in grads], axis=1))[0]

        return make

    def backward_two(layer):
        (upstream,) = take(f"dy{layer}")
        upstream_low = upstream.astype(low_type)
        out = {}
        sums = []
        for side, name in enumerate(("here", "there")):
            (slope,) = take(f"slope_{name}{layer}")
            grad_active = back_dot(upstream_low, state[f"G3{layer}"][side])
            grad_pre = (grad_active * slope.astype(wide)).astype(low_type)
            out[f"grad_pre_{name}{layer}"] = grad_pre
            sums.append(jnp.sum(grad_pre.astype(wide), axis=0))
        give(**out)
        state[f"bias_in{layer}"] = sums
        state[f"bias_out{layer}"] = jnp.sum(upstream_low.astype(wide), axis=0)

    def backward_three(layer):
        here, there, middle, rows, upstream = take(
            f"grad_pre_here{layer}",
            f"grad_pre_there{layer}",
            f"middle{layer}",
            f"rows{layer}",
            f"dy{layer}",
        )
        weights = state[f"G2{layer}"]
        _, proj, _ = split_first(layer)
        scaled, inverse = normalize(middle)
        grad_hidden = back_dot(here, weights[0]) + back_dot(there, weights[1])
        gain, bias = jnp.sum(grad_hidden * scaled, axis=0), jnp.sum(grad_hidden, axis=0)
        grad_middle = upstream + normalize_back(grad_hidden * rows[5], scaled, inverse)
        branch = grad_middle.astype(low_type)
        sides = choose(halves_of(branch, 1))
        grad_mixed = back_dot(sides[0], proj[0]) + back_dot(sides[1], proj[1])
        mixed_sides = choose(halves_of(grad_mixed.astype(low_type), 1))
        state[f"norm_two{layer}"] = (gain, bias, jnp.sum(branch.astype(wide), axis=0))
        give(
            **{
                f"grad_middle{layer}": grad_middle,
                f"grad_branch_here{layer}": sides[0],
                f"grad_branch_there{layer}": sides[1],
                f"grad_mixed_here{layer}": mixed_sides[0],
                f"grad_mixed_there{layer}": mixed_sides[1],
            }
        )

    def backward_four(layer):
        out = {}
        for name in ("here", "there"):
            packed, upstream = take(f"packed_{name}{layer}", f"grad_mixed_{name}{layer}")
            out[f"grad_packed_{name}{layer}"] = attend_back(packed, upstream)
        give(**out)

    def backward_five(layer):
        here, there, inputs, rows, grad_middle = take(
            f"grad_packed_here{layer}",
            f"grad_packed_there{layer}",
            f"x{layer}",
            f"rows{layer}",
            f"grad_middle{layer}",
        )
        qkv, _, _ = split_first(layer)
        scaled, inverse = normalize(inputs)
        grad_hidden = back_dot(here, qkv[0]) + back_dot(there, qkv[1])
        gain, bias = jnp.sum(grad_hidden * scaled, axis=0), jnp.sum(grad_hidden, axis=0)
        grad_entry = grad_middle + normalize_back(grad_hidden * rows[0], scaled, inverse)
        grad_entry = grad_entry.astype(low_type)
        third = half_qkv // 3
        columns = [jnp.sum(side.astype(wide), axis=0)[None] for side in (here, there)]
        query = join(*[c[:, :third] for c in columns])[0]
        value = join(*[c[:, 2 * third :] for c in columns])[0]
        gain_two, bias_two, bias_proj = state[f"norm_two{layer}"]
        bias_in = jnp.where(
            first,
            jnp.stack([s.reshape(count_dp, stripe) for s in state[f"bias_in{layer}"]], axis=1),
            jnp.stack([s.reshape(count_dp, stripe) for s in state[f"bias_in{layer}"][::-1]], axis=1),
        )
        grad_rows = jnp.stack(
            [gain, bias, query, value, bias_proj, gain_two, bias_two, state[f"bias_out{layer}"]]
        )
        grad_rows = jnp.concatenate([grad_rows, bias_in.reshape(4, width)], axis=0)
        give(**{f"entry{layer}": grad_entry, f"grad_rows{layer}": grad_rows})
        if layer == 1:
            state["dy0"] = state["entry1"].astype(wide)

    steps = {
        "F1": forward_one,
        "F2": forward_two,
        "F3": forward_three,
        "F4": forward_four,
        "B2": backward_two,
        "B3": backward_three,
        "B4": backward_four,
        "B5": backward_five,
    }
    makers = {"1": first_grad, "2": in_grad, "3": out_grad}
    prepare()
    flows = {}
    for layer in range(2):
        for number in "123":
            key = f"G{number}{layer}"
            part = state[f"part{number}{layer}"]
            if not tuned:
                flows[key] = gather_plain(line, part, key, state)
            elif key in LATE:
                flows[key] = gather_flow_late(line, part, level, me, key, state)
            else:
                flows[key] = gather_flow(line, part, level, me, key, state)
            key = f"H{number}{layer}"
            there, here = makers[number](layer, 1), makers[number](layer, 0)
            if not tuned:
                flows[key] = scatter_plain(line, there, here, key, state)
            elif key in LATE:
                flows[key] = scatter_flow_late(line, there, here, level, me, key, state)
            else:
                flows[key] = scatter_flow(line, there, here, level, me, key, state)
    for event in ORDER:
        if event in flows:
            next(flows[event], None)
        else:
            steps[event[:2]](int(event[2]))
    for key in flows:
        for _ in flows[key]:
            pass

    halves = [[state[f"H{number}{layer}"] for layer in range(2)] for number in "123"]
    local_sum = sum((jnp.sum(part * part) for pair in halves for part in pair))
    if tuned:
        global_sum = total_of(local_sum)
    else:
        global_sum = lax.psum(local_sum, ("section", "dp"))
    grad_norm = jnp.sqrt(global_sum)
    factor = clip_norm / jnp.maximum(grad_norm, clip_norm)

    def own_layer(pair):
        got = swap_cores(jnp.where(first, pair[1], pair[0]))
        mine = jnp.where(first, pair[0], pair[1])
        return jnp.where(first, mine, got), jnp.where(first, got, mine)

    def woven(pair, groups):
        rows = pair[0].shape[0]
        return jnp.stack([p.reshape(rows, groups, -1) for p in pair], axis=2).reshape(rows, -1)

    one, inner, outer = [own_layer(pair) for pair in halves]
    start = half_qkv + half_width
    shards = (
        woven([p[:, :half_qkv] for p in one], 3),
        jnp.concatenate([p[:, half_qkv:start] for p in one], axis=1),
        woven(inner, count_dp),
        jnp.concatenate(outer, axis=0),
        jnp.concatenate([p[:, start : start + half_vectors] for p in one], axis=1).T,
    )

    def own_tokens(zero, one):
        got = swap_cores(jnp.where(first, one, zero))
        mine = jnp.where(first, zero, one)
        return jnp.where(
            first, jnp.concatenate([mine, got], axis=0), jnp.concatenate([got, mine], axis=0)
        )

    blocks = own_tokens(state["block0"], state["block1"])
    input_grad = own_tokens(state["entry0"], state["entry1"])
    firsts = (first_qkv[0], first_proj[0], first_in[0], first_out[0], first_vectors[0])
    seconds = (second_qkv[0], second_proj[0], second_in[0], second_out[0], second_vectors[0])
    rates = (rate_matrix, rate_matrix, rate_matrix, rate_matrix, rate_vector)
    decays = (decay_matrix, decay_matrix, decay_matrix, decay_matrix, 0.0)
    results = [
        adam_update(w, g, f, s, factor, r, d)
        for w, g, f, s, r, d in zip(masters, shards, firsts, seconds, rates, decays)
    ]
    news = tuple((item[0][None] for item in results))
    momenta = tuple((item[1][None] for item in results))
    variances = tuple((item[2][None] for item in results))
    copies = tuple((n.astype(low_type) for n in news))
    grads_out = tuple((s[None] for s in shards))
    return (
        blocks[None],
        input_grad[None],
        *grads_out,
        grad_norm,
        *news,
        *copies,
        *momenta,
        *variances,
    )


def solution(mesh):
    in_specs = (
        P("dp", None),
        P("dp"),
        P("dp", None),
        P("section", "dp", None),
        P("section", "dp", None),
        P("section", "dp", None),
        P("section", "dp", None),
        P("section", None, "dp"),
        P("section", "dp", None),
        P("section", "dp", None),
        P("section", "dp", None),
        P("section", "dp", None),
        P("section", None, "dp"),
        P("section", "dp", None),
        P("section", "dp", None),
        P("section", "dp", None),
        P("section", "dp", None),
        P("section", None, "dp"),
    )
    out_specs = (
        P("section", "dp", None),
        P("section", "dp", None),
        P("section", "dp", None),
        P("section", "dp", None),
        P("section", "dp", None),
        P("section", "dp", None),
        P("section", None, "dp"),
        P(),
        P("section", "dp", None),
        P("section", "dp", None),
        P("section", "dp", None),
        P("section", "dp", None),
        P("section", None, "dp"),
        P("section", "dp", None),
        P("section", "dp", None),
        P("section", "dp", None),
        P("section", "dp", None),
        P("section", None, "dp"),
        P("section", "dp", None),
        P("section", "dp", None),
        P("section", "dp", None),
        P("section", "dp", None),
        P("section", None, "dp"),
        P("section", "dp", None),
        P("section", "dp", None),
        P("section", "dp", None),
        P("section", "dp", None),
        P("section", None, "dp"),
    )
    return jax.shard_map(body, mesh=mesh, in_specs=in_specs, out_specs=out_specs, check_vma=False)
```

time: 2690 us -> 1010 us (0.38)
  Pallas kernels: 1610 us -> 71.7 us
  waiting for transfers between devices: 441 us -> 228 us
  local copies, waits for them, and re-layouts: 59.3 us -> 138 us
  starting transfers between devices: 308 us -> 249 us
    pallas_call x10 -> x8, Pallas kernels: 1610 us -> 71.7 us  [the longest x4 41.1 us: attend_back(): pl.pallas_call(attend_back_kernel, grid=(groups, blocks), in_specs=[block...]
    ppermute x51, waiting for transfers between devices: 319 us -> 128 us  [flip(): return lax.ppermute(x, 'dp', [(i, i ^ bit) for i in range(count)])]
    ppermute x72, starting transfers between devices: 206 us -> 177 us  [shift(): return lax.ppermute(x, 'dp', pairs)]
    dynamic_update_slice x0 -> x28, local copies, waits for them, and re-layouts: none -> 27.6 us  [the longest x18 22.4 us: place_blocks(): full = lax.dynamic_update_slice(full, jnp.expand_dims(block, axis), start)]
    dot_general x8 -> x16, matrix products: 44.4 us -> 63.1 us  [back_dot(): return jnp.einsum('nf,df->nd', left, right, preferred_element_type=wide)]
    dot_general x8 -> x16, matrix products: 64.4 us -> 57.1 us  [dot(): return jnp.dot(left, right, preferred_element_type=wide)]
  transfers between devices with their start and end apart: 171 -> 147, of which waited for: 77 -> 37; matrix products, arithmetic and copies ran while one was open for 4% -> 37% of each run, Pallas kernels for 48% -> 7%
where the time goes in v2:
time: 1010 us; the launch traced here: 996 us
  starting transfers between devices  249 us (25%)
  waiting for transfers between devices  228 us (23%)
  matrix products  173 us (17%)
  local copies, waits for them, and re-layouts  138 us (14%)
  other arithmetic  121 us (12%)
  Pallas kernels  71.7 us (7%)
  between operations  15.6 us (2%)
    ppermute x72, starting transfers between devices, shift(): return lax.ppermute(x, 'dp', pairs)  177 us
    ppermute x51, waiting for transfers between devices, flip(): return lax.ppermute(x, 'dp', [(i, i ^ bit) for i in range(count)])  128 us
    ppermute x72, waiting for transfers between devices, shift(): return lax.ppermute(x, 'dp', pairs)  100 us
    dot_general x16, matrix products, back_dot(): return jnp.einsum('nf,df->nd', left, right, preferred_element_type=wide)  63.1 us
    ppermute x51, starting transfers between devices, flip(): return lax.ppermute(x, 'dp', [(i, i ^ bit) for i in range(count)])  59.9 us
    dot_general x16, matrix products, dot(): return jnp.dot(left, right, preferred_element_type=wide)  57.1 us
    dot_general x16, matrix products, weight_dot(): return jnp.einsum('nd,nf->df', left, right, preferred_element_type=wide)  52.8 us
    pallas_call x4, Pallas kernels, attend_back(): pl.pallas_call(attend_back_kernel, grid=(groups, blocks), in_specs=[block...  41.1 us
  transfers between devices with their start and end apart: 147, of which 37 were waited for; matrix products, arithmetic and copies ran while one was open for 37% of the time, Pallas kernels for 7%

profile of v2, /device:TPU:0, one launch (start us, length us, event | category | flops | bytes accessed | tf_op | source)
XLA Modules:
  0.0 995.6 jit_solution(3659847626792406770)
XLA Ops:
  33.8 9.3 collective-permute-done.6
  64.7 11.1 %collective-permute-done.14 = bf16[64,2176]{1,0:T(8,128)(2,1)S(1)} collective-permute-done((bf16[64,2176]{1,0:T(8,128)(2,1)}, bf16[64,2176]{1,0:T(8,128)(2,1)S(1)}, u32[]{:S(2)}, u32[]{:S(2)}) %collective-permute-start.14) | collective-permute-done | bytes 278560 | tf_op jit(solution)/shard_map/ppermute | solution.py:54
  100.4 8.7 collective-permute-done.26
  109.6 10.9 %collective-permute-done.27 = bf16[64,1024]{1,0:T(8,128)(2,1)S(1)} collective-permute-done((bf16[64,1024]{1,0:T(8,128)(2,1)S(1)}, bf16[64,1024]{1,0:T(8,128)(2,1)S(1)}, u32[]{:S(2)}, u32[]{:S(2)}) %collective-permute-start.27) | collective-permute-done | bytes 131104 | tf_op jit(solution)/shard_map/ppermute | solution.py:47
  127.3 15.7 %collective-permute-done.31 = bf16[4,64,2048]{2,1,0:T(8,128)(2,1)S(1)} collective-permute-done((bf16[4,64,2048]{2,1,0:T(8,128)(2,1)S(1)}, bf16[4,64,2048]{2,1,0:T(8,128)(2,1)S(1)}, u32[]{:S(2)}, u32[]{:S(2)}) %collective-permute-start.31) | collective-permute-done | bytes 1048608 | tf_op jit(solution)/shard_map/ppermute | solution.py:47
  160.6 13.8 %collective-permute-done.38 = bf16[64,2048]{1,0:T(8,128)(2,1)S(1)} collective-permute-done((bf16[64,2048]{1,0:T(8,128)(2,1)S(1)}, bf16[64,2048]{1,0:T(8,128)(2,1)S(1)}, u32[]{:S(2)}, u32[]{:S(2)}) %collective-permute-start.38) | collective-permute-done | bytes 262176 | tf_op jit(solution)/shard_map/ppermute | solution.py:54
  196.9 7.7 attend.5
  205.6 7.6 attend.4
  228.6 21.6 %collective-permute-done.49 = bf16[4,64,2176]{2,1,0:T(8,128)(2,1)} collective-permute-done((bf16[4,64,2176]{2,1,0:T(8,128)(2,1)S(1)}, bf16[4,64,2176]{2,1,0:T(8,128)(2,1)}, u32[]{:S(2)}, u32[]{:S(2)}) %collective-permute-start.49) | collective-permute-done | bytes 1114144 | tf_op jit(solution)/shard_map/ppermute | solution.py:47
  251.5 6.6 fusion.8
  258.1 6.9 fusion.13
  265.1 7.9 collective-permute-done.50
  273.7 12.4 %collective-permute-start.59 = (bf16[128,1024]{1,0:T(8,128)(2,1)S(1)}, bf16[128,1024]{1,0:T(8,128)(2,1)S(1)}, u32[]{:S(2)}, u32[]{:S(2)}) collective-permute-start(bf16[128,1024]{1,0:T(8,128)(2,1)S(1)} %copy-done.132), channel_id=1, source_target_pairs={{4,0},{5,1},{6,2},{7,3},{20,16},{21,17},{22,18},{23,19}} | collective-permute-start | bytes 786440 | tf_op jit(solution)/shard_map/ppermute | solution.py:54
  340.7 7.7 attend.7
  348.3 7.7 attend.6
  361.7 6.8 fusion.18
  368.5 6.8 fusion.23
  399.4 7.6 fusion.84
  455.3 10.1 %attend_back.4 = (bf16[2,200,512]{2,1,0:T(8,128)(2,1)S(1)}, bf16[2,200,512]{2,1,0:T(8,128)(2,1)S(1)}, bf16[2,200,512]{2,1,0:T(8,128)(2,1)S(1)}) custom-call(bf16[2,200,1536]{2,1,0:T(8,128)(2,1)S(1)} %bitcast.795, bf16[2,200,1536]{2,1,0:T(8,128)(2,1)S(1)} %bitcast.796, bf16[2,200,1536]{2,1,0:T(8,128)(2,1)S(1)} %bitcast.797, bf16[2,200,512]{2,1,0:T(8,128)(2,1)S(1)} %bitcast.804), custom_call_target="tpu_custom_call" | custom-call | flops 819200000 | bytes 2867200 | tf_op jit(solution)/shard_map/attend_back/pallas_call | solution.py:370
  465.5 10.3 %attend_back.5 = (bf16[2,200,512]{2,1,0:T(8,128)(2,1)S(1)}, bf16[2,200,512]{2,1,0:T(8,128)(2,1)S(1)}, bf16[2,200,512]{2,1,0:T(8,128)(2,1)S(1)}) custom-call(bf16[2,200,1536]{2,1,0:T(8,128)(2,1)S(1)} %bitcast.789, bf16[2,200,1536]{2,1,0:T(8,128)(2,1)S(1)} %bitcast.790, bf16[2,200,1536]{2,1,0:T(8,128)(2,1)S(1)} %bitcast.791, bf16[2,200,512]{2,1,0:T(8,128)(2,1)S(1)} %bitcast.802), custom_call_target="tpu_custom_call" | custom-call | flops 819200000 | bytes 2867200 | tf_op jit(solution)/shard_map/attend_back/pallas_call | solution.py:370
  567.4 8.5 collective-permute-start.131
  592.3 7.7 convolution_convert_fusion
  614.8 8.0 collective-permute-done.75
  649.8 10.1 %attend_back.6 = (bf16[2,200,512]{2,1,0:T(8,128)(2,1)S(1)}, bf16[2,200,512]{2,1,0:T(8,128)(2,1)S(1)}, bf16[2,200,512]{2,1,0:T(8,128)(2,1)S(1)}) custom-call(bf16[2,200,1536]{2,1,0:T(8,128)(2,1)S(1)} %bitcast.783, bf16[2,200,1536]{2,1,0:T(8,128)(2,1)S(1)} %bitcast.784, bf16[2,200,1536]{2,1,0:T(8,128)(2,1)S(1)} %bitcast.785, bf16[2,200,512]{2,1,0:T(8,128)(2,1)S(1)} %bitcast.805), custom_call_target="tpu_custom_call" | custom-call | flops 819200000 | bytes 2867200 | tf_op jit(solution)/shard_map/attend_back/pallas_call | solution.py:370
  660.0 10.5 %attend_back.7 = (bf16[2,200,512]{2,1,0:T(8,128)(2,1)S(1)}, bf16[2,200,512]{2,1,0:T(8,128)(2,1)S(1)}, bf16[2,200,512]{2,1,0:T(8,128)(2,1)S(1)}) custom-call(bf16[2,200,1536]{2,1,0:T(8,128)(2,1)S(1)} %bitcast.777, bf16[2,200,1536]{2,1,0:T(8,128)(2,1)S(1)} %bitcast.778, bf16[2,200,1536]{2,1,0:T(8,128)(2,1)S(1)} %bitcast.779, bf16[2,200,512]{2,1,0:T(8,128)(2,1)S(1)} %bitcast.803), custom_call_target="tpu_custom_call" | custom-call | flops 819200000 | bytes 2867200 | tf_op jit(solution)/shard_map/attend_back/pallas_call | solution.py:370
  699.5 7.8 collective-permute-done.81
  768.5 8.2 collective-permute-done.94
  779.7 10.4 %collective-permute-done.113 = bf16[64,2048]{1,0:T(8,128)(2,1)S(1)} collective-permute-done((bf16[64,2048]{1,0:T(8,128)(2,1)S(1)}, bf16[64,2048]{1,0:T(8,128)(2,1)S(1)}, u32[]{:S(2)}, u32[]{:S(2)}) %collective-permute-start.113) | collective-permute-done | bytes 262176 | tf_op jit(solution)/shard_map/ppermute | solution.py:54
  816.7 25.2 %collective-permute-done.137 = bf16[128,1024]{1,0:T(8,128)(2,1)S(1)} collective-permute-done((bf16[128,1024]{1,0:T(8,128)(2,1)S(1)}, bf16[128,1024]{1,0:T(8,128)(2,1)S(1)}, u32[]{:S(2)}, u32[]{:S(2)}) %collective-permute-start.137) | collective-permute-done | bytes 262176 | tf_op jit(solution)/shard_map/ppermute | solution.py:47
  863.7 6.5 copy.663
  891.5 17.4 %collective-permute-done.105 = bf16[4,64,2176]{2,1,0:T(8,128)(2,1)S(1)} collective-permute-done((bf16[4,64,2176]{2,1,0:T(8,128)(2,1)S(1)}, bf16[4,64,2176]{2,1,0:T(8,128)(2,1)S(1)}, u32[]{:S(2)}, u32[]{:S(2)}) %collective-permute-start.105) | collective-permute-done | bytes 1114144 | tf_op jit(solution)/shard_map/ppermute | solution.py:47
  925.7 7.0 collective-permute-start.111
  (1054 shorter events, 655.3 us)
Async XLA Ops:
  90.2 33.2 %collective-permute-start.29 = (bf16[4,64,2176]{2,1,0:T(8,128)(2,1)S(1)}, bf16[4,64,2176]{2,1,0:T(8,128)(2,1)S(1)}, u32[]{:S(2)}, u32[]{:S(2)}) collective-permute-start(bf16[4,64,2176]{2,1,0:T(8,128)(2,1)S(1)} %constant_dynamic-slice_fusion.5), channel_id=1, source_target_pairs={{0,1},{1,0},{2,3},{3,2},{4,5},{5,4},{6,7},{7,6},{8,9},{9,8},{10,11... | collective-permute-start | bytes 3342344 | tf_op jit(solution)/shard_map/ppermute | solution.py:47
  109.1 33.9 %collective-permute-start.31 = (bf16[4,64,2048]{2,1,0:T(8,128)(2,1)S(1)}, bf16[4,64,2048]{2,1,0:T(8,128)(2,1)S(1)}, u32[]{:S(2)}, u32[]{:S(2)}) collective-permute-start(bf16[4,64,2048]{2,1,0:T(8,128)(2,1)S(1)} %constant_dynamic-slice_fusion.4), channel_id=1, source_target_pairs={{0,1},{1,0},{2,3},{3,2},{4,5},{5,4},{6,7},{7,6},{8,9},{9,8},{10,11... | collective-permute-start | bytes 3145736 | tf_op jit(solution)/shard_map/ppermute | solution.py:47
  152.8 34.4 %collective-permute-start.43 = (bf16[1024,2176]{1,0:T(8,128)(2,1)S(1)}, bf16[1024,2176]{1,0:T(8,128)(2,1)S(1)}, u32[]{:S(2)}, u32[]{:S(2)}) collective-permute-start(bf16[1024,2176]{1,0:T(8,128)(2,1)S(1)} %bitcast.844), channel_id=1, source_target_pairs={{0,16},{16,0},{1,17},{17,1},{2,18},{18,2},{3,19},{19,3},{4,20},{20... | collective-permute-start | bytes 13369352 | tf_op jit(solution)/shard_map/ppermute | solution.py:42
  175.3 42.9 %collective-permute-start.44 = (bf16[64,2176]{1,0:T(8,128)(2,1)}, bf16[64,2176]{1,0:T(8,128)(2,1)}, u32[]{:S(2)}, u32[]{:S(2)}) collective-permute-start(bf16[64,2176]{1,0:T(8,128)(2,1)} %collective-permute-done.33), channel_id=1, source_target_pairs={{8,12},{9,13},{10,14},{11,15},{24,28},{25,29},{26,30},{27,31}} | collective-permute-start | bytes 835592 | tf_op jit(solution)/shard_map/ppermute | solution.py:54
  176.6 41.5 %collective-permute-start.45 = (bf16[64,2176]{1,0:T(8,128)(2,1)}, bf16[64,2176]{1,0:T(8,128)(2,1)}, u32[]{:S(2)}, u32[]{:S(2)}) collective-permute-start(bf16[64,2176]{1,0:T(8,128)(2,1)} %collective-permute-done.34), channel_id=1, source_target_pairs={{4,0},{5,1},{6,2},{7,3},{20,16},{21,17},{22,18},{23,19}} | collective-permute-start | bytes 835592 | tf_op jit(solution)/shard_map/ppermute | solution.py:54
  178.2 47.5 %collective-permute-start.46 = (bf16[4,128,1024]{2,1,0:T(8,128)(2,1)}, bf16[4,128,1024]{2,1,0:T(8,128)(2,1)}, u32[]{:S(2)}, u32[]{:S(2)}) collective-permute-start(bf16[4,128,1024]{2,1,0:T(8,128)(2,1)} %collective-permute-done.39), channel_id=1, source_target_pairs={{4,8},{5,9},{6,10},{7,11},{8,12},{9,13},{10,14},{11,15},{20,24},{2... | collective-permute-start | bytes 3145736 | tf_op jit(solution)/shard_map/ppermute | solution.py:54
  184.2 41.6 %collective-permute-start.47 = (bf16[4,128,1024]{2,1,0:T(8,128)(2,1)}, bf16[4,128,1024]{2,1,0:T(8,128)(2,1)}, u32[]{:S(2)}, u32[]{:S(2)}) collective-permute-start(bf16[4,128,1024]{2,1,0:T(8,128)(2,1)} %collective-permute-done.40), channel_id=1, source_target_pairs={{4,0},{5,1},{6,2},{7,3},{8,4},{9,5},{10,6},{11,7},{20,16},{21,17},... | collective-permute-start | bytes 3145736 | tf_op jit(solution)/shard_map/ppermute | solution.py:54
  187.2 40.6 %collective-permute-start.48 = (bf16[1024,2048]{1,0:T(8,128)(2,1)}, bf16[1024,2048]{1,0:T(8,128)(2,1)}, u32[]{:S(2)}, u32[]{:S(2)}) collective-permute-start(bf16[1024,2048]{1,0:T(8,128)(2,1)} %bitcast.59), channel_id=1, source_target_pairs={{0,16},{16,0},{1,17},{17,1},{2,18},{18,2},{3,19},{19,3},{4,20},{20... | collective-permute-start | bytes 12582920 | tf_op jit(solution)/shard_map/ppermute | solution.py:42
  225.2 60.8 %collective-permute-start.53 = (bf16[4,64,2048]{2,1,0:T(8,128)(2,1)}, bf16[4,64,2048]{2,1,0:T(8,128)(2,1)}, u32[]{:S(2)}, u32[]{:S(2)}) collective-permute-start(bf16[4,64,2048]{2,1,0:T(8,128)(2,1)} %constant_dynamic-slice_fusion.2), channel_id=1, source_target_pairs={{0,1},{1,0},{2,3},{3,2},{4,5},{5,4},{6,7},{7,6},{8,9},{9,8},{10,11... | collective-permute-start | bytes 3145736 | tf_op jit(solution)/shard_map/ppermute | solution.py:47
  225.7 60.4 %collective-permute-start.54 = (bf16[4,64,2048]{2,1,0:T(8,128)(2,1)}, bf16[4,64,2048]{2,1,0:T(8,128)(2,1)}, u32[]{:S(2)}, u32[]{:S(2)}) collective-permute-start(bf16[4,64,2048]{2,1,0:T(8,128)(2,1)} %constant_dynamic-slice_fusion.2), channel_id=1, source_target_pairs={{0,2},{1,3},{2,0},{3,1},{4,6},{5,7},{6,4},{7,5},{8,10},{9,11},{10,... | collective-permute-start | bytes 3145736 | tf_op jit(solution)/shard_map/ppermute | solution.py:47
  225.9 47.1 %collective-permute-start.50 = (bf16[4,64,2176]{2,1,0:T(8,128)(2,1)S(1)}, bf16[4,64,2176]{2,1,0:T(8,128)(2,1)}, u32[]{:S(2)}, u32[]{:S(2)}) collective-permute-start(bf16[4,64,2176]{2,1,0:T(8,128)(2,1)S(1)} %constant_dynamic-slice_fusion.3), channel_id=1, source_target_pairs={{0,2},{1,3},{2,0},{3,1},{4,6},{5,7},{6,4},{7,5},{8,10},{9,11},{10,... | collective-permute-start | bytes 3342344 | tf_op jit(solution)/shard_map/ppermute | solution.py:47
  227.8 45.8 %collective-permute-start.51 = (bf16[4,128,1024]{2,1,0:T(8,128)(2,1)}, bf16[4,128,1024]{2,1,0:T(8,128)(2,1)S(1)}, u32[]{:S(2)}, u32[]{:S(2)}) collective-permute-start(bf16[4,128,1024]{2,1,0:T(8,128)(2,1)} %collective-permute-done.46), channel_id=1, source_target_pairs={{8,12},{9,13},{10,14},{11,15},{24,28},{25,29},{26,30},{27,31}} | collective-permute-start | bytes 3145736 | tf_op jit(solution)/shard_map/ppermute | solution.py:54
  250.2 35.9 %collective-permute-start.52 = (bf16[4,128,1024]{2,1,0:T(8,128)(2,1)}, bf16[4,128,1024]{2,1,0:T(8,128)(2,1)S(1)}, u32[]{:S(2)}, u32[]{:S(2)}) collective-permute-start(bf16[4,128,1024]{2,1,0:T(8,128)(2,1)} %collective-permute-done.47), channel_id=1, source_target_pairs={{4,0},{5,1},{6,2},{7,3},{20,16},{21,17},{22,18},{23,19}} | collective-permute-start | bytes 3145736 | tf_op jit(solution)/shard_map/ppermute | solution.py:54
  273.0 43.2 %collective-permute-start.58 = (bf16[128,1024]{1,0:T(8,128)(2,1)S(1)}, bf16[128,1024]{1,0:T(8,128)(2,1)S(1)}, u32[]{:S(2)}, u32[]{:S(2)}) collective-permute-start(bf16[128,1024]{1,0:T(8,128)(2,1)S(1)} %copy-done.134), channel_id=1, source_target_pairs={{8,12},{9,13},{10,14},{11,15},{24,28},{25,29},{26,30},{27,31}} | collective-permute-start | bytes 786440 | tf_op jit(solution)/shard_map/ppermute | solution.py:54
  273.7 42.5 %collective-permute-start.59 = (bf16[128,1024]{1,0:T(8,128)(2,1)S(1)}, bf16[128,1024]{1,0:T(8,128)(2,1)S(1)}, u32[]{:S(2)}, u32[]{:S(2)}) collective-permute-start(bf16[128,1024]{1,0:T(8,128)(2,1)S(1)} %copy-done.132), channel_id=1, source_target_pairs={{4,0},{5,1},{6,2},{7,3},{20,16},{21,17},{22,18},{23,19}} | collective-permute-start | bytes 786440 | tf_op jit(solution)/shard_map/ppermute | solution.py:54
  317.4 57.9 %collective-permute-start.64 = (bf16[4,128,1024]{2,1,0:T(8,128)(2,1)}, bf16[4,128,1024]{2,1,0:T(8,128)(2,1)}, u32[]{:S(2)}, u32[]{:S(2)}) collective-permute-start(bf16[4,128,1024]{2,1,0:T(8,128)(2,1)} %constant_dynamic-slice_fusion), channel_id=1, source_target_pairs={{0,1},{1,0},{2,3},{3,2},{4,5},{5,4},{6,7},{7,6},{8,9},{9,8},{10,11... | collective-permute-start | bytes 3145736 | tf_op jit(solution)/shard_map/ppermute | solution.py:47
  318.9 56.4 %collective-permute-start.65 = (bf16[4,128,1024]{2,1,0:T(8,128)(2,1)}, bf16[4,128,1024]{2,1,0:T(8,128)(2,1)}, u32[]{:S(2)}, u32[]{:S(2)}) collective-permute-start(bf16[4,128,1024]{2,1,0:T(8,128)(2,1)} %constant_dynamic-slice_fusion), channel_id=1, source_target_pairs={{0,2},{1,3},{2,0},{3,1},{4,6},{5,7},{6,4},{7,5},{8,10},{9,11},{10,... | collective-permute-start | bytes 3145736 | tf_op jit(solution)/shard_map/ppermute | solution.py:47
  414.4 61.6 %collective-permute-start.70 = (bf16[2,128,1024]{2,1,0:T(8,128)(2,1)}, bf16[2,128,1024]{2,1,0:T(8,128)(2,1)}, u32[]{:S(2)}, u32[]{:S(2)}) collective-permute-start(bf16[2,128,1024]{2,1,0:T(8,128)(2,1)} %get-tuple-element.1303), channel_id=1, source_target_pairs={{0,1},{1,0},{2,3},{3,2},{4,5},{5,4},{6,7},{7,6},{8,9},{9,8},{10,11... | collective-permute-start | bytes 1572872 | tf_op jit(solution)/shard_map/ppermute | solution.py:47
  414.7 61.3 %collective-permute-start.71 = (bf16[2,128,1024]{2,1,0:T(8,128)(2,1)}, bf16[2,128,1024]{2,1,0:T(8,128)(2,1)}, u32[]{:S(2)}, u32[]{:S(2)}) collective-permute-start(bf16[2,128,1024]{2,1,0:T(8,128)(2,1)} %get-tuple-element.1302), channel_id=1, source_target_pairs={{0,2},{1,3},{2,0},{3,1},{4,6},{5,7},{6,4},{7,5},{8,10},{9,11},{10,... | collective-permute-start | bytes 1572872 | tf_op jit(solution)/shard_map/ppermute | solution.py:47
  511.1 75.1 %collective-permute-start.73 = (bf16[1024,2048]{1,0:T(8,128)(2,1)}, bf16[1024,2048]{1,0:T(8,128)(2,1)}, u32[]{:S(2)}, u32[]{:S(2)}) collective-permute-start(bf16[1024,2048]{1,0:T(8,128)(2,1)} %convolution_convert_fusion.1), channel_id=1, source_target_pairs={{0,16},{16,0},{1,17},{17,1},{2,18},{18,2},{3,19},{19,3},{4,20},{20... | collective-permute-start | bytes 12582920 | tf_op jit(solution)/shard_map/ppermute | solution.py:42
  541.6 63.7 %collective-permute-start.74 = (bf16[1024,2176]{0,1:T(8,128)(2,1)}, bf16[1024,2176]{0,1:T(8,128)(2,1)}, u32[]{:S(2)}, u32[]{:S(2)}) collective-permute-start(bf16[1024,2176]{0,1:T(8,128)(2,1)} %fusion.2), channel_id=1, source_target_pairs={{0,16},{16,0},{1,17},{17,1},{2,18},{18,2},{3,19},{19,3},{4,20},{20... | collective-permute-start | bytes 13369352 | tf_op jit(solution)/shard_map/ppermute | solution.py:42
  605.3 122.3 %collective-permute-start.83 = (bf16[1024,2048]{1,0:T(8,128)(2,1)}, bf16[1024,2048]{1,0:T(8,128)(2,1)}, u32[]{:S(2)}, u32[]{:S(2)}) collective-permute-start(bf16[1024,2048]{1,0:T(8,128)(2,1)} %convolution_convert_fusion), channel_id=1, source_target_pairs={{0,16},{16,0},{1,17},{17,1},{2,18},{18,2},{3,19},{19,3},{4,20},{20... | collective-permute-start | bytes 12582920 | tf_op jit(solution)/shard_map/ppermute | solution.py:42
  693.4 40.4 %collective-permute-start.84 = (bf16[4,64,2048]{2,1,0:T(8,128)(2,1)}, bf16[4,64,2048]{2,1,0:T(8,128)(2,1)}, u32[]{:S(2)}, u32[]{:S(2)}) collective-permute-start(bf16[4,64,2048]{2,1,0:T(8,128)(2,1)} %pad_maximum_fusion.10), channel_id=1, source_target_pairs={{0,1},{1,0},{2,3},{3,2},{4,5},{5,4},{6,7},{7,6},{8,9},{9,8},{10,11... | collective-permute-start | bytes 3145736 | tf_op jit(solution)/shard_map/ppermute | solution.py:47
  694.4 39.4 %collective-permute-start.85 = (bf16[4,64,2048]{2,1,0:T(8,128)(2,1)}, bf16[4,64,2048]{2,1,0:T(8,128)(2,1)}, u32[]{:S(2)}, u32[]{:S(2)}) collective-permute-start(bf16[4,64,2048]{2,1,0:T(8,128)(2,1)} %pad_maximum_fusion.11), channel_id=1, source_target_pairs={{0,2},{1,3},{2,0},{3,1},{4,6},{5,7},{6,4},{7,5},{8,10},{9,11},{10,... | collective-permute-start | bytes 3145736 | tf_op jit(solution)/shard_map/ppermute | solution.py:47
  707.3 56.5 %collective-permute-start.93 = (bf16[4,64,2176]{2,1,0:T(8,128)(2,1)}, bf16[4,64,2176]{2,1,0:T(8,128)(2,1)}, u32[]{:S(2)}, u32[]{:S(2)}) collective-permute-start(bf16[4,64,2176]{2,1,0:T(8,128)(2,1)} %pad_maximum_fusion.8), channel_id=1, source_target_pairs={{0,1},{1,0},{2,3},{3,2},{4,5},{5,4},{6,7},{7,6},{8,9},{9,8},{10,11... | collective-permute-start | bytes 3342344 | tf_op jit(solution)/shard_map/ppermute | solution.py:47
  755.6 102.3 %collective-permute-start.86 = (bf16[1024,2176]{0,1:T(8,128)(2,1)S(1)}, bf16[1024,2176]{0,1:T(8,128)(2,1)S(1)}, u32[]{:S(2)}, u32[]{:S(2)}) collective-permute-start(bf16[1024,2176]{0,1:T(8,128)(2,1)S(1)} %bitcast.859), channel_id=1, source_target_pairs={{0,16},{16,0},{1,17},{17,1},{2,18},{18,2},{3,19},{19,3},{4,20},{20... | collective-permute-start | bytes 13369352 | tf_op jit(solution)/shard_map/ppermute | solution.py:42
  755.6 49.2 %collective-permute-start.133 = (bf16[4,128,1024]{2,1,0:T(8,128)(2,1)S(1)}, bf16[4,128,1024]{2,1,0:T(8,128)(2,1)S(1)}, u32[]{:S(2)}, u32[]{:S(2)}) collective-permute-start(bf16[4,128,1024]{2,1,0:T(8,128)(2,1)S(1)} %get-tuple-element.1281), channel_id=1, source_target_pairs={{0,4},{1,5},{2,6},{3,7},{4,8},{5,9},{6,10},{7,11},{8,12},{9,13},{1... | collective-permute-start | bytes 3145736 | tf_op jit(solution)/shard_map/ppermute | solution.py:54
  761.6 44.0 %collective-permute-start.134 = (bf16[4,128,1024]{2,1,0:T(8,128)(2,1)S(1)}, bf16[4,128,1024]{2,1,0:T(8,128)(2,1)S(1)}, u32[]{:S(2)}, u32[]{:S(2)}) collective-permute-start(bf16[4,128,1024]{2,1,0:T(8,128)(2,1)S(1)} %get-tuple-element.1280), channel_id=1, source_target_pairs={{4,0},{5,1},{6,2},{7,3},{8,4},{9,5},{10,6},{11,7},{12,8},{13,9},{1... | collective-permute-start | bytes 3145736 | tf_op jit(solution)/shard_map/ppermute | solution.py:54
  811.4 37.1 %collective-permute-start.117 = (bf16[4,64,2048]{2,1,0:T(8,128)(2,1)S(1)}, bf16[4,64,2048]{2,1,0:T(8,128)(2,1)S(1)}, u32[]{:S(2)}, u32[]{:S(2)}) collective-permute-start(bf16[4,64,2048]{2,1,0:T(8,128)(2,1)S(1)} %pad_maximum_fusion.13), channel_id=1, source_target_pairs={{0,1},{1,0},{2,3},{3,2},{4,5},{5,4},{6,7},{7,6},{8,9},{9,8},{10,11... | collective-permute-start | bytes 3145736 | tf_op jit(solution)/shard_map/ppermute | solution.py:47
  812.5 36.1 %collective-permute-start.118 = (bf16[4,64,2048]{2,1,0:T(8,128)(2,1)S(1)}, bf16[4,64,2048]{2,1,0:T(8,128)(2,1)S(1)}, u32[]{:S(2)}, u32[]{:S(2)}) collective-permute-start(bf16[4,64,2048]{2,1,0:T(8,128)(2,1)S(1)} %pad_maximum_fusion.14), channel_id=1, source_target_pairs={{0,2},{1,3},{2,0},{3,1},{4,6},{5,7},{6,4},{7,5},{8,10},{9,11},{10,... | collective-permute-start | bytes 3145736 | tf_op jit(solution)/shard_map/ppermute | solution.py:47
  874.8 37.5 %collective-permute-start.139 = (f32[128,1024]{1,0:T(8,128)S(1)}, f32[128,1024]{1,0:T(8,128)S(1)}, u32[]{:S(2)}, u32[]{:S(2)}) collective-permute-start(f32[128,1024]{1,0:T(8,128)S(1)} %get-tuple-element.1386), channel_id=1, source_target_pairs={{0,16},{16,0},{1,17},{17,1},{2,18},{18,2},{3,19},{19,3},{4,20},{20... | collective-permute-start | bytes 1572872 | tf_op jit(solution)/shard_map/ppermute | solution.py:42
  944.1 33.6 %collective-permute-start.123 = (f32[64,2176]{1,0:T(8,128)}, f32[64,2176]{1,0:T(8,128)}, u32[]{:S(2)}, u32[]{:S(2)}) collective-permute-start(f32[64,2176]{1,0:T(8,128)} %get-tuple-element.1383), channel_id=1, source_target_pairs={{0,16},{16,0},{1,17},{17,1},{2,18},{18,2},{3,19},{19,3},{4,20},{20... | collective-permute-start | bytes 1671176 | tf_op jit(solution)/shard_map/ppermute | solution.py:42
  (292 other events, 3778.9 us)

commit v3 on v0

v3 whole, which is shorter than its diff:
```python
import functools
import jax
import jax.numpy as jnp
from jax import lax
from jax.experimental import pallas as pl
from jax.experimental.pallas import tpu as pltpu
from jax.sharding import Mesh
from jax.sharding import PartitionSpec as P

HEAD = 64
SEQ = 50
STEP = 10
SIDE = 4
LEVELS = 4
GROUP = 200
SLABS = 16
TILE = 512
STEPS = 4
VMEM_MB = 48
SECTION = "section"
DP = ("z", "y", "x")
X, Y, Z = DP[2], DP[1], DP[0]
GATHERS = ((10, 0, 1), (20,), (30,), (11,), (21,), (31,))
SCATTERS = ((31,), (21,), (11,), (30,), (20,), (10,))
LATE_GATHERS = ()
LATE_SCATTERS = ()
ORDER = (
    101, 102, 104, 105, 100, 101, 103, 100, 102, 101, 100, 101, 103, 100, 100, 10,
    20, 102, 103, 102, 104, 103, 101, 30, 104, 102, 40, 104, 103, 105, 11, 21,
    105, 105, 104, 31, 331, 105, 621, 631, 200, 641, 200, 651, 311, 202, 620, 200,
    202, 321, 320, 201, 200, 204, 202, 630, 204, 640, 201, 202, 204, 330, 203, 650,
    201, 204, 203, 310, 205, 203, 201, 205, 41, 203, 402, 205, 403, 500, 205,
)

norm_epsilon = 1e-06
clip_norm = 1.0
beta_one = 0.9
beta_two = 0.95
rate_matrix = 0.05
rate_vector = 1.0
decay_matrix = 0.1
epsilon = 1e-08
low_type = jnp.bfloat16
wide = jnp.float32


def swap_cores(x):
    return lax.ppermute(x, SECTION, [(0, 1), (1, 0)])


def flip(x, axis):
    return lax.ppermute(x, axis, [(0, 1), (1, 0)])


class Line:
    def __init__(self):
        self.token = jnp.zeros((), wide)

    def sync(self, *values):
        fenced = lax.optimization_barrier((self.token, *values))
        self.token = fenced[0]
        return fenced[1:]


class Layer:
    def __init__(self):
        self.weights = {}
        self.chip_grads = {}
        self.grads = {}


def swap_halves(here, there, first):
    got = swap_cores(there)
    return jnp.where(first, here, got), jnp.where(first, got, here)


def place_blocks(blocks, me, axis):
    shape = list(blocks[0].shape)
    shape.insert(axis, SIDE)
    full = jnp.zeros(shape, blocks[0].dtype)
    for relative, block in enumerate(blocks):
        start = [0] * len(shape)
        start[axis] = jnp.bitwise_xor(me, relative)
        full = lax.dynamic_update_slice(full, jnp.expand_dims(block, axis), start)
    return full


def add_low(left, right):
    return (left.astype(wide) + right.astype(wide)).astype(low_type)


def pick(array, index, axis):
    last = array.shape[axis] - 1
    return lax.dynamic_index_in_dim(array, jnp.clip(index, 0, last), axis, keepdims=False)


def gather_flow(line, parts, me, keys, layers):
    half = LEVELS // 2
    counts = [part.shape[0] for part in parts]
    extras = {}
    while keys[-1] < 10:
        extras[keys[-1]] = (sum(counts[: len(keys) - 1]), counts[len(keys) - 1])
        keys = keys[:-1]
    counts = counts[: len(keys) - 1] + [sum(counts[len(keys) - 1 :])]
    (part,) = line.sync(jnp.concatenate(parts, axis=0))
    column = lax.all_gather(part, Z, axis=0, tiled=False)
    yield
    (column,) = line.sync(column)
    across = flip(column, X)
    along = flip(column, Y)
    yield
    across, along, column = line.sync(across, along, column)
    corner_low, corner_high = line.sync(along[:half], across[half:])
    corner_low = flip(corner_low, X)
    corner_high = flip(corner_high, Y)
    fulls = []
    start = 0
    for count in counts:
        stop = start + count
        fulls.append(
            place_blocks([piece[:, start:stop] for piece in (column, across, along)], me, 1)
        )
        start = stop
    fulls = line.sync(*fulls)
    yield
    corner_low, corner_high, *fulls = line.sync(corner_low, corner_high, *fulls)
    corner = jnp.bitwise_xor(me, 3)
    start = 0
    for key, count, full in zip(keys, counts, fulls):
        stop = start + count
        full = lax.dynamic_update_slice(full, corner_low[:, None, start:stop], (0, corner, 0, 0))
        full = lax.dynamic_update_slice(
            full, corner_high[:, None, start:stop], (half, corner, 0, 0)
        )
        start = stop
        (own,) = line.sync(full.reshape(LEVELS * SIDE, count, -1))
        for name, (row, size) in extras.items():
            layers[name].spread = own[:, row : row + size]
        other = swap_cores(own)
        yield
        layers[key % 10].weights[key // 10] = line.sync(own, other)
    yield


def gather_flow_late(line, parts, me, keys, layers):
    (part,) = line.sync(*parts)
    half = part.shape[0] // 2
    across = flip(part, X)
    along = flip(part, Y)
    yield
    across, along = line.sync(across, along)
    corner_low, corner_high = line.sync(along[:half], across[half:])
    corner_low = flip(corner_low, X)
    corner_high = flip(corner_high, Y)
    yield
    corner_low, corner_high = line.sync(corner_low, corner_high)
    block = place_blocks([part, across, along, jnp.concatenate([corner_low, corner_high])], me, 0)
    (block,) = line.sync(block)
    full = lax.all_gather(block, Z, axis=0, tiled=False)
    yield
    (own,) = line.sync(full.reshape(LEVELS * SIDE, *part.shape))
    other = swap_cores(own)
    yield
    layers[keys[0] % 10].weights[keys[0] // 10] = line.sync(own, other)
    yield


def scatter_flow(line, me, keys, layers):
    half = LEVELS // 2
    chips = [layers[key % 10].chip_grads[key // 10] for key in keys]
    chips = [chip.reshape(LEVELS, SIDE, *chip.shape[1:]) for chip in chips]
    counts = [chip.shape[2] for chip in chips]

    def toward(relative):
        to = jnp.bitwise_xor(me, relative)
        return jnp.concatenate([pick(chip, to, 1) for chip in chips], axis=1)

    chips = line.sync(*chips)
    corner = toward(3)
    from_across, from_along = line.sync(corner[:half], corner[half:])
    from_across = flip(from_across, X)
    from_along = flip(from_along, Y)
    yield
    from_across, from_along, *chips = line.sync(from_across, from_along, *chips)
    along, across = toward(2), toward(1)
    along = jnp.concatenate([add_low(along[:half], from_across), along[half:]])
    across = jnp.concatenate([across[:half], add_low(across[half:], from_along)])
    across, along = line.sync(across, along)
    got_across = flip(across, X)
    got_along = flip(along, Y)
    own = toward(0)
    yield
    got_across, got_along, own = line.sync(got_across, got_along, own)
    column = own.astype(wide) + got_across.astype(wide) + got_along.astype(wide)
    (column,) = line.sync(column.astype(low_type))
    total = lax.psum_scatter(column, Z, scatter_dimension=0, tiled=False)
    yield
    (total,) = line.sync(total)
    total = total.astype(wide)
    start = 0
    for key, count in zip(keys, counts):
        layers[key % 10].grads[key // 10] = total[start : start + count]
        start += count
    yield


def scatter_flow_late(line, me, keys, layers):
    chip = layers[keys[0] % 10].chip_grads[keys[0] // 10]
    (chip,) = line.sync(chip.reshape(LEVELS, SIDE, *chip.shape[1:]))
    half = chip.shape[2] // 2
    block = lax.psum_scatter(chip, Z, scatter_dimension=0, tiled=False)
    yield
    (block,) = line.sync(block)

    def toward(relative):
        return pick(block, jnp.bitwise_xor(me, relative), 0)

    corner = toward(3)
    from_across, from_along = line.sync(corner[:half], corner[half:])
    from_across = flip(from_across, X)
    from_along = flip(from_along, Y)
    yield
    from_across, from_along = line.sync(from_across, from_along)
    along, across = toward(2), toward(1)
    along = jnp.concatenate([add_low(along[:half], from_across), along[half:]])
    across = jnp.concatenate([across[:half], add_low(across[half:], from_along)])
    across, along = line.sync(across, along)
    got_across = flip(across, X)
    got_along = flip(along, Y)
    yield
    got_across, got_along = line.sync(got_across, got_along)
    total = toward(0).astype(wide) + got_across.astype(wide) + got_along.astype(wide)
    layers[keys[0] % 10].grads[keys[0] // 10] = line.sync(total)[0]
    yield


def total_of(line, value):
    (value,) = line.sync(value + swap_cores(value))
    value = value + flip(value, X)
    value = value + flip(value, Y)
    for bit in (1, 2):
        pairs = [(i, i ^ bit) for i in range(LEVELS)]
        value = value + lax.ppermute(value, Z, pairs)
    return value


def normalize(inputs):
    centered = inputs - jnp.mean(inputs, axis=-1, keepdims=True)
    inverse = lax.rsqrt(jnp.mean(centered * centered, axis=-1, keepdims=True) + norm_epsilon)
    return (centered * inverse, inverse)


def normalize_back(upstream, scaled, inverse):
    return inverse * (
        upstream
        - jnp.mean(upstream, axis=-1, keepdims=True)
        - scaled * jnp.mean(upstream * scaled, axis=-1, keepdims=True)
    )


def dot_nt(left, right):
    return lax.dot_general(left, right, (((1,), (1,)), ((), ())), preferred_element_type=wide)


def dot_nn(left, right):
    return lax.dot_general(left, right, (((1,), (0,)), ((), ())), preferred_element_type=wide)


def dot_tn(left, right):
    return lax.dot_general(left, right, (((0,), (0,)), ((), ())), preferred_element_type=wide)


def same_image(rows):
    image_row = lax.broadcasted_iota(jnp.int32, (rows, rows), 0) // SEQ
    image_col = lax.broadcasted_iota(jnp.int32, (rows, rows), 1) // SEQ
    return image_row == image_col


def attend_kernel(q_ref, k_ref, v_ref, o_ref):
    rows, columns = q_ref.shape[1:]
    mask = same_image(rows)
    lane = lax.broadcasted_iota(jnp.int32, (rows, 2 * HEAD), 1)
    for start in range(0, columns, 2 * HEAD):
        place = pl.ds(start, 2 * HEAD)
        queries, keys, values = q_ref[0, :, place], k_ref[0, :, place], v_ref[0, :, place]
        queries = queries * jnp.asarray(HEAD ** (-0.5), low_type)
        mixed = []
        for head in range(2):
            inside = (lane >= head * HEAD) & (lane < (head + 1) * HEAD)
            own = jnp.where(inside, queries, jnp.zeros_like(queries))
            scores = jnp.where(mask, dot_nt(own, keys), -jnp.inf)
            raised = jnp.exp(scores - jnp.max(scores, axis=1, keepdims=True))
            weights = raised * (1.0 / jnp.sum(raised, axis=1, keepdims=True))
            mixed.append(dot_nn(weights.astype(low_type), values))
        o_ref[0, :, place] = jnp.where(lane < HEAD, mixed[0], mixed[1]).astype(low_type)


def third_at(third, rows, columns):
    return pl.BlockSpec((1, rows, columns), lambda i: (i, 0, third))


def attend(packed):
    sides, rows, columns = packed.shape
    groups, width = sides * rows // GROUP, columns // 3
    packed = packed.reshape(groups, GROUP, columns)
    mixed = pl.pallas_call(
        attend_kernel,
        grid=(groups,),
        in_specs=[third_at(third, GROUP, width) for third in range(3)],
        out_specs=third_at(0, GROUP, width),
        out_shape=jax.ShapeDtypeStruct((groups, GROUP, width), low_type),
        cost_estimate=cost(8 * sides * rows * GROUP * width, 8 * sides * rows * width),
        compiler_params=limits(),
        name="attend",
    )(packed, packed, packed)
    return mixed.reshape(sides, rows, width)


def attend_back_kernel(q_ref, k_ref, v_ref, g_ref, b_ref, d_ref):
    rows, columns = q_ref.shape[1:]
    mask = same_image(rows)
    lane = lax.broadcasted_iota(jnp.int32, (rows, 2 * HEAD), 1)
    scaling = HEAD ** (-0.5)
    lower = lane < HEAD
    d_ref[0, :, pl.ds(3 * columns, columns)] = b_ref[0]
    for start in range(0, columns, 2 * HEAD):
        place = pl.ds(start, 2 * HEAD)
        queries, keys, values = q_ref[0, :, place], k_ref[0, :, place], v_ref[0, :, place]
        upstream = g_ref[0, :, place]
        queries = queries * jnp.asarray(scaling, low_type)
        to_queries, to_keys, to_values = [], [], []
        for head in range(2):
            inside = (lane >= head * HEAD) & (lane < (head + 1) * HEAD)
            zero = jnp.zeros_like(queries)
            own_queries = jnp.where(inside, queries, zero)
            own_upstream = jnp.where(inside, upstream, zero)
            scores = jnp.where(mask, dot_nt(keys, own_queries), -jnp.inf)
            raised = jnp.exp(scores - jnp.max(scores, axis=0, keepdims=True))
            weights = raised * (1.0 / jnp.sum(raised, axis=0, keepdims=True))
            to_values.append(dot_nn(weights.astype(low_type), upstream))
            slope = dot_nt(values, own_upstream)
            inner = jnp.sum(weights * slope, axis=0, keepdims=True)
            change = (weights * (slope - inner)).astype(low_type)
            to_keys.append(dot_nn(change, queries))
            to_queries.append(dot_tn(keys, change))
        turned = jnp.concatenate([to_queries[0][:HEAD], to_queries[1][HEAD:]], axis=0)
        d_ref[0, :, place] = (turned.T * scaling).astype(low_type)
        keys_place = pl.ds(columns + start, 2 * HEAD)
        d_ref[0, :, keys_place] = jnp.where(lower, to_keys[0], to_keys[1]).astype(low_type)
        values_place = pl.ds(2 * columns + start, 2 * HEAD)
        d_ref[0, :, values_place] = jnp.where(lower, to_values[0], to_values[1]).astype(low_type)


def attend_back(packed, upstream, branch):
    sides, rows, columns = packed.shape
    groups, width = sides * rows // GROUP, columns // 3
    packed = packed.reshape(groups, GROUP, columns)
    upstream = upstream.reshape(groups, GROUP, width)
    branch = branch.reshape(groups, GROUP, width)
    total = columns + width
    slopes = pl.pallas_call(
        attend_back_kernel,
        grid=(groups,),
        in_specs=[third_at(third, GROUP, width) for third in (0, 1, 2, 0, 0)],
        out_specs=pl.BlockSpec((1, GROUP, total), lambda i: (i, 0, 0)),
        out_shape=jax.ShapeDtypeStruct((groups, GROUP, total), low_type),
        cost_estimate=cost(20 * sides * rows * GROUP * width, 14 * sides * rows * width),
        compiler_params=limits(),
        name="attend_back",
    )(packed, packed, packed, upstream, branch)
    return slopes.reshape(sides, rows, total)


def limits():
    return pltpu.CompilerParams(vmem_limit_bytes=VMEM_MB * 1024 * 1024)


def cost(flops, moved, special=0):
    return pl.CostEstimate(flops=flops, bytes_accessed=moved, transcendentals=special)


def early(count):
    return lambda i: jnp.minimum(i, count - 1)


def late(count):
    return lambda i: jnp.maximum(i - count, 0)


def tile_spec(width, first, turn):
    per = width // TILE

    def at(i):
        tile = first + turn(i)
        return (0, tile // per, tile % per)

    return pl.BlockSpec((SLABS, width // SLABS, TILE), at)


def side_spec(count, *shape):
    return pl.BlockSpec((1, *shape), lambda i: (i // count, 0, i % count))


def flat(ref):
    return ref[...].reshape(ref.shape[0] * ref.shape[1], ref.shape[2])


def project_kernel(smooth, count, x_ref, here_ref, there_ref, b_ref, *outs):
    def work(w_ref):
        total = dot_nn(x_ref[...], flat(w_ref)) + b_ref[0]
        if smooth:
            cdf = 0.5 * (1.0 + lax.erf(total * 0.7071067811865476))
            density = jnp.exp(-0.5 * total * total) * 0.3989422804014327
            outs[0][0] = (total * cdf).astype(low_type)
            outs[1][0] = (cdf + total * density).astype(low_type)
        else:
            outs[0][0] = total.astype(outs[0].dtype)

    i = pl.program_id(0)
    pl.when(i < count)(lambda: work(here_ref))
    pl.when(i >= count)(lambda: work(there_ref))


def project(x, weights, first, count, bias, kind, smooth=False):
    rows, depth = x.shape
    number = 2 if smooth else 1
    return pl.pallas_call(
        functools.partial(project_kernel, smooth, count),
        grid=(2 * count,),
        in_specs=[
            pl.BlockSpec((rows, depth), lambda i: (0, 0)),
            tile_spec(depth, first, early(count)),
            tile_spec(depth, first, late(count)),
            side_spec(count, 1, TILE),
        ],
        out_specs=[side_spec(count, rows, TILE)] * number,
        out_shape=[jax.ShapeDtypeStruct((2, rows, count * TILE), kind)] * number,
        cost_estimate=cost(4 * rows * depth * count * TILE, 4 * depth * count * TILE),
        compiler_params=limits(),
        name="project",
    )(x, *weights, bias)


def output_kernel(active_ref, w_here, w_there, middle_ref, b_ref, o_ref):
    total = dot_nn(active_ref[0], flat(w_here)) + dot_nn(active_ref[1], flat(w_there))
    o_ref[...] = (total + middle_ref[...] + b_ref[...]).astype(low_type)


def output_rows(active, weights, middle, bias):
    _, rows, depth = active.shape
    width = middle.shape[1]
    tile = width // STEPS
    weight = pl.BlockSpec((SLABS, depth // SLABS, tile), lambda i: (0, 0, i))
    part = pl.BlockSpec((rows, tile), lambda i: (0, i))
    return pl.pallas_call(
        output_kernel,
        grid=(STEPS,),
        in_specs=[
            pl.BlockSpec(active.shape, lambda i: (0, 0, 0)),
            weight,
            weight,
            part,
            pl.BlockSpec((1, tile), lambda i: (0, i)),
        ],
        out_specs=part,
        out_shape=jax.ShapeDtypeStruct((rows, width), low_type),
        cost_estimate=cost(4 * rows * depth * width, 4 * depth * width),
        compiler_params=limits(),
        name="output",
    )(active, *weights, middle, bias)


def active_grad_kernel(count, up_ref, w_here, w_there, slope_ref, o_ref, sum_ref):
    def work(w_ref):
        low = (dot_nt(up_ref[...], flat(w_ref)) * slope_ref[0].astype(wide)).astype(low_type)
        o_ref[0] = low
        sum_ref[0] = jnp.sum(low.astype(wide), axis=0, keepdims=True)

    i = pl.program_id(0)
    pl.when(i < count)(lambda: work(w_here))
    pl.when(i >= count)(lambda: work(w_there))


def active_grad(upstream, weights, slope):
    rows, width = upstream.shape
    depth = slope.shape[2]
    count = depth // TILE
    slabs = SLABS // count

    def weight(turn):
        return pl.BlockSpec((slabs, depth // SLABS, width), lambda i: (turn(i), 0, 0))

    return pl.pallas_call(
        functools.partial(active_grad_kernel, count),
        grid=(2 * count,),
        in_specs=[
            pl.BlockSpec((rows, width), lambda i: (0, 0)),
            weight(early(count)),
            weight(late(count)),
            side_spec(count, rows, TILE),
        ],
        out_specs=[side_spec(count, rows, TILE), side_spec(count, 1, TILE)],
        out_shape=[
            jax.ShapeDtypeStruct((2, rows, depth), low_type),
            jax.ShapeDtypeStruct((2, 1, depth), wide),
        ],
        cost_estimate=cost(4 * rows * depth * width, 6 * depth * width),
        compiler_params=limits(),
        name="active",
    )(upstream, *weights, slope)


def back_tile(left, packed, depth):
    slabs, _, width = packed.shape
    rows = width // SLABS
    total = None
    for block in range(2):
        count = min(depth - block * width, width)
        part = packed[:, pl.ds(block * rows, rows), pl.ds(0, count)].reshape(slabs * rows, count)
        term = dot_nt(left[:, pl.ds(block * width, count)], part)
        total = term if total is None else total + term
    return total


def middle_grad_kernel(place, *refs):
    left, w_here, w_there, middle, gain, up, proj_here, proj_there = refs[:8]
    o_middle, o_branch, o_mixed, sums, acc = refs[8:]
    i = pl.program_id(0)
    tile = acc.shape[1] // STEPS
    columns = pl.ds(pl.multiple_of(i * tile, tile), tile)
    depth = left.shape[2]
    acc[:, columns] = back_tile(left.at[0], w_here, depth) + back_tile(left.at[1], w_there, depth)

    @pl.when(i == STEPS - 1)
    def _():
        first = place[0] == 0
        grad = acc[...]
        scaled, inverse = normalize(middle[...])
        sums[0:1] = jnp.sum(grad * scaled, axis=0, keepdims=True)
        sums[1:2] = jnp.sum(grad, axis=0, keepdims=True)
        total = up[...].astype(wide) + normalize_back(grad * gain[...], scaled, inverse)
        o_middle[...] = total
        branch = total.astype(low_type)
        sums[2:3] = jnp.sum(branch.astype(wide), axis=0, keepdims=True)
        width = branch.shape[1] // 2
        near = jnp.where(first, branch[:, :width], branch[:, width:])
        far = jnp.where(first, branch[:, width:], branch[:, :width])
        o_branch[0] = near
        o_branch[1] = far
        mixed = dot_nt(near, flat(proj_here)) + dot_nt(far, flat(proj_there))
        mixed = mixed.astype(low_type)
        o_mixed[0] = jnp.where(first, mixed[:, :width], mixed[:, width:])
        o_mixed[1] = jnp.where(first, mixed[:, width:], mixed[:, :width])


def few_slabs(width):
    return pl.BlockSpec((SLABS // STEPS, 2 * width // SLABS, width), lambda i: (i, 0, 0))


def middle_grad(place, left, weights, middle, gain, upstream, firsts):
    rows, width = middle.shape
    depth = left.shape[2]
    whole = pl.BlockSpec((rows, width), lambda i: (0, 0))
    pair = pl.BlockSpec((2, rows, width // 2), lambda i: (0, 0, 0))
    halves = jax.ShapeDtypeStruct((2, rows, width // 2), low_type)
    return pl.pallas_call(
        middle_grad_kernel,
        grid=(STEPS,),
        in_specs=[
            pl.BlockSpec(memory_space=pltpu.SMEM),
            pl.BlockSpec(left.shape, lambda i: (0, 0, 0)),
            few_slabs(width),
            few_slabs(width),
            whole,
            pl.BlockSpec((1, width), lambda i: (0, 0)),
            whole,
            tile_spec(width, 3, lambda i: 0),
            tile_spec(width, 3, lambda i: 0),
        ],
        out_specs=[whole, pair, pair, pl.BlockSpec((8, width), lambda i: (0, 0))],
        out_shape=[
            jax.ShapeDtypeStruct((rows, width), wide),
            halves,
            halves,
            jax.ShapeDtypeStruct((8, width), wide),
        ],
        scratch_shapes=[pltpu.VMEM((rows, width), wide)],
        cost_estimate=cost(4 * rows * width * (depth + width // 2), 4 * depth * width),
        compiler_params=limits(),
        name="middle",
    )(place, left, *weights, middle, gain, upstream, *firsts)


def entry_grad_kernel(depth, left, w_here, w_there, inputs, gain, middle, *rest):
    o_ref, sums, side_sums, acc = rest
    i = pl.program_id(0)
    tile = acc.shape[1] // STEPS
    columns = pl.ds(pl.multiple_of(i * tile, tile), tile)
    acc[:, columns] = back_tile(left.at[0], w_here, depth) + back_tile(left.at[1], w_there, depth)

    @pl.when(i == STEPS - 1)
    def _():
        for side in range(2):
            side_sums[side] = jnp.sum(left[side, :, :depth].astype(wide), axis=0, keepdims=True)
        grad = acc[...]
        scaled, inverse = normalize(inputs[...].astype(wide))
        sums[0:1] = jnp.sum(grad * scaled, axis=0, keepdims=True)
        sums[1:2] = jnp.sum(grad, axis=0, keepdims=True)
        total = middle[...] + normalize_back(grad * gain[...], scaled, inverse)
        o_ref[...] = total.astype(low_type)


def entry_grad(left, depth, weights, inputs, gain, middle):
    rows, width = inputs.shape
    whole = pl.BlockSpec((rows, width), lambda i: (0, 0))
    return pl.pallas_call(
        functools.partial(entry_grad_kernel, depth),
        grid=(STEPS,),
        in_specs=[
            pl.BlockSpec(left.shape, lambda i: (0, 0, 0)),
            few_slabs(width),
            few_slabs(width),
            whole,
            pl.BlockSpec((1, width), lambda i: (0, 0)),
            whole,
        ],
        out_specs=[
            whole,
            pl.BlockSpec((8, width), lambda i: (0, 0)),
            pl.BlockSpec((2, 1, depth), lambda i: (0, 0, 0)),
        ],
        out_shape=[
            jax.ShapeDtypeStruct((rows, width), low_type),
            jax.ShapeDtypeStruct((8, width), wide),
            jax.ShapeDtypeStruct((2, 1, depth), wide),
        ],
        scratch_shapes=[pltpu.VMEM((rows, width), wide)],
        cost_estimate=cost(4 * rows * width * depth, 4 * depth * width),
        compiler_params=limits(),
        name="entry",
    )(left, *weights, inputs, gain, middle)


def grad_kernel(pairs, count, extra, *refs):
    out_ref = refs[-1]
    slabs, deep = out_ref.shape[:2]

    def matrix(number):
        ref = refs[number]
        return ref.at[0] if len(ref.shape) == 3 else ref

    for left, right, start, size, row, rows, column in pairs:
        place = pl.ds(start, size)
        total = dot_tn(matrix(left)[...], matrix(right)[:, place])
        total = total + dot_tn(matrix(count + left)[...], matrix(count + right)[:, place])
        total = total.reshape(slabs, rows, size).astype(low_type)
        out_ref[:, pl.ds(row, rows), pl.ds(column, size)] = total
    if extra:
        out_ref[:, pl.ds(deep - SLABS, SLABS)] = refs[2 * count][...]


def weight_grad(own, other, moving, pairs, extra=None):
    rows, depth = own[0][0].shape[-2:]
    width = 1024
    block = depth // STEPS
    slabs = SLABS // STEPS
    deep = sum(p[3] * p[5] for p in pairs) // width
    operands = [array for array, _ in (*own, *other)]

    def spec(index, array, which):
        by = int(index < moving)
        size = block if by else array.shape[-1]
        if array.ndim == 3:
            return pl.BlockSpec((1, rows, size), lambda i: (which, 0, i * by))
        return pl.BlockSpec((rows, size), lambda i: (0, i * by))

    specs = [spec(i, *pair) for pairs_of in (own, other) for i, pair in enumerate(pairs_of)]
    if extra is not None:
        deep += extra.shape[1]
        operands.append(extra)
        specs.append(pl.BlockSpec((slabs, *extra.shape[1:]), lambda i: (i, 0, 0)))
    return pl.pallas_call(
        functools.partial(grad_kernel, pairs, len(own), extra is not None),
        grid=(STEPS,),
        in_specs=specs,
        out_specs=pl.BlockSpec((slabs, deep, width), lambda i: (i, 0, 0)),
        out_shape=jax.ShapeDtypeStruct((SLABS, deep, width), low_type),
        cost_estimate=cost(4 * rows * SLABS * deep * width, 4 * SLABS * deep * width),
        compiler_params=limits(),
        name="grad",
    )(*operands)


def adam_update(weight, grad, first, second, factor, rate, decay):
    clipped = grad * factor
    momentum = beta_one * first + (1.0 - beta_one) * clipped
    variance = beta_two * second + (1.0 - beta_two) * clipped * clipped
    corrected_m = momentum / (1.0 - beta_one**STEP)
    corrected_v = variance / (1.0 - beta_two**STEP)
    updated = weight - rate * (corrected_m / (jnp.sqrt(corrected_v) + epsilon) + decay * weight)
    return (updated, momentum, variance)


def body(
    patches,
    live,
    cotangent,
    w_qkv,
    w_proj,
    w_in,
    w_out,
    vectors,
    first_qkv,
    first_proj,
    first_in,
    first_out,
    first_vectors,
    second_qkv,
    second_proj,
    second_in,
    second_out,
    second_vectors,
):
    core = lax.axis_index(SECTION)
    first = core == 0
    count_dp = lax.axis_size(DP)
    tuned = count_dp == LEVELS * SIDE
    me = 2 * lax.axis_index(Y) + lax.axis_index(X)
    place = core.astype(jnp.int32).reshape(1)
    masters = (w_qkv[0], w_proj[0], w_in[0], w_out[0], vectors[0])
    width = patches.shape[1]
    deep = width // SLABS
    hidden_width = w_in.shape[2]
    count_vectors = vectors.shape[1]
    half_vectors = count_vectors // 2
    half_qkv = w_qkv.shape[2] // 2
    stripe = hidden_width // (2 * count_dp)
    tokens = patches.shape[0] // 2
    images = live.shape[0] // 2
    line = Line()
    layers = (Layer(), Layer())

    def halves_of(array, groups):
        rows, columns = array.shape
        if groups == 1:
            return array[:, : columns // 2], array[:, columns // 2 :]
        shaped = array.reshape(rows, groups, 2, -1)
        return tuple(shaped[:, :, side].reshape(rows, -1) for side in range(2))

    def choose(pair):
        return jnp.where(first, pair[0], pair[1]), jnp.where(first, pair[1], pair[0])

    def join(here, there, axis):
        return jnp.where(
            first,
            jnp.concatenate([here, there], axis=axis),
            jnp.concatenate([there, here], axis=axis),
        )

    def pack(array):
        return jnp.concatenate([array[:, :width], array[:, width:]], axis=0)

    def unpack(array):
        rows = array.shape[0] // 2
        return jnp.concatenate([array[:rows], array[rows:]], axis=1)

    def slabs_of(array):
        shaped = array.reshape(SLABS, -1, 2, width)
        return shaped.transpose(0, 2, 1, 3).reshape(SLABS, -1, width)

    def from_slabs(array):
        shaped = array.reshape(SLABS, 2, -1, width)
        return shaped.transpose(0, 2, 1, 3).reshape(-1, 2 * width)

    lowered = [m.astype(low_type) for m in masters]
    qkv, proj = halves_of(lowered[0], 3), halves_of(lowered[1], 1)
    pairs = {
        1: tuple(jnp.concatenate([a, b], axis=1) for a, b in zip(qkv, proj)),
        2: halves_of(lowered[2], count_dp),
        3: tuple(jnp.split(lowered[3], 2, axis=0)),
    }
    parts = ({}, {})
    if tuned:
        pairs[1] = tuple(pack(a) for a in pairs[1])
        pairs[2] = tuple(pack(a) for a in pairs[2])
        spread = jnp.pad(
            lowered[4], ((0, SLABS - count_vectors), (0, width - lowered[4].shape[1]))
        )
        pairs[0] = (spread, spread)
        names = list(pairs)
        here = jnp.concatenate([choose(pairs[name])[0] for name in names], axis=0)
        there = jnp.concatenate([choose(pairs[name])[1] for name in names], axis=0)
        both = swap_halves(here, there, first)
        start = 0
        for name in names:
            stop = start + pairs[name][0].shape[0]
            for layer in range(2):
                parts[layer][name] = both[layer][start:stop]
            start = stop
    else:
        for name in pairs:
            parts[0][name], parts[1][name] = swap_halves(*choose(pairs[name]), first)
        other = swap_cores(lowered[4])
        parts[0][0] = jnp.where(first, lowered[4], other)
        parts[1][0] = jnp.where(first, other, lowered[4])

    layers[0].x = lax.dynamic_slice_in_dim(patches, core * tokens, tokens, axis=0)

    def target_of(side):
        weighting = lax.dynamic_slice_in_dim(live, side * images, images, axis=0).astype(low_type)
        target = lax.dynamic_slice_in_dim(cotangent, side * tokens, tokens, axis=0)
        target = target.reshape(images, SEQ, width) * weighting.reshape(images, 1, 1)
        return target.reshape(tokens, width)

    layers[1].dy = target_of(core)
    layers[1].dy_other = target_of(1 - core)

    def forward_one(number):
        layer = layers[number]
        (inputs,) = line.sync(layer.x)
        if tuned:
            spread = layer.spread[:, :count_vectors, :deep]
            rows = spread.transpose(1, 0, 2).reshape(count_vectors, width).astype(wide)
        else:
            rows = layer.spread.astype(wide)
        scaled, _ = normalize(inputs.astype(wide))
        hidden = (scaled * rows[0] + rows[1]).astype(low_type)
        query, value = [choose(halves_of(rows[i : i + 1], 1)) for i in (2, 3)]
        zero = jnp.zeros_like(query[0])
        bias = jnp.stack(
            [jnp.concatenate([query[s], zero, value[s]], axis=1) for s in range(2)]
        )
        hidden, bias, layer.rows = line.sync(hidden, bias, rows)
        layer.hidden = hidden
        weights = layer.weights[1]
        (packed,) = project(hidden, weights, 0, half_qkv // TILE, bias, low_type)
        (layer.packed,) = line.sync(packed)

    def forward_two(number):
        layer = layers[number]
        packed, rows, inputs = line.sync(layer.packed, layer.rows, layer.x)
        mixed = attend(packed)
        mixed = join(mixed[0], mixed[1], 1)
        bias = jnp.stack(choose(halves_of(rows[4:5], 1)))
        (branch,) = project(mixed, layer.weights[1], half_qkv // TILE, 1, bias, wide)
        middle = inputs.astype(wide) + join(branch[0], branch[1], 1)
        scaled, _ = normalize(middle)
        hidden = (scaled * rows[5] + rows[6]).astype(low_type)
        layer.mixed, layer.middle, layer.hidden_two = line.sync(mixed, middle, hidden)
        (kept,) = line.sync(jnp.stack([layer.hidden, layer.mixed, layer.hidden_two]))
        layer.kept_other = swap_cores(kept)

    def forward_three(number):
        layer = layers[number]
        hidden, rows, layer.kept_other = line.sync(
            layer.hidden_two, layer.rows, layer.kept_other
        )
        bias = jnp.stack(choose(halves_of(rows[8:12].reshape(1, -1), count_dp)))
        count = hidden_width // 2 // TILE
        pair = project(hidden, layer.weights[2], 0, count, bias, low_type, True)
        layer.active, layer.slope = line.sync(*pair)
        layer.active_other = swap_cores(layer.active[1])

    def forward_four(number):
        layer = layers[number]
        active, middle, rows, layer.active_other = line.sync(
            layer.active, layer.middle, layer.rows, layer.active_other
        )
        output = output_rows(active, layer.weights[3], middle, rows[7:8])
        (layer.block,) = line.sync(output)
        if number == 0:
            layers[1].x = layer.block

    def out_grad(number):
        layer = layers[number]
        active, upstream, *other = line.sync(
            layer.active, layer.dy, layer.active_other, layer.dy_other
        )
        plan = ((0, 1, 0, width, 0, hidden_width // 2 // SLABS, 0),)
        grad = weight_grad([(active, 0), (upstream, 0)], [(o, 0) for o in other], 1, plan)
        (layer.chip_grads[3],) = line.sync(grad)

    def in_grad(number):
        layer = layers[number]
        hidden, grad_pre, kept, other = line.sync(
            layer.hidden_two, layer.grad_pre, layer.kept_other, layer.grad_pre_other
        )
        plan = tuple((0, 1, b * width, width, b * deep, deep, 0) for b in range(2))
        grad = weight_grad([(hidden, 0), (grad_pre, 0)], [(kept, 2), (other, 0)], 1, plan)
        (layer.chip_grads[2],) = line.sync(grad)

    def first_grad(number):
        layer = layers[number]
        rows, rows_other = line.sync(layer.grad_rows, layer.rows_other)
        extra = choose(jnp.split(rows + rows_other, 2, axis=0))[0]
        extra = extra.reshape(half_vectors, SLABS, deep).transpose(1, 0, 2).astype(low_type)
        extra = jnp.pad(extra, ((0, 0), (0, SLABS - half_vectors), (0, width - deep)))
        hidden, mixed, slopes, kept, other, extra = line.sync(
            layer.hidden, layer.mixed, layer.slopes, layer.kept_other, layer.slopes_other, extra
        )
        half = width // 2
        plan = (
            (0, 2, 0, width, 0, deep, 0),
            (0, 2, width, half, deep, deep, 0),
            (1, 2, half_qkv, half, deep, deep, half),
        )
        grad = weight_grad(
            [(hidden, 0), (mixed, 0), (slopes, 0)],
            [(kept, 0), (kept, 1), (other, 0)],
            2,
            plan,
            extra,
        )
        (layer.chip_grads[1],) = line.sync(grad)

    def backward_two(number):
        layer = layers[number]
        upstream, slope, layer.dy_other = line.sync(layer.dy, layer.slope, layer.dy_other)
        pair = active_grad(upstream, layer.weights[3], slope)
        layer.grad_pre, layer.bias_in = line.sync(*pair)
        layer.grad_pre_other = swap_cores(layer.grad_pre[1])
        layer.bias_out = jnp.sum(upstream.astype(wide), axis=0, keepdims=True)

    def backward_three(number):
        layer = layers[number]
        grad_pre, middle, rows, upstream = line.sync(
            layer.grad_pre, layer.middle, layer.rows, layer.dy
        )
        results = middle_grad(
            place, grad_pre, layer.weights[2], middle, rows[5:6], upstream, layer.weights[1]
        )
        layer.grad_middle, layer.branch, layer.grad_mixed, layer.norm_two = line.sync(*results)

    def backward_four(number):
        layer = layers[number]
        packed, upstream, branch = line.sync(layer.packed, layer.grad_mixed, layer.branch)
        (layer.slopes,) = line.sync(attend_back(packed, upstream, branch))
        layer.slopes_other = swap_cores(layer.slopes[1])

    def backward_five(number):
        layer = layers[number]
        slopes, inputs, rows, grad_middle = line.sync(
            layer.slopes, layer.x, layer.rows, layer.grad_middle
        )
        entry, sums, columns = entry_grad(
            slopes, half_qkv, layer.weights[1], inputs, rows[0:1], grad_middle
        )
        third = half_qkv // 3
        query = join(columns[0, :, :third], columns[1, :, :third], 1)
        value = join(columns[0, :, 2 * third :], columns[1, :, 2 * third :], 1)
        inner = [s.reshape(count_dp, stripe) for s in layer.bias_in]
        bias_in = jnp.where(first, jnp.stack(inner, axis=1), jnp.stack(inner[::-1], axis=1))
        grad_rows = jnp.concatenate(
            [
                sums[0:2],
                query,
                value,
                layer.norm_two[2:3],
                layer.norm_two[0:2],
                layer.bias_out,
                bias_in.reshape(4, width),
            ],
            axis=0,
        )
        layer.entry, layer.grad_rows = line.sync(entry, grad_rows)
        layer.rows_other = swap_cores(layer.grad_rows)
        if number == 1:
            layers[0].dy = layer.entry
            layers[0].dy_other = swap_cores(layer.entry)

    joined = {}
    squares = [jnp.zeros((), wide)]

    def add_squares(kind):
        pair = line.sync(layers[0].grads[kind], layers[1].grads[kind])
        squares[:] = line.sync(squares[0] + sum(jnp.sum(part * part) for part in pair))

    def join_layers(kind):
        pair = line.sync(layers[0].grads[kind], layers[1].grads[kind])
        got = swap_cores(jnp.where(first, pair[1], pair[0]))
        mine = jnp.where(first, pair[0], pair[1])
        joined[kind] = jnp.where(first, mine, got), jnp.where(first, got, mine)

    def own_tokens(zero, one):
        zero, one = line.sync(zero, one)
        got = swap_cores(jnp.where(first, one, zero))
        return join(jnp.where(first, zero, one), got, 0)

    tokens_out = []

    def token_outputs():
        tokens_out.append(own_tokens(layers[0].block, layers[1].block))
        tokens_out.append(own_tokens(layers[0].entry, layers[1].entry))

    steps = {
        1: forward_one,
        2: forward_two,
        3: forward_three,
        4: forward_four,
        62: backward_two,
        63: backward_three,
        64: backward_four,
        65: backward_five,
        31: first_grad,
        32: in_grad,
        33: out_grad,
    }
    flows = {}
    for index, batch in enumerate(GATHERS):
        values = [parts[key % 10][key // 10] for key in batch]
        if tuned:
            flow = gather_flow_late if index in LATE_GATHERS else gather_flow
            flows[100 + index] = flow(line, values, me, batch, layers)
            continue
        for key, value in zip(batch, values):
            layer = layers[key % 10]
            if key < 10:
                layer.spread = lax.all_gather(value, DP, axis=1, tiled=True)
                continue
            mine = lax.all_gather(value, DP, axis=0, tiled=True)
            mine = mine.reshape(SLABS, -1, width) if key // 10 == 3 else slabs_of(mine)
            layer.weights[key // 10] = (mine, swap_cores(mine))
    if tuned:
        for index, batch in enumerate(SCATTERS):
            flow = scatter_flow_late if index in LATE_SCATTERS else scatter_flow
            flows[200 + index] = flow(line, me, batch, layers)
    for event in ORDER:
        if event in flows:
            next(flows[event], None)
        elif event // 10 in steps:
            steps[event // 10](event % 10)
        elif event == 500:
            token_outputs()
        elif event > 400 and tuned:
            add_squares(event - 400)
            join_layers(event - 400)
    for key in [key for batch in SCATTERS for key in batch if not tuned]:
        layer = layers[key % 10]
        total = layer.chip_grads[key // 10].astype(wide)
        if key // 10 == 3:
            natural = total.reshape(-1, width)
        else:
            natural = from_slabs(total[:, : 2 * deep])
        layer.grads[key // 10] = lax.psum_scatter(natural, DP, scatter_dimension=0, tiled=True)
        if key // 10 == 1:
            thin = total[:, 2 * deep : 2 * deep + half_vectors, :deep].transpose(1, 0, 2)
            thin = thin.reshape(half_vectors, width)
            layer.grads[0] = lax.psum_scatter(thin, DP, scatter_dimension=1, tiled=True)

    kinds = [kind for kind in layers[0].grads if kind not in joined]
    for kind in kinds:
        add_squares(kind)
    if tuned:
        global_sum = total_of(line, squares[0])
    else:
        global_sum = lax.psum(squares[0], (SECTION, *DP))
    for kind in kinds:
        join_layers(kind)

    def woven(pair, groups):
        rows = pair[0].shape[0]
        return jnp.stack([p.reshape(rows, groups, -1) for p in pair], axis=2).reshape(rows, -1)

    one, inner, outer = [joined[kind] for kind in (1, 2, 3)]
    if tuned:
        thin = [p[2 * deep : 2 * deep + half_vectors, :deep] for p in one]
        one, inner = [tuple(unpack(p[: 2 * deep]) for p in pair) for pair in (one, inner)]
    else:
        thin = joined[0]
    shards = (
        woven([p[:, :half_qkv] for p in one], 3),
        jnp.concatenate([p[:, half_qkv:] for p in one], axis=1),
        woven(inner, count_dp),
        jnp.concatenate(outer, axis=0),
        jnp.concatenate(thin, axis=0),
    )
    global_sum, *shards = line.sync(global_sum, *shards)
    grad_norm = jnp.sqrt(global_sum)
    factor = clip_norm / jnp.maximum(grad_norm, clip_norm)
    blocks, input_grad = tokens_out
    firsts = (first_qkv[0], first_proj[0], first_in[0], first_out[0], first_vectors[0])
    seconds = (second_qkv[0], second_proj[0], second_in[0], second_out[0], second_vectors[0])
    rates = (rate_matrix, rate_matrix, rate_matrix, rate_matrix, rate_vector)
    decays = (decay_matrix, decay_matrix, decay_matrix, decay_matrix, 0.0)
    results = [
        adam_update(w, g, f, s, factor, r, d)
        for w, g, f, s, r, d in zip(masters, shards, firsts, seconds, rates, decays)
    ]
    news = tuple((item[0][None] for item in results))
    momenta = tuple((item[1][None] for item in results))
    variances = tuple((item[2][None] for item in results))
    copies = tuple((n.astype(low_type) for n in news))
    grads_out = tuple((s[None] for s in shards))
    return (
        blocks[None],
        input_grad[None],
        *grads_out,
        grad_norm,
        *news,
        *copies,
        *momenta,
        *variances,
    )


def solution(mesh):
    devices = mesh.devices
    split = devices.reshape(devices.shape[0], devices.shape[1] // SIDE, 2, 2)
    mesh = Mesh(split, (SECTION, *DP))
    tokens = P(DP, None)
    matrix = P(SECTION, DP, None)
    columns = P(SECTION, None, DP)
    group = (matrix, matrix, matrix, matrix, columns)
    in_specs = (tokens, P(DP), tokens, *group, *group, *group)
    out_specs = (matrix, matrix, *group, P(), *group, *group, *group, *group)
    return jax.shard_map(body, mesh=mesh, in_specs=in_specs, out_specs=out_specs, check_vma=False)
```

time: 1980 us -> 784 us (0.40)
  waiting for transfers between devices: 1190 us -> 227 us
  matrix products: 463 us -> 0 us
  Pallas kernels: 0 us -> 206 us
  blocking collectives: 87.7 us -> 0 us
  starting transfers between devices: 13.6 us -> 69.5 us
  local copies, waits for them, and re-layouts: 126 us -> 158 us
  other arithmetic: 67.8 us -> 87.9 us
    reduce_scatter x4 -> x6, waiting for transfers between devices: 873 us -> 14.7 us  [scatter_flow(): total = lax.psum_scatter(column, Z, scatter_dimension=0, tiled=False)]
    dot_general x85 -> x0, matrix products: 446 us -> none  [the longest x5 66.1 us: layer_backward(): jnp.einsum('nf,nd->fd', active_low, grad_out_low, preferred_element_type=...]
    all_gather x4 -> x6, waiting for transfers between devices: 317 us -> 85.4 us  [gather_flow(): column = lax.all_gather(part, Z, axis=0, tiled=False)]
    pallas_call x0 -> x24, Pallas kernels: none -> 206 us  [the longest x6 49.8 us: weight_grad(): pl.pallas_call(functools.partial(grad_kernel, pairs, len(own), extra is n...]
    ppermute x8 -> x76, waiting for transfers between devices: 2.67 us -> 126 us  [the longest x50 116 us: flip(): return lax.ppermute(x, axis, [(0, 1), (1, 0)])]
    ppermute x8 -> x76, starting transfers between devices: 13.3 us -> 68.8 us  [the longest x50 59.6 us: flip(): return lax.ppermute(x, axis, [(0, 1), (1, 0)])]
    dynamic_update_slice x0 -> x30, local copies, waits for them, and re-layouts: none -> 45.3 us  [the longest x18 30.8 us: place_blocks(): full = lax.dynamic_update_slice(full, jnp.expand_dims(block, axis), start)]
    convert_element_type x21 -> x10, local copies, waits for them, and re-layouts: 45.9 us -> 1.1 us  [the longest x2 0.64 us: body(): lowered = [m.astype(low_type) for m in masters]]
  transfers between devices with their start and end apart: 17 -> 88, of which waited for: 9 -> 41; matrix products, arithmetic and copies ran while one was open for 14% -> 25% of each run, Pallas kernels for 0% -> 22%
where the time goes in v3:
time: 784 us; the launch traced here: 772 us
  waiting for transfers between devices  227 us (29%)
  Pallas kernels  206 us (26%)
  local copies, waits for them, and re-layouts  158 us (20%)
  other arithmetic  87.9 us (11%)
  starting transfers between devices  69.5 us (9%)
  between operations  24.6 us (3%)
    ppermute x50, waiting for transfers between devices, flip(): return lax.ppermute(x, axis, [(0, 1), (1, 0)])  116 us
    all_gather x6, waiting for transfers between devices, gather_flow(): column = lax.all_gather(part, Z, axis=0, tiled=False)  85.4 us
    ppermute x50, starting transfers between devices, flip(): return lax.ppermute(x, axis, [(0, 1), (1, 0)])  59.6 us
    pallas_call x6, Pallas kernels, weight_grad(): pl.pallas_call(functools.partial(grad_kernel, pairs, len(own), extra is n...  49.8 us
    pallas_call x6, Pallas kernels, project(): pl.pallas_call(functools.partial(project_kernel, smooth, count), grid=(2...  43.2 us
    dynamic_update_slice x18, local copies, waits for them, and re-layouts, place_blocks(): full = lax.dynamic_update_slice(full, jnp.expand_dims(block, axis), start)  30.8 us
    pallas_call x2, Pallas kernels, attend_back(): pl.pallas_call(attend_back_kernel, grid=(groups,), in_specs=[third_at(thi...  29.1 us
    pallas_call x2, Pallas kernels, middle_grad(): pl.pallas_call(middle_grad_kernel, grid=(STEPS,), in_specs=[pl.BlockSpec(...  21.5 us
  transfers between devices with their start and end apart: 88, of which 41 were waited for; matrix products, arithmetic and copies ran while one was open for 25% of the time, Pallas kernels for 22%

profile of v3, /device:TPU:0, one launch (start us, length us, event | category | flops | bytes accessed | tf_op | source)
XLA Modules:
  0.0 772.5 jit_solution(14013818037192469435)
XLA Ops:
  26.5 26.8 %all-gather.13.cloned.1.call-done = bf16[512,1024]{1,0:T(8,128)(2,1)} async-done(((bf16[128,1024]{1,0:T(8,128)(2,1)}), bf16[512,1024]{1,0:T(8,128)(2,1)}) %all-gather.13.cloned.1.call-update) | async-done | bytes 1048592 | tf_op jit(solution)/shard_map/all_gather | solution.py:106
  56.2 31.4 %all-gather.15.cloned.1.call-done = bf16[640,1024]{1,0:T(8,128)(2,1)} async-done(((bf16[160,1024]{1,0:T(8,128)(2,1)}), bf16[640,1024]{1,0:T(8,128)(2,1)}) %all-gather.15.cloned.1.call-update) | async-done | bytes 1310736 | tf_op jit(solution)/shard_map/all_gather | solution.py:106
  90.7 26.1 %all-gather.17.cloned.1.call-done = bf16[512,1024]{1,0:T(8,128)(2,1)} async-done(((bf16[128,1024]{1,0:T(8,128)(2,1)}), bf16[512,1024]{1,0:T(8,128)(2,1)}) %all-gather.17.cloned.1.call-update) | async-done | bytes 1048592 | tf_op jit(solution)/shard_map/all_gather | solution.py:106
  146.2 8.5 %collective-permute-done.7 = bf16[2,160,1024]{2,1,0:T(8,128)(2,1)} collective-permute-done((bf16[2,160,1024]{2,1,0:T(8,128)(2,1)}, bf16[2,160,1024]{2,1,0:T(8,128)(2,1)}, u32[]{:S(2)}, u32[]{:S(2)}) %collective-permute-start.7) | collective-permute-done | bytes 655392 | tf_op jit(solution)/shard_map/ppermute | solution.py:52
  170.1 7.2 project.6
  200.7 8.1 %collective-permute-done.12 = bf16[4,128,1024]{2,1,0:T(8,128)(2,1)} collective-permute-done((bf16[4,128,1024]{2,1,0:T(8,128)(2,1)}, bf16[4,128,1024]{2,1,0:T(8,128)(2,1)}, u32[]{:S(2)}, u32[]{:S(2)}) %collective-permute-start.12) | collective-permute-done | bytes 1048608 | tf_op jit(solution)/shard_map/ppermute | solution.py:52
  230.6 6.8 collective-permute-done.16
  246.8 11.3 %project.8 = (bf16[2,400,2048]{2,1,0:T(8,128)(2,1)S(1)}, bf16[2,400,2048]{2,1,0:T(8,128)(2,1)}) custom-call(bf16[400,1024]{1,0:T(8,128)(2,1)S(1)} %add_convert_fusion.7.x_ref.refs_0_, bf16[16,128,1024]{2,1,0:T(8,128)(2,1)} %bitcast.21.here_ref.refs_1_, bf16[16,128,1024]{2,1,0:T(8,128)(2,1)} %collective-permute-done.18.there_ref.refs_2_, ...), custom_call_target="tpu_custom_call" | custom-call | flops 3355443200 | bytes 8388608 | tf_op jit(solution)/shard_map/project/pallas_call | solution.py:427
  261.4 7.1 collective-permute-done.20
  282.4 6.8 output.2.inputs
  293.9 7.2 project.9
  331.2 11.2 %project.11 = (bf16[2,400,2048]{2,1,0:T(8,128)(2,1)S(1)}, bf16[2,400,2048]{2,1,0:T(8,128)(2,1)}) custom-call(bf16[400,1024]{1,0:T(8,128)(2,1)S(1)} %copy-done.36, bf16[16,128,1024]{2,1,0:T(8,128)(2,1)} %bitcast.79.here_ref.refs_1_, bf16[16,128,1024]{2,1,0:T(8,128)(2,1)} %collective-permute-done.31.there_ref.refs_2_, f32[2,1,2048]{2,1,0:T(1,128)S(1)} %pad_maximum_fusion.26.b_ref), custom_call_target="tpu_custom_call" | custom-call | flops 3355443200 | bytes 8388608 | tf_op jit(solution)/shard_map/project/pallas_call | solution.py:427
  349.3 7.5 grad.6
  356.8 9.6 %active.2 = (bf16[2,400,2048]{2,1,0:T(8,128)(2,1)S(1)}, f32[2,1,2048]{2,1,0:T(1,128)S(1)}) custom-call(bf16[400,1024]{1,0:T(8,128)(2,1)S(1)} %get-tuple-element.699.refs_1_.up_ref.refs_5_, bf16[16,128,1024]{2,1,0:T(8,128)(2,1)} %bitcast.106.w_here, bf16[16,128,1024]{2,1,0:T(8,128)(2,1)} %collective-permute-done.34.w_there, ...), custom_call_target="tpu_custom_call" | custom-call | flops 3355443200 | bytes 12582912 | tf_op jit(solution)/shard_map/active/pallas_call | solution.py:493
  368.2 10.6 %middle.2 = (f32[400,1024]{1,0:T(8,128)S(1)}, bf16[2,400,512]{2,1,0:T(8,128)(2,1)S(1)}, bf16[2,400,512]{2,1,0:T(8,128)(2,1)S(1)}, f32[8,1024]{1,0:T(8,128)S(1)}) custom-call(s32[1]{0:T(128)} %bitcast.112.place, bf16[2,400,2048]{2,1,0:T(8,128)(2,1)} %copy-done.30, bf16[16,128,1024]{2,1,0:T(8,128)(2,1)} %bitcast.79.here_ref.refs_1_, ...), custom_call_target="tpu_custom_call" | custom-call | flops 4194304000 | bytes 8388608 | tf_op jit(solution)/shard_map/middle/pallas_call | solution.py:566
  382.3 14.5 %attend_back.2 = bf16[4,200,2048]{2,1,0:T(8,128)(2,1)} custom-call(bf16[4,200,1536]{2,1,0:T(8,128)(2,1)S(1)} %bitcast.576, bf16[4,200,1536]{2,1,0:T(8,128)(2,1)S(1)} %bitcast.577, bf16[4,200,1536]{2,1,0:T(8,128)(2,1)S(1)} %bitcast.578, bf16[4,200,512]{2,1,0:T(8,128)(2,1)S(1)} %bitcast.588, bf16[4,200,512]{2,1,0:T(8,128)(2,1)S(1)} %bitcast.587), custom_call_target="tpu_custom_call" | custom-call | flops 1638400000 | bytes 5734400 | tf_op jit(solution)/shard_map/attend_back/pallas_call | solution.py:361
  404.1 7.3 collective-permute-done.35
  417.7 8.5 %entry.2 = (bf16[400,1024]{1,0:T(8,128)(2,1)S(1)}, f32[8,1024]{1,0:T(8,128)S(1)}, f32[2,1,1536]{2,1,0:T(1,128)S(1)}) custom-call(bf16[2,400,2048]{2,1,0:T(8,128)(2,1)} %bitcast.593, bf16[16,128,1024]{2,1,0:T(8,128)(2,1)} %bitcast.65.here_ref.refs_6_.w_here, bf16[16,128,1024]{2,1,0:T(8,128)(2,1)} %collective-permute-done.26.there_ref.refs_7_.w_there, ...), custom_call_target="tpu_custom_call" | custom-call | flops 2516582400 | bytes 6291456 | tf_op jit(solution)/shard_map/entry/pallas_call | solution.py:616
  434.2 8.7 %grad.7 = bf16[16,144,1024]{2,1,0:T(8,128)(2,1)} custom-call(bf16[400,1024]{1,0:T(8,128)(2,1)S(1)} %copy-done.17, bf16[400,1024]{1,0:T(8,128)(2,1)S(1)} %copy-done.19, bf16[2,400,2048]{2,1,0:T(8,128)(2,1)} %bitcast.594, bf16[3,400,1024]{2,1,0:T(8,128)(2,1)} %collective-permute-done.32.refs_3_.refs_4_.refs_2_, ...), custom_call_target="tpu_custom_call" | custom-call | flops 3774873600 | bytes 9437184 | tf_op jit(solution)/shard_map/grad/pallas_call | solution.py:682
  445.3 9.7 %active.3 = (bf16[2,400,2048]{2,1,0:T(8,128)(2,1)S(1)}, f32[2,1,2048]{2,1,0:T(1,128)S(1)}) custom-call(bf16[400,1024]{1,0:T(8,128)(2,1)S(1)} %copy-done.21, bf16[16,128,1024]{2,1,0:T(8,128)(2,1)} %bitcast.59.w_here, bf16[16,128,1024]{2,1,0:T(8,128)(2,1)} %collective-permute-done.22.w_there, bf16[2,400,2048]{2,1,0:T(8,128)(2,1)} %get-tuple-element.757.slope_ref), custom_call_target="tpu_custom_call" | custom-call | flops 3355443200 | bytes 12582912 | tf_op jit(solution)/shard_map/active/pallas_call | solution.py:493
  478.8 8.3 %grad.8 = bf16[16,128,1024]{2,1,0:T(8,128)(2,1)} custom-call(bf16[400,1024]{1,0:T(8,128)(2,1)S(1)} %copy-done.37, bf16[2,400,2048]{2,1,0:T(8,128)(2,1)} %copy-done.30, bf16[3,400,1024]{2,1,0:T(8,128)(2,1)} %collective-permute-done.32.refs_3_.refs_4_.refs_2_, bf16[400,2048]{1,0:T(8,128)(2,1)} %collective-permute-done.44.refs_3_), custom_call_target="tpu_custom_call" | custom-call | flops 3355443200 | bytes 8388608 | tf_op jit(solution)/shard_map/grad/pallas_call | solution.py:682
  489.6 8.3 %grad.9 = bf16[16,128,1024]{2,1,0:T(8,128)(2,1)} custom-call(bf16[400,1024]{1,0:T(8,128)(2,1)S(1)} %copy-done.34, bf16[2,400,2048]{2,1,0:T(8,128)(2,1)} %copy-done.32, bf16[3,400,1024]{2,1,0:T(8,128)(2,1)} %collective-permute-done.19.refs_2_.refs_3_.refs_4_, bf16[400,2048]{1,0:T(8,128)(2,1)} %collective-permute-done.45.refs_3_), custom_call_target="tpu_custom_call" | custom-call | flops 3355443200 | bytes 8388608 | tf_op jit(solution)/shard_map/grad/pallas_call | solution.py:682
  514.6 10.9 %middle.3 = (f32[400,1024]{1,0:T(8,128)S(1)}, bf16[2,400,512]{2,1,0:T(8,128)(2,1)S(1)}, bf16[2,400,512]{2,1,0:T(8,128)(2,1)S(1)}, f32[8,1024]{1,0:T(8,128)S(1)}) custom-call(s32[1]{0:T(128)} %bitcast.112.place, bf16[2,400,2048]{2,1,0:T(8,128)(2,1)} %copy-done.32, bf16[16,128,1024]{2,1,0:T(8,128)(2,1)} %bitcast.21.here_ref.refs_1_, ...), custom_call_target="tpu_custom_call" | custom-call | flops 4194304000 | bytes 8388608 | tf_op jit(solution)/shard_map/middle/pallas_call | solution.py:566
  532.2 14.5 %attend_back.3 = bf16[4,200,2048]{2,1,0:T(8,128)(2,1)} custom-call(bf16[4,200,1536]{2,1,0:T(8,128)(2,1)S(1)} %bitcast.570, bf16[4,200,1536]{2,1,0:T(8,128)(2,1)S(1)} %bitcast.571, bf16[4,200,1536]{2,1,0:T(8,128)(2,1)S(1)} %bitcast.572, bf16[4,200,512]{2,1,0:T(8,128)(2,1)S(1)} %bitcast.586, bf16[4,200,512]{2,1,0:T(8,128)(2,1)S(1)} %bitcast.585), custom_call_target="tpu_custom_call" | custom-call | flops 1638400000 | bytes 5734400 | tf_op jit(solution)/shard_map/attend_back/pallas_call | solution.py:361
  564.5 8.3 %grad.10 = bf16[16,128,1024]{2,1,0:T(8,128)(2,1)} custom-call(bf16[2,400,2048]{2,1,0:T(8,128)(2,1)} %copy-done.26, bf16[400,1024]{1,0:T(8,128)(2,1)S(1)} %copy-done.23, bf16[400,2048]{1,0:T(8,128)(2,1)} %collective-permute-done.23.refs_2_, bf16[400,1024]{1,0:T(8,128)(2,1)} %collective-permute-done.39.refs_3_), custom_call_target="tpu_custom_call" | custom-call | flops 3355443200 | bytes 8388608 | tf_op jit(solution)/shard_map/grad/pallas_call | solution.py:682
  575.1 8.6 %entry.3 = (bf16[400,1024]{1,0:T(8,128)(2,1)S(1)}, f32[8,1024]{1,0:T(8,128)S(1)}, f32[2,1,1536]{2,1,0:T(1,128)S(1)}) custom-call(bf16[2,400,2048]{2,1,0:T(8,128)(2,1)} %bitcast.590, bf16[16,160,1024]{2,1,0:T(8,128)(2,1)} %bitcast.27.here_ref.refs_6_.w_here, bf16[16,160,1024]{2,1,0:T(8,128)(2,1)} %collective-permute-done.9.there_ref.refs_7_.w_there, ...), custom_call_target="tpu_custom_call" | custom-call | flops 2516582400 | bytes 6291456 | tf_op jit(solution)/shard_map/entry/pallas_call | solution.py:616
  591.3 8.0 %collective-permute-done.56 = bf16[2,128,1024]{2,1,0:T(8,128)(2,1)S(1)} collective-permute-done((bf16[2,128,1024]{2,1,0:T(8,128)(2,1)}, bf16[2,128,1024]{2,1,0:T(8,128)(2,1)S(1)}, u32[]{:S(2)}, u32[]{:S(2)}) %collective-permute-start.56) | collective-permute-done | bytes 524320 | tf_op jit(solution)/shard_map/ppermute | solution.py:52
  606.4 8.7 %grad.11 = bf16[16,144,1024]{2,1,0:T(8,128)(2,1)} custom-call(bf16[400,1024]{1,0:T(8,128)(2,1)S(1)} %copy-done.13, bf16[400,1024]{1,0:T(8,128)(2,1)S(1)} %copy-done.15, bf16[2,400,2048]{2,1,0:T(8,128)(2,1)} %bitcast.591, bf16[3,400,1024]{2,1,0:T(8,128)(2,1)} %collective-permute-done.19.refs_2_.refs_3_.refs_4_, ...), custom_call_target="tpu_custom_call" | custom-call | flops 3774873600 | bytes 9437184 | tf_op jit(solution)/shard_map/grad/pallas_call | solution.py:682
  619.9 21.7 %collective-permute-done.62 = bf16[2,144,1024]{2,1,0:T(8,128)(2,1)S(1)} collective-permute-done((bf16[2,144,1024]{2,1,0:T(8,128)(2,1)S(1)}, bf16[2,144,1024]{2,1,0:T(8,128)(2,1)S(1)}, u32[]{:S(2)}, u32[]{:S(2)}) %collective-permute-start.62) | collective-permute-done | bytes 589856 | tf_op jit(solution)/shard_map/ppermute | solution.py:52
  650.6 6.6 output.3
  659.6 15.9 %collective-permute-done.66 = bf16[4,144,1024]{2,1,0:T(8,128)(2,1)S(1)} collective-permute-done((bf16[4,144,1024]{2,1,0:T(8,128)(2,1)S(1)}, bf16[4,144,1024]{2,1,0:T(8,128)(2,1)S(1)}, u32[]{:S(2)}, u32[]{:S(2)}) %collective-permute-start.66) | collective-permute-done | bytes 1179680 | tf_op jit(solution)/shard_map/ppermute | solution.py:52
  691.7 14.6 %reduce-scatter.17.cloned.1.call-done = bf16[1,144,1024]{2,1,0:T(8,128)(2,1)} async-done(((bf16[4,144,1024]{2,1,0:T(8,128)(2,1)}), bf16[1,144,1024]{2,1,0:T(8,128)(2,1)}) %reduce-scatter.17.cloned.1.call-update) | async-done | bytes 294928 | tf_op jit(solution)/shard_map/reduce_scatter | solution.py:196
  (630 shorter events, 378.5 us)
Async XLA Ops:
  7.2 46.1 %all-gather.13.cloned.1.call-start = ((), (), s32[]{:S(2)}) async-start(), calls=%async_computation.12 | async-start | bytes 1310720 | tf_op jit(solution)/shard_map/all_gather | solution.py:106
  22.6 65.1 %all-gather.15.cloned.1.call-start = ((), (), s32[]{:S(2)}) async-start(), calls=%async_computation.13 | async-start | bytes 1638400 | tf_op jit(solution)/shard_map/all_gather | solution.py:106
  25.7 91.1 %all-gather.17.cloned.1.call-start = ((), (), s32[]{:S(2)}) async-start(), calls=%async_computation.14 | async-start | bytes 1310720 | tf_op jit(solution)/shard_map/all_gather | solution.py:106
  26.4 119.8 %all-gather.19.cloned.1.call-start = ((), (), s32[]{:S(2)}) async-start(), calls=%async_computation.15 | async-start | bytes 1310720 | tf_op jit(solution)/shard_map/all_gather | solution.py:106
  53.3 63.5 %collective-permute-start.1 = (bf16[4,128,1024]{2,1,0:T(8,128)(2,1)}, bf16[4,128,1024]{2,1,0:T(8,128)(2,1)}, u32[]{:S(2)}, u32[]{:S(2)}) collective-permute-start(bf16[4,128,1024]{2,1,0:T(8,128)(2,1)} %bitcast.651), channel_id=1, source_target_pairs={{0,1},{1,0},{2,3},{3,2},{4,5},{5,4},{6,7},{7,6},{8,9},{9,8},{10,11... | collective-permute-start | bytes 3145736 | tf_op jit(solution)/shard_map/ppermute | solution.py:52
  54.8 62.0 %collective-permute-start.2 = (bf16[4,128,1024]{2,1,0:T(8,128)(2,1)}, bf16[4,128,1024]{2,1,0:T(8,128)(2,1)}, u32[]{:S(2)}, u32[]{:S(2)}) collective-permute-start(bf16[4,128,1024]{2,1,0:T(8,128)(2,1)} %bitcast.652), channel_id=1, source_target_pairs={{0,2},{2,0},{1,3},{3,1},{4,6},{6,4},{5,7},{7,5},{8,10},{10,8},{9,1... | collective-permute-start | bytes 3145736 | tf_op jit(solution)/shard_map/ppermute | solution.py:52
  87.7 42.4 %collective-permute-start.3 = (bf16[4,160,1024]{2,1,0:T(8,128)(2,1)}, bf16[4,160,1024]{2,1,0:T(8,128)(2,1)S(1)}, u32[]{:S(2)}, u32[]{:S(2)}) collective-permute-start(bf16[4,160,1024]{2,1,0:T(8,128)(2,1)} %bitcast.632), channel_id=1, source_target_pairs={{0,1},{1,0},{2,3},{3,2},{4,5},{5,4},{6,7},{7,6},{8,9},{9,8},{10,11... | collective-permute-start | bytes 3932168 | tf_op jit(solution)/shard_map/ppermute | solution.py:52
  89.1 40.9 %collective-permute-start.4 = (bf16[4,160,1024]{2,1,0:T(8,128)(2,1)}, bf16[4,160,1024]{2,1,0:T(8,128)(2,1)}, u32[]{:S(2)}, u32[]{:S(2)}) collective-permute-start(bf16[4,160,1024]{2,1,0:T(8,128)(2,1)} %bitcast.633), channel_id=1, source_target_pairs={{0,2},{2,0},{1,3},{3,1},{4,6},{6,4},{5,7},{7,5},{8,10},{10,8},{9,1... | collective-permute-start | bytes 3932168 | tf_op jit(solution)/shard_map/ppermute | solution.py:52
  90.6 140.0 %all-gather.21.cloned.1.call-start = ((), (), s32[]{:S(2)}) async-start(), calls=%async_computation.16 | async-start | bytes 1310720 | tf_op jit(solution)/shard_map/all_gather | solution.py:106
  160.1 130.8 %all-gather.23.cloned.1.call-start = ((), (), s32[]{:S(2)}) async-start(), calls=%async_computation.17 | async-start | bytes 1310720 | tf_op jit(solution)/shard_map/all_gather | solution.py:106
  160.4 29.5 %collective-permute-start.10 = (bf16[4,128,1024]{2,1,0:T(8,128)(2,1)}, bf16[4,128,1024]{2,1,0:T(8,128)(2,1)}, u32[]{:S(2)}, u32[]{:S(2)}) collective-permute-start(bf16[4,128,1024]{2,1,0:T(8,128)(2,1)} %bitcast.639), channel_id=1, source_target_pairs={{0,1},{1,0},{2,3},{3,2},{4,5},{5,4},{6,7},{7,6},{8,9},{9,8},{10,11... | collective-permute-start | bytes 3145736 | tf_op jit(solution)/shard_map/ppermute | solution.py:52
  162.5 46.4 %collective-permute-start.12 = (bf16[4,128,1024]{2,1,0:T(8,128)(2,1)}, bf16[4,128,1024]{2,1,0:T(8,128)(2,1)}, u32[]{:S(2)}, u32[]{:S(2)}) collective-permute-start(bf16[4,128,1024]{2,1,0:T(8,128)(2,1)} %bitcast.645), channel_id=1, source_target_pairs={{0,1},{1,0},{2,3},{3,2},{4,5},{5,4},{6,7},{7,6},{8,9},{9,8},{10,11... | collective-permute-start | bytes 3145736 | tf_op jit(solution)/shard_map/ppermute | solution.py:52
  163.9 45.1 %collective-permute-start.13 = (bf16[4,128,1024]{2,1,0:T(8,128)(2,1)}, bf16[4,128,1024]{2,1,0:T(8,128)(2,1)}, u32[]{:S(2)}, u32[]{:S(2)}) collective-permute-start(bf16[4,128,1024]{2,1,0:T(8,128)(2,1)} %bitcast.646), channel_id=1, source_target_pairs={{0,2},{2,0},{1,3},{3,1},{4,6},{6,4},{5,7},{7,5},{8,10},{10,8},{9,1... | collective-permute-start | bytes 3145736 | tf_op jit(solution)/shard_map/ppermute | solution.py:52
  169.0 74.9 %collective-permute-start.18 = (bf16[16,128,1024]{2,1,0:T(8,128)(2,1)}, bf16[16,128,1024]{2,1,0:T(8,128)(2,1)}, u32[]{:S(2)}, u32[]{:S(2)}) collective-permute-start(bf16[16,128,1024]{2,1,0:T(8,128)(2,1)} %bitcast.21.here_ref.refs_1_), channel_id=1, source_target_pairs={{0,16},{16,0},{1,17},{17,1},{2,18},{18,2},{3,19},{19,3},{4,20},{20... | collective-permute-start | bytes 12582920 | tf_op jit(solution)/shard_map/ppermute | solution.py:48
  189.9 55.5 %collective-permute-start.19 = (bf16[3,400,1024]{2,1,0:T(8,128)(2,1)}, bf16[3,400,1024]{2,1,0:T(8,128)(2,1)}, u32[]{:S(2)}, u32[]{:S(2)}) collective-permute-start(bf16[3,400,1024]{2,1,0:T(8,128)(2,1)} %pad_maximum_fusion), channel_id=1, source_target_pairs={{0,16},{16,0},{1,17},{17,1},{2,18},{18,2},{3,19},{19,3},{4,20},{20... | collective-permute-start | bytes 7372808 | tf_op jit(solution)/shard_map/ppermute | solution.py:48
  230.6 51.7 %collective-permute-start.22 = (bf16[16,128,1024]{2,1,0:T(8,128)(2,1)}, bf16[16,128,1024]{2,1,0:T(8,128)(2,1)}, u32[]{:S(2)}, u32[]{:S(2)}) collective-permute-start(bf16[16,128,1024]{2,1,0:T(8,128)(2,1)} %bitcast.59.w_here), channel_id=1, source_target_pairs={{0,16},{16,0},{1,17},{17,1},{2,18},{18,2},{3,19},{19,3},{4,20},{20... | collective-permute-start | bytes 12582920 | tf_op jit(solution)/shard_map/ppermute | solution.py:48
  242.6 48.3 %collective-permute-start.26 = (bf16[16,128,1024]{2,1,0:T(8,128)(2,1)}, bf16[16,128,1024]{2,1,0:T(8,128)(2,1)}, u32[]{:S(2)}, u32[]{:S(2)}) collective-permute-start(bf16[16,128,1024]{2,1,0:T(8,128)(2,1)} %bitcast.65.here_ref.refs_6_.w_here), channel_id=1, source_target_pairs={{0,16},{16,0},{1,17},{17,1},{2,18},{18,2},{3,19},{19,3},{4,20},{20... | collective-permute-start | bytes 12582920 | tf_op jit(solution)/shard_map/ppermute | solution.py:48
  261.1 241.5 %reduce-scatter.7.cloned.1.call-start = ((), (), s32[]{:S(2)}) async-start(), calls=%async_computation.6 | async-start | bytes 1310720 | tf_op jit(solution)/shard_map/reduce_scatter | solution.py:196
  402.2 29.8 %collective-permute-start.38 = (bf16[400,2048]{1,0:T(8,128)(2,1)}, bf16[400,2048]{1,0:T(8,128)(2,1)}, u32[]{:S(2)}, u32[]{:S(2)}) collective-permute-start(bf16[400,2048]{1,0:T(8,128)(2,1)} %slice_bitcast_fusion.3), channel_id=1, source_target_pairs={{0,16},{16,0},{1,17},{17,1},{2,18},{18,2},{3,19},{19,3},{4,20},{20... | collective-permute-start | bytes 4915208 | tf_op jit(solution)/shard_map/ppermute | solution.py:48
  403.4 73.8 %collective-permute-start.44 = (bf16[400,2048]{1,0:T(8,128)(2,1)}, bf16[400,2048]{1,0:T(8,128)(2,1)}, u32[]{:S(2)}, u32[]{:S(2)}) collective-permute-start(bf16[400,2048]{1,0:T(8,128)(2,1)} %slice_bitcast_fusion.2), channel_id=1, source_target_pairs={{0,16},{16,0},{1,17},{17,1},{2,18},{18,2},{3,19},{19,3},{4,20},{20... | collective-permute-start | bytes 4915208 | tf_op jit(solution)/shard_map/ppermute | solution.py:48
  462.9 90.7 %reduce-scatter.9.cloned.1.call-start = ((), (), s32[]{:S(2)}) async-start(), calls=%async_computation.7 | async-start | bytes 1474560 | tf_op jit(solution)/shard_map/reduce_scatter | solution.py:196
  500.2 46.5 %collective-permute-start.50 = (bf16[2,128,1024]{2,1,0:T(8,128)(2,1)}, bf16[2,128,1024]{2,1,0:T(8,128)(2,1)}, u32[]{:S(2)}, u32[]{:S(2)}) collective-permute-start(bf16[2,128,1024]{2,1,0:T(8,128)(2,1)} %get-tuple-element.830), channel_id=1, source_target_pairs={{0,1},{1,0},{2,3},{3,2},{4,5},{5,4},{6,7},{7,6},{8,9},{9,8},{10,11... | collective-permute-start | bytes 1572872 | tf_op jit(solution)/shard_map/ppermute | solution.py:52
  501.6 45.1 %collective-permute-start.51 = (bf16[2,128,1024]{2,1,0:T(8,128)(2,1)}, bf16[2,128,1024]{2,1,0:T(8,128)(2,1)}, u32[]{:S(2)}, u32[]{:S(2)}) collective-permute-start(bf16[2,128,1024]{2,1,0:T(8,128)(2,1)} %get-tuple-element.831), channel_id=1, source_target_pairs={{0,2},{2,0},{1,3},{3,1},{4,6},{6,4},{5,7},{7,5},{8,10},{10,8},{9,1... | collective-permute-start | bytes 1572872 | tf_op jit(solution)/shard_map/ppermute | solution.py:52
  512.0 166.7 %reduce-scatter.11.cloned.1.call-start = ((), (), s32[]{:S(2)}) async-start(), calls=%async_computation.8 | async-start | bytes 1310720 | tf_op jit(solution)/shard_map/reduce_scatter | solution.py:196
  550.5 34.2 %collective-permute-start.54 = (bf16[4,128,1024]{2,1,0:T(8,128)(2,1)}, bf16[4,128,1024]{2,1,0:T(8,128)(2,1)}, u32[]{:S(2)}, u32[]{:S(2)}) collective-permute-start(bf16[4,128,1024]{2,1,0:T(8,128)(2,1)} %pad_maximum_fusion.10), channel_id=1, source_target_pairs={{0,1},{1,0},{2,3},{3,2},{4,5},{5,4},{6,7},{7,6},{8,9},{9,8},{10,11... | collective-permute-start | bytes 3145736 | tf_op jit(solution)/shard_map/ppermute | solution.py:52
  551.4 33.3 %collective-permute-start.55 = (bf16[4,128,1024]{2,1,0:T(8,128)(2,1)}, bf16[4,128,1024]{2,1,0:T(8,128)(2,1)}, u32[]{:S(2)}, u32[]{:S(2)}) collective-permute-start(bf16[4,128,1024]{2,1,0:T(8,128)(2,1)} %pad_maximum_fusion.11), channel_id=1, source_target_pairs={{0,2},{2,0},{1,3},{3,1},{4,6},{6,4},{5,7},{7,5},{8,10},{10,8},{9,1... | collective-permute-start | bytes 3145736 | tf_op jit(solution)/shard_map/ppermute | solution.py:52
  559.3 120.4 %reduce-scatter.13.cloned.1.call-start = ((), (), s32[]{:S(2)}) async-start(), calls=%async_computation.9 | async-start | bytes 1310720 | tf_op jit(solution)/shard_map/reduce_scatter | solution.py:196
  562.2 29.1 %collective-permute-start.59 = (bf16[400,2048]{1,0:T(8,128)(2,1)}, bf16[400,2048]{1,0:T(8,128)(2,1)}, u32[]{:S(2)}, u32[]{:S(2)}) collective-permute-start(bf16[400,2048]{1,0:T(8,128)(2,1)} %slice_bitcast_fusion), channel_id=1, source_target_pairs={{0,16},{16,0},{1,17},{17,1},{2,18},{18,2},{3,19},{19,3},{4,20},{20... | collective-permute-start | bytes 4915208 | tf_op jit(solution)/shard_map/ppermute | solution.py:48
  591.1 98.8 %reduce-scatter.15.cloned.1.call-start = ((), (), s32[]{:S(2)}) async-start(), calls=%async_computation.10 | async-start | bytes 1310720 | tf_op jit(solution)/shard_map/reduce_scatter | solution.py:196
  604.4 38.3 %collective-permute-start.60 = (bf16[4,128,1024]{2,1,0:T(8,128)(2,1)S(1)}, bf16[4,128,1024]{2,1,0:T(8,128)(2,1)S(1)}, u32[]{:S(2)}, u32[]{:S(2)}) collective-permute-start(bf16[4,128,1024]{2,1,0:T(8,128)(2,1)S(1)} %pad_maximum_fusion.12), channel_id=1, source_target_pairs={{0,1},{1,0},{2,3},{3,2},{4,5},{5,4},{6,7},{7,6},{8,9},{9,8},{10,11... | collective-permute-start | bytes 3145736 | tf_op jit(solution)/shard_map/ppermute | solution.py:52
  605.4 37.3 %collective-permute-start.61 = (bf16[4,128,1024]{2,1,0:T(8,128)(2,1)S(1)}, bf16[4,128,1024]{2,1,0:T(8,128)(2,1)S(1)}, u32[]{:S(2)}, u32[]{:S(2)}) collective-permute-start(bf16[4,128,1024]{2,1,0:T(8,128)(2,1)S(1)} %pad_maximum_fusion.13), channel_id=1, source_target_pairs={{0,2},{2,0},{1,3},{3,1},{4,6},{6,4},{5,7},{7,5},{8,10},{10,8},{9,1... | collective-permute-start | bytes 3145736 | tf_op jit(solution)/shard_map/ppermute | solution.py:52
  645.1 61.3 %reduce-scatter.17.cloned.1.call-start = ((), (), s32[]{:S(2)}) async-start(), calls=%async_computation.11 | async-start | bytes 1474560 | tf_op jit(solution)/shard_map/reduce_scatter | solution.py:196
  (142 other events, 1718.1 us)
Sparse Core Ops, SparseCore 0:
  22.7 30.5 all-gather.12
  55.4 32.1 all-gather.14
  89.8 26.9 all-gather.16
  118.8 27.4 all-gather.18
  160.3 26.8 all-gather.20
  261.2 26.2 all-gather.22
  463.0 25.8 reduce-scatter.6
  512.1 27.7 reduce-scatter.8
  559.4 26.5 reduce-scatter.10
  591.2 25.8 reduce-scatter.12
  645.2 25.6 reduce-scatter.14
  677.8 28.5 reduce-scatter.16

commit v4 on v3

--- a/solution.py
+++ b/solution.py
@@ -22,14 +22,12 @@
 X, Y, Z = DP[2], DP[1], DP[0]
 GATHERS = ((10, 0, 1), (20,), (30,), (11,), (21,), (31,))
 SCATTERS = ((31,), (21,), (11,), (30,), (20,), (10,))
-LATE_GATHERS = ()
-LATE_SCATTERS = ()
 ORDER = (
-    101, 102, 104, 105, 100, 101, 103, 100, 102, 101, 100, 101, 103, 100, 100, 10,
-    20, 102, 103, 102, 104, 103, 101, 30, 104, 102, 40, 104, 103, 105, 11, 21,
-    105, 105, 104, 31, 331, 105, 621, 631, 200, 641, 200, 651, 311, 202, 620, 200,
-    202, 321, 320, 201, 200, 204, 202, 630, 204, 640, 201, 202, 204, 330, 203, 650,
-    201, 204, 203, 310, 205, 203, 201, 205, 41, 203, 402, 205, 403, 500, 205,
+    100, 105, 102, 101, 103, 100, 103, 100, 103, 101, 104, 100, 100, 10, 101, 103,
+    102, 101, 104, 20, 102, 105, 104, 102, 101, 30, 104, 103, 102, 40, 11, 21,
+    105, 104, 105, 31, 105, 621, 331, 200, 631, 200, 321, 201, 641, 651, 201, 200,
+    620, 330, 201, 203, 311, 202, 203, 320, 630, 202, 204, 201, 640, 203, 650, 202,
+    200, 204, 310, 205, 41, 205, 203, 500, 202, 204, 205, 403, 204, 402, 205,
 )
 
 norm_epsilon = 1e-06
@@ -87,11 +85,6 @@
 
 def add_low(left, right):
     return (left.astype(wide) + right.astype(wide)).astype(low_type)
-
-
-def pick(array, index, axis):
-    last = array.shape[axis] - 1
-    return lax.dynamic_index_in_dim(array, jnp.clip(index, 0, last), axis, keepdims=False)
 
 
 def gather_flow(line, parts, me, keys, layers):
@@ -142,95 +135,24 @@
     yield
 
 
-def gather_flow_late(line, parts, me, keys, layers):
-    (part,) = line.sync(*parts)
-    half = part.shape[0] // 2
-    across = flip(part, X)
-    along = flip(part, Y)
+def scatter_flow(line, key, layers):
+    blocks = layers[key % 10].chip_grads[key // 10]
+    corner_low, corner_high, own, across, along = line.sync(*blocks)
+    from_across = flip(corner_low, X)
+    from_along = flip(corner_high, Y)
     yield
-    across, along = line.sync(across, along)
-    corner_low, corner_high = line.sync(along[:half], across[half:])
-    corner_low = flip(corner_low, X)
-    corner_high = flip(corner_high, Y)
-    yield
-    corner_low, corner_high = line.sync(corner_low, corner_high)
-    block = place_blocks([part, across, along, jnp.concatenate([corner_low, corner_high])], me, 0)
-    (block,) = line.sync(block)
-    full = lax.all_gather(block, Z, axis=0, tiled=False)
-    yield
-    (own,) = line.sync(full.reshape(LEVELS * SIDE, *part.shape))
-    other = swap_cores(own)
-    yield
-    layers[keys[0] % 10].weights[keys[0] // 10] = line.sync(own, other)
-    yield
-
-
-def scatter_flow(line, me, keys, layers):
-    half = LEVELS // 2
-    chips = [layers[key % 10].chip_grads[key // 10] for key in keys]
-    chips = [chip.reshape(LEVELS, SIDE, *chip.shape[1:]) for chip in chips]
-    counts = [chip.shape[2] for chip in chips]
-
-    def toward(relative):
-        to = jnp.bitwise_xor(me, relative)
-        return jnp.concatenate([pick(chip, to, 1) for chip in chips], axis=1)
-
-    chips = line.sync(*chips)
-    corner = toward(3)
-    from_across, from_along = line.sync(corner[:half], corner[half:])
-    from_across = flip(from_across, X)
-    from_along = flip(from_along, Y)
-    yield
-    from_across, from_along, *chips = line.sync(from_across, from_along, *chips)
-    along, across = toward(2), toward(1)
-    along = jnp.concatenate([add_low(along[:half], from_across), along[half:]])
-    across = jnp.concatenate([across[:half], add_low(across[half:], from_along)])
-    across, along = line.sync(across, along)
+    from_across, from_along = line.sync(from_across, from_along)
+    across, along = line.sync(*add_corners(across, along, from_across, from_along))
     got_across = flip(across, X)
     got_along = flip(along, Y)
-    own = toward(0)
     yield
-    got_across, got_along, own = line.sync(got_across, got_along, own)
+    got_across, got_along = line.sync(got_across, got_along)
     column = own.astype(wide) + got_across.astype(wide) + got_along.astype(wide)
     (column,) = line.sync(column.astype(low_type))
     total = lax.psum_scatter(column, Z, scatter_dimension=0, tiled=False)
     yield
     (total,) = line.sync(total)
-    total = total.astype(wide)
-    start = 0
-    for key, count in zip(keys, counts):
-        layers[key % 10].grads[key // 10] = total[start : start + count]
-        start += count
-    yield
-
-
-def scatter_flow_late(line, me, keys, layers):
-    chip = layers[keys[0] % 10].chip_grads[keys[0] // 10]
-    (chip,) = line.sync(chip.reshape(LEVELS, SIDE, *chip.shape[1:]))
-    half = chip.shape[2] // 2
-    block = lax.psum_scatter(chip, Z, scatter_dimension=0, tiled=False)
-    yield
-    (block,) = line.sync(block)
-
-    def toward(relative):
-        return pick(block, jnp.bitwise_xor(me, relative), 0)
-
-    corner = toward(3)
-    from_across, from_along = line.sync(corner[:half], corner[half:])
-    from_across = flip(from_across, X)
-    from_along = flip(from_along, Y)
-    yield
-    from_across, from_along = line.sync(from_across, from_along)
-    along, across = toward(2), toward(1)
-    along = jnp.concatenate([add_low(along[:half], from_across), along[half:]])
-    across = jnp.concatenate([across[:half], add_low(across[half:], from_along)])
-    across, along = line.sync(across, along)
-    got_across = flip(across, X)
-    got_along = flip(along, Y)
-    yield
-    got_across, got_along = line.sync(got_across, got_along)
-    total = toward(0).astype(wide) + got_across.astype(wide) + got_along.astype(wide)
-    layers[keys[0] % 10].grads[keys[0] // 10] = line.sync(total)[0]
+    layers[key % 10].grads[key // 10] = total.astype(wide)
     yield
 
 
@@ -641,7 +563,7 @@
     )(left, *weights, inputs, gain, middle)
 
 
-def grad_kernel(pairs, count, extra, *refs):
+def grad_kernel(pairs, count, extra, chip, *refs):
     out_ref = refs[-1]
     slabs, deep = out_ref.shape[:2]
 
@@ -657,9 +579,27 @@
         out_ref[:, pl.ds(row, rows), pl.ds(column, size)] = total
     if extra:
         out_ref[:, pl.ds(deep - SLABS, SLABS)] = refs[2 * count][...]
-
-
-def weight_grad(own, other, moving, pairs, extra=None):
+    if chip is None:
+        return
+    low_ref, high_ref, *sides = refs[-6:-1]
+    i = pl.program_id(0)
+    for relative, ref in enumerate(sides):
+        ref[0] = out_ref[jnp.bitwise_xor(chip[0], relative)]
+
+    @pl.when(i < LEVELS // 2)
+    def _():
+        low_ref[0] = out_ref[jnp.bitwise_xor(chip[0], 3)]
+
+    @pl.when(i >= LEVELS // 2)
+    def _():
+        high_ref[0] = out_ref[jnp.bitwise_xor(chip[0], 3)]
+
+
+def grad_whole_kernel(pairs, count, extra, *refs):
+    grad_kernel(pairs, count, extra, None, *refs)
+
+
+def weight_grad(chip, own, other, moving, pairs, extra=None):
     rows, depth = own[0][0].shape[-2:]
     width = 1024
     block = depth // STEPS
@@ -679,16 +619,61 @@
         deep += extra.shape[1]
         operands.append(extra)
         specs.append(pl.BlockSpec((slabs, *extra.shape[1:]), lambda i: (i, 0, 0)))
+    flops = cost(4 * rows * SLABS * deep * width, 4 * SLABS * deep * width)
+    if chip is None:
+        return pl.pallas_call(
+            functools.partial(grad_whole_kernel, pairs, len(own), extra is not None),
+            grid=(STEPS,),
+            in_specs=specs,
+            out_specs=pl.BlockSpec((slabs, deep, width), lambda i: (i, 0, 0)),
+            out_shape=jax.ShapeDtypeStruct((SLABS, deep, width), low_type),
+            cost_estimate=flops,
+            compiler_params=limits(),
+            name="grad",
+        )(*operands)
+    half = LEVELS // 2
+
+    def block(turn):
+        return pl.BlockSpec((1, deep, width), lambda i: (turn(i), 0, 0))
+
+    def shape(levels):
+        return jax.ShapeDtypeStruct((levels, deep, width), low_type)
+
     return pl.pallas_call(
         functools.partial(grad_kernel, pairs, len(own), extra is not None),
         grid=(STEPS,),
-        in_specs=specs,
-        out_specs=pl.BlockSpec((slabs, deep, width), lambda i: (i, 0, 0)),
-        out_shape=jax.ShapeDtypeStruct((SLABS, deep, width), low_type),
-        cost_estimate=cost(4 * rows * SLABS * deep * width, 4 * SLABS * deep * width),
+        in_specs=[pl.BlockSpec(memory_space=pltpu.SMEM)] + specs,
+        out_specs=[block(early(half)), block(late(half))] + [block(lambda i: i)] * 3,
+        out_shape=[shape(half)] * 2 + [shape(LEVELS)] * 3,
+        scratch_shapes=[pltpu.VMEM((slabs, deep, width), low_type)],
+        cost_estimate=flops,
         compiler_params=limits(),
         name="grad",
-    )(*operands)
+    )(chip, *operands)
+
+
+def add_kernel(across_ref, along_ref, from_across, from_along, across_out, along_out):
+    along_out[...] = add_low(along_ref[...], from_across[...])
+    across_out[...] = add_low(across_ref[...], from_along[...])
+
+
+def add_corners(across, along, from_across, from_along):
+    half, rows, width = from_across.shape
+
+    def block(first):
+        return pl.BlockSpec((1, rows, width), lambda i: (first + i, 0, 0))
+
+    return pl.pallas_call(
+        add_kernel,
+        grid=(half,),
+        in_specs=[block(half), block(0), block(0), block(0)],
+        out_specs=[block(half), block(0)],
+        out_shape=[jax.ShapeDtypeStruct(across.shape, low_type)] * 2,
+        input_output_aliases={0: 0, 1: 1},
+        cost_estimate=cost(half * rows * width, 12 * half * rows * width),
+        compiler_params=limits(),
+        name="add",
+    )(across, along, from_across, from_along)
 
 
 def adam_update(weight, grad, first, second, factor, rate, decay):
@@ -871,14 +856,19 @@
         if number == 0:
             layers[1].x = layer.block
 
+    chip = me.astype(jnp.int32).reshape(1) if tuned else None
+
+    def keep(layer, kind, grad):
+        layer.chip_grads[kind] = line.sync(*grad) if tuned else line.sync(grad)[0]
+
     def out_grad(number):
         layer = layers[number]
         active, upstream, *other = line.sync(
             layer.active, layer.dy, layer.active_other, layer.dy_other
         )
         plan = ((0, 1, 0, width, 0, hidden_width // 2 // SLABS, 0),)
-        grad = weight_grad([(active, 0), (upstream, 0)], [(o, 0) for o in other], 1, plan)
-        (layer.chip_grads[3],) = line.sync(grad)
+        grad = weight_grad(chip, [(active, 0), (upstream, 0)], [(o, 0) for o in other], 1, plan)
+        keep(layer, 3, grad)
 
     def in_grad(number):
         layer = layers[number]
@@ -886,8 +876,8 @@
             layer.hidden_two, layer.grad_pre, layer.kept_other, layer.grad_pre_other
         )
         plan = tuple((0, 1, b * width, width, b * deep, deep, 0) for b in range(2))
-        grad = weight_grad([(hidden, 0), (grad_pre, 0)], [(kept, 2), (other, 0)], 1, plan)
-        (layer.chip_grads[2],) = line.sync(grad)
+        grad = weight_grad(chip, [(hidden, 0), (grad_pre, 0)], [(kept, 2), (other, 0)], 1, plan)
+        keep(layer, 2, grad)
 
     def first_grad(number):
         layer = layers[number]
@@ -905,13 +895,14 @@
             (1, 2, half_qkv, half, deep, deep, half),
         )
         grad = weight_grad(
+            chip,
             [(hidden, 0), (mixed, 0), (slopes, 0)],
             [(kept, 0), (kept, 1), (other, 0)],
             2,
             plan,
             extra,
         )
-        (layer.chip_grads[1],) = line.sync(grad)
+        keep(layer, 1, grad)
 
     def backward_two(number):
         layer = layers[number]
@@ -975,11 +966,30 @@
         pair = line.sync(layers[0].grads[kind], layers[1].grads[kind])
         squares[:] = line.sync(squares[0] + sum(jnp.sum(part * part) for part in pair))
 
+    def woven(pair, groups):
+        rows = pair[0].shape[0]
+        return jnp.stack([p.reshape(rows, groups, -1) for p in pair], axis=2).reshape(rows, -1)
+
     def join_layers(kind):
         pair = line.sync(layers[0].grads[kind], layers[1].grads[kind])
         got = swap_cores(jnp.where(first, pair[1], pair[0]))
         mine = jnp.where(first, pair[0], pair[1])
-        joined[kind] = jnp.where(first, mine, got), jnp.where(first, got, mine)
+        pair = jnp.where(first, mine, got), jnp.where(first, got, mine)
+        if kind in (0, 3):
+            shards = [jnp.concatenate(pair, axis=0)]
+        elif kind == 2:
+            shards = [woven([unpack(p) if tuned else p for p in pair], count_dp)]
+        else:
+            thin = [p[2 * deep : 2 * deep + half_vectors, :deep] for p in pair]
+            if tuned:
+                pair = [unpack(p[: 2 * deep]) for p in pair]
+            shards = [
+                woven([p[:, :half_qkv] for p in pair], 3),
+                jnp.concatenate([p[:, half_qkv:] for p in pair], axis=1),
+            ]
+            if tuned:
+                shards.append(jnp.concatenate(thin, axis=0))
+        joined[kind] = line.sync(*shards)
 
     def own_tokens(zero, one):
         zero, one = line.sync(zero, one)
@@ -1009,8 +1019,7 @@
     for index, batch in enumerate(GATHERS):
         values = [parts[key % 10][key // 10] for key in batch]
         if tuned:
-            flow = gather_flow_late if index in LATE_GATHERS else gather_flow
-            flows[100 + index] = flow(line, values, me, batch, layers)
+            flows[100 + index] = gather_flow(line, values, me, batch, layers)
             continue
         for key, value in zip(batch, values):
             layer = layers[key % 10]
@@ -1022,8 +1031,7 @@
             layer.weights[key // 10] = (mine, swap_cores(mine))
     if tuned:
         for index, batch in enumerate(SCATTERS):
-            flow = scatter_flow_late if index in LATE_SCATTERS else scatter_flow
-            flows[200 + index] = flow(line, me, batch, layers)
+            flows[200 + index] = scatter_flow(line, batch[0], layers)
     for event in ORDER:
         if event in flows:
             next(flows[event], None)
@@ -1057,23 +1065,8 @@
     for kind in kinds:
         join_layers(kind)
 
-    def woven(pair, groups):
-        rows = pair[0].shape[0]
-        return jnp.stack([p.reshape(rows, groups, -1) for p in pair], axis=2).reshape(rows, -1)
-
-    one, inner, outer = [joined[kind] for kind in (1, 2, 3)]
-    if tuned:
-        thin = [p[2 * deep : 2 * deep + half_vectors, :deep] for p in one]
-        one, inner = [tuple(unpack(p[: 2 * deep]) for p in pair) for pair in (one, inner)]
-    else:
-        thin = joined[0]
-    shards = (
-        woven([p[:, :half_qkv] for p in one], 3),
-        jnp.concatenate([p[:, half_qkv:] for p in one], axis=1),
-        woven(inner, count_dp),
-        jnp.concatenate(outer, axis=0),
-        jnp.concatenate(thin, axis=0),
-    )
+    thin = joined[1][2] if tuned else joined[0][0]
+    shards = (*joined[1][:2], *joined[2], *joined[3], thin)
     global_sum, *shards = line.sync(global_sum, *shards)
     grad_norm = jnp.sqrt(global_sum)
     factor = clip_norm / jnp.maximum(grad_norm, clip_norm)

time: 784 us -> 748 us (0.954)
  other arithmetic: 87.9 us -> 69 us
  waiting for transfers between devices: 227 us -> 212 us
  Pallas kernels: 206 us -> 217 us
  local copies, waits for them, and re-layouts: 158 us -> 147 us
    all_gather x6, waiting for transfers between devices: 85.4 us -> 63.3 us  [gather_flow(): column = lax.all_gather(part, Z, axis=0, tiled=False)]
    slice x16 -> x4, local copies, waits for them, and re-layouts: 19.1 us -> 0.68 us  [the longest x2 0.67 us: join_layers(): p[:, half_qkv:]]
    unnamed x183 -> x225, local copies, waits for them, and re-layouts: 20.9 us -> 37.9 us
    ppermute x50, waiting for transfers between devices: 116 us -> 128 us  [flip(): return lax.ppermute(x, axis, [(0, 1), (1, 0)])]
    pallas_call x0 -> x6, Pallas kernels: none -> 11.3 us  [add_corners(): pl.pallas_call(add_kernel, grid=(half,), in_specs=[block(half), block(0),...]
    convert_element_type x12 -> x6, other arithmetic: 15.4 us -> 4.21 us  [scatter_flow(): layers[key % 10].grads[key // 10] = total.astype(wide)]
    squeeze x6 -> x0, local copies, waits for them, and re-layouts: 10.9 us -> none  [pick(): lax.dynamic_index_in_dim(array, jnp.clip(index, 0, last), axis, keepdims=...]
    concatenate x15 -> x3, other arithmetic: 11.3 us -> 1.07 us  [the longest x1 1.04 us: join_layers(): shards = [jnp.concatenate(pair, axis=0)]]
  transfers between devices with their start and end apart: 88 -> 88, of which waited for: 41 -> 39; matrix products, arithmetic and copies ran while one was open for 25% -> 19% of each run, Pallas kernels for 22% -> 29%
where the time goes in v4:
time: 748 us; the launch traced here: 736 us
  Pallas kernels  217 us (29%)
  waiting for transfers between devices  212 us (28%)
  local copies, waits for them, and re-layouts  147 us (20%)
  other arithmetic  69 us (9%)
  starting transfers between devices  65.8 us (9%)
  between operations  25.3 us (3%)
    ppermute x50, waiting for transfers between devices, flip(): return lax.ppermute(x, axis, [(0, 1), (1, 0)])  128 us
    all_gather x6, waiting for transfers between devices, gather_flow(): column = lax.all_gather(part, Z, axis=0, tiled=False)  63.3 us
    ppermute x50, starting transfers between devices, flip(): return lax.ppermute(x, axis, [(0, 1), (1, 0)])  56.6 us
    pallas_call x6, Pallas kernels, weight_grad(): pl.pallas_call(functools.partial(grad_kernel, pairs, len(own), extra is n...  50.3 us
    pallas_call x6, Pallas kernels, project(): pl.pallas_call(functools.partial(project_kernel, smooth, count), grid=(2...  43.2 us
    unnamed x225, local copies, waits for them, and re-layouts  37.9 us
    pallas_call x2, Pallas kernels, attend_back(): pl.pallas_call(attend_back_kernel, grid=(groups,), in_specs=[third_at(thi...  29 us
    dynamic_update_slice x18, local copies, waits for them, and re-layouts, place_blocks(): full = lax.dynamic_update_slice(full, jnp.expand_dims(block, axis), start)  28.6 us
  transfers between devices with their start and end apart: 88, of which 39 were waited for; matrix products, arithmetic and copies ran while one was open for 19% of the time, Pallas kernels for 29%

profile of v4, /device:TPU:0, one launch (start us, length us, event | category | flops | bytes accessed | tf_op | source)
XLA Modules:
  0.0 736.0 jit_solution(10516085734504860412)
XLA Ops:
  27.2 34.5 %all-gather.13.cloned.1.call-done = bf16[640,1024]{1,0:T(8,128)(2,1)} async-done(((bf16[160,1024]{1,0:T(8,128)(2,1)}), bf16[640,1024]{1,0:T(8,128)(2,1)}) %all-gather.13.cloned.1.call-update) | async-done | bytes 1310736 | tf_op jit(solution)/shard_map/all_gather | solution.py:99
  64.6 26.2 %all-gather.15.cloned.1.call-done = bf16[512,1024]{1,0:T(8,128)(2,1)} async-done(((bf16[128,1024]{1,0:T(8,128)(2,1)}), bf16[512,1024]{1,0:T(8,128)(2,1)}) %all-gather.15.cloned.1.call-update) | async-done | bytes 1048592 | tf_op jit(solution)/shard_map/all_gather | solution.py:99
  100.4 16.7 %collective-permute-done.4 = bf16[4,128,1024]{2,1,0:T(8,128)(2,1)} collective-permute-done((bf16[4,128,1024]{2,1,0:T(8,128)(2,1)}, bf16[4,128,1024]{2,1,0:T(8,128)(2,1)}, u32[]{:S(2)}, u32[]{:S(2)}) %collective-permute-start.4) | collective-permute-done | bytes 1048608 | tf_op jit(solution)/shard_map/ppermute | solution.py:50
  145.0 7.2 project.6
  152.2 10.4 %collective-permute-done.9 = bf16[4,128,1024]{2,1,0:T(8,128)(2,1)} collective-permute-done((bf16[4,128,1024]{2,1,0:T(8,128)(2,1)}, bf16[4,128,1024]{2,1,0:T(8,128)(2,1)}, u32[]{:S(2)}, u32[]{:S(2)}) %collective-permute-start.9) | collective-permute-done | bytes 1048608 | tf_op jit(solution)/shard_map/ppermute | solution.py:50
  194.6 6.2 attend.2
  221.1 8.5 %collective-permute-done.17 = bf16[4,128,1024]{2,1,0:T(8,128)(2,1)} collective-permute-done((bf16[4,128,1024]{2,1,0:T(8,128)(2,1)}, bf16[4,128,1024]{2,1,0:T(8,128)(2,1)}, u32[]{:S(2)}, u32[]{:S(2)}) %collective-permute-start.17) | collective-permute-done | bytes 1048608 | tf_op jit(solution)/shard_map/ppermute | solution.py:50
  247.7 11.3 %project.8 = (bf16[2,400,2048]{2,1,0:T(8,128)(2,1)S(1)}, bf16[2,400,2048]{2,1,0:T(8,128)(2,1)}) custom-call(bf16[400,1024]{1,0:T(8,128)(2,1)S(1)} %add_convert_fusion.7.x_ref.refs_0_, bf16[16,128,1024]{2,1,0:T(8,128)(2,1)} %bitcast.41.here_ref.refs_1_, bf16[16,128,1024]{2,1,0:T(8,128)(2,1)} %collective-permute-done.20.there_ref.refs_2_, ...), custom_call_target="tpu_custom_call" | custom-call | flops 3355443200 | bytes 8388608 | tf_op jit(solution)/shard_map/project/pallas_call | solution.py:349
  263.7 12.2 %collective-permute-done.22 = bf16[2,128,1024]{2,1,0:T(8,128)(2,1)} collective-permute-done((bf16[2,128,1024]{2,1,0:T(8,128)(2,1)}, bf16[2,128,1024]{2,1,0:T(8,128)(2,1)}, u32[]{:S(2)}, u32[]{:S(2)}) %collective-permute-start.22) | collective-permute-done | bytes 524320 | tf_op jit(solution)/shard_map/ppermute | solution.py:50
  283.3 6.4 output.2.inputs
  290.7 7.1 project.9
  297.8 6.2 attend.3
  328.8 11.2 %project.11 = (bf16[2,400,2048]{2,1,0:T(8,128)(2,1)S(1)}, bf16[2,400,2048]{2,1,0:T(8,128)(2,1)}) custom-call(bf16[400,1024]{1,0:T(8,128)(2,1)S(1)} %copy-done.36, bf16[16,128,1024]{2,1,0:T(8,128)(2,1)} %bitcast.79.here_ref.refs_1_, bf16[16,128,1024]{2,1,0:T(8,128)(2,1)} %collective-permute-done.29.there_ref.refs_2_, f32[2,1,2048]{2,1,0:T(1,128)S(1)} %pad_maximum_fusion.14.b_ref), custom_call_target="tpu_custom_call" | custom-call | flops 3355443200 | bytes 8388608 | tf_op jit(solution)/shard_map/project/pallas_call | solution.py:349
  344.9 9.8 %active.2 = (bf16[2,400,2048]{2,1,0:T(8,128)(2,1)S(1)}, f32[2,1,2048]{2,1,0:T(1,128)S(1)}) custom-call(bf16[400,1024]{1,0:T(8,128)(2,1)S(1)} %get-tuple-element.746.up_ref.refs_1_.refs_5_, bf16[16,128,1024]{2,1,0:T(8,128)(2,1)} %bitcast.106.w_here, bf16[16,128,1024]{2,1,0:T(8,128)(2,1)} %collective-permute-done.33.w_there, ...), custom_call_target="tpu_custom_call" | custom-call | flops 3355443200 | bytes 12582912 | tf_op jit(solution)/shard_map/active/pallas_call | solution.py:415
  357.1 7.8 %grad.6 = (bf16[2,128,1024]{2,1,0:T(8,128)(2,1)}, bf16[2,128,1024]{2,1,0:T(8,128)(2,1)}, bf16[4,128,1024]{2,1,0:T(8,128)(2,1)S(1)}, bf16[4,128,1024]{2,1,0:T(8,128)(2,1)}, bf16[4,128,1024]{2,1,0:T(8,128)(2,1)}) custom-call(s32[1]{0:T(128)} %bitcast.112.chip, bf16[2,400,2048]{2,1,0:T(8,128)(2,1)} %copy-done.26, ...), custom_call_target="tpu_custom_call" | custom-call | flops 3355443200 | bytes 8388608 | tf_op jit(solution)/shard_map/grad/pallas_call | solution.py:642
  367.8 10.7 %middle.2 = (f32[400,1024]{1,0:T(8,128)S(1)}, bf16[2,400,512]{2,1,0:T(8,128)(2,1)S(1)}, bf16[2,400,512]{2,1,0:T(8,128)(2,1)S(1)}, f32[8,1024]{1,0:T(8,128)S(1)}) custom-call(s32[1]{0:T(128)} %bitcast.113.place, bf16[2,400,2048]{2,1,0:T(8,128)(2,1)} %copy-done.32, bf16[16,128,1024]{2,1,0:T(8,128)(2,1)} %bitcast.79.here_ref.refs_1_, ...), custom_call_target="tpu_custom_call" | custom-call | flops 4194304000 | bytes 8388608 | tf_op jit(solution)/shard_map/middle/pallas_call | solution.py:488
  387.6 8.9 %grad.7 = (bf16[2,128,1024]{2,1,0:T(8,128)(2,1)}, bf16[2,128,1024]{2,1,0:T(8,128)(2,1)}, bf16[4,128,1024]{2,1,0:T(8,128)(2,1)S(1)}, bf16[4,128,1024]{2,1,0:T(8,128)(2,1)}, bf16[4,128,1024]{2,1,0:T(8,128)(2,1)}) custom-call(s32[1]{0:T(128)} %bitcast.112.chip, bf16[400,1024]{1,0:T(8,128)(2,1)S(1)} %copy-done.37, bf16[2,400,2048]{2,1,0:T(8,128)(2,1)} %copy-done.32, ...), custom_call_target="tpu_custom_call" | custom-call | flops 3355443200 | bytes 8388608 | tf_op jit(solution)/shard_map/grad/pallas_call | solution.py:642
  397.4 14.5 %attend_back.2 = bf16[4,200,2048]{2,1,0:T(8,128)(2,1)} custom-call(bf16[4,200,1536]{2,1,0:T(8,128)(2,1)S(1)} %bitcast.451, bf16[4,200,1536]{2,1,0:T(8,128)(2,1)S(1)} %bitcast.452, bf16[4,200,1536]{2,1,0:T(8,128)(2,1)S(1)} %bitcast.453, bf16[4,200,512]{2,1,0:T(8,128)(2,1)S(1)} %bitcast.461, bf16[4,200,512]{2,1,0:T(8,128)(2,1)S(1)} %bitcast.460), custom_call_target="tpu_custom_call" | custom-call | flops 1638400000 | bytes 5734400 | tf_op jit(solution)/shard_map/attend_back/pallas_call | solution.py:283
  413.8 8.5 %entry.2 = (bf16[400,1024]{1,0:T(8,128)(2,1)S(1)}, f32[8,1024]{1,0:T(8,128)S(1)}, f32[2,1,1536]{2,1,0:T(1,128)S(1)}) custom-call(bf16[2,400,2048]{2,1,0:T(8,128)(2,1)} %bitcast.473, bf16[16,128,1024]{2,1,0:T(8,128)(2,1)} %bitcast.35.here_ref.refs_6_.w_here, bf16[16,128,1024]{2,1,0:T(8,128)(2,1)} %collective-permute-done.24.there_ref.refs_7_.w_there, ...), custom_call_target="tpu_custom_call" | custom-call | flops 2516582400 | bytes 6291456 | tf_op jit(solution)/shard_map/entry/pallas_call | solution.py:538
  435.4 9.6 %active.3 = (bf16[2,400,2048]{2,1,0:T(8,128)(2,1)S(1)}, f32[2,1,2048]{2,1,0:T(1,128)S(1)}) custom-call(bf16[400,1024]{1,0:T(8,128)(2,1)S(1)} %copy-done.13, bf16[16,128,1024]{2,1,0:T(8,128)(2,1)} %bitcast.72.w_here, bf16[16,128,1024]{2,1,0:T(8,128)(2,1)} %collective-permute-done.25.w_there, bf16[2,400,2048]{2,1,0:T(8,128)(2,1)} %get-tuple-element.815.slope_ref), custom_call_target="tpu_custom_call" | custom-call | flops 3355443200 | bytes 12582912 | tf_op jit(solution)/shard_map/active/pallas_call | solution.py:415
  446.7 7.8 %grad.8 = (bf16[2,128,1024]{2,1,0:T(8,128)(2,1)S(1)}, bf16[2,128,1024]{2,1,0:T(8,128)(2,1)S(1)}, bf16[4,128,1024]{2,1,0:T(8,128)(2,1)S(1)}, bf16[4,128,1024]{2,1,0:T(8,128)(2,1)}, bf16[4,128,1024]{2,1,0:T(8,128)(2,1)}) custom-call(s32[1]{0:T(128)} %bitcast.112.chip, bf16[2,400,2048]{2,1,0:T(8,128)(2,1)} %copy-done.28, bf16[400,1024]{1,0:T(8,128)(2,1)S(1)} %copy-done.13, ...), custom_call_target="tpu_custom_call" | custom-call | flops 3355443200 | bytes 8388608 | tf_op jit(solution)/shard_map/grad/pallas_call | solution.py:642
  472.1 8.7 %grad.9 = (bf16[2,144,1024]{2,1,0:T(8,128)(2,1)S(1)}, bf16[2,144,1024]{2,1,0:T(8,128)(2,1)S(1)}, bf16[4,144,1024]{2,1,0:T(8,128)(2,1)S(1)}, bf16[4,144,1024]{2,1,0:T(8,128)(2,1)}, bf16[4,144,1024]{2,1,0:T(8,128)(2,1)}) custom-call(s32[1]{0:T(128)} %bitcast.112.chip, bf16[400,1024]{1,0:T(8,128)(2,1)S(1)} %copy-done.23, bf16[400,1024]{1,0:T(8,128)(2,1)S(1)} %copy-done.25, ...), custom_call_target="tpu_custom_call" | custom-call | flops 3774873600 | bytes 9437184 | tf_op jit(solution)/shard_map/grad/pallas_call | solution.py:642
  488.4 8.4 %grad.10 = (bf16[2,128,1024]{2,1,0:T(8,128)(2,1)S(1)}, bf16[2,128,1024]{2,1,0:T(8,128)(2,1)}, bf16[4,128,1024]{2,1,0:T(8,128)(2,1)S(1)}, bf16[4,128,1024]{2,1,0:T(8,128)(2,1)S(1)}, bf16[4,128,1024]{2,1,0:T(8,128)(2,1)S(1)}) custom-call(s32[1]{0:T(128)} %bitcast.112.chip, bf16[400,1024]{1,0:T(8,128)(2,1)S(1)} %copy-done.34, bf16[2,400,2048]{2,1,0:T(8,128)(2,1)} %copy-done.30, ...), custom_call_target="tpu_custom_call" | custom-call | flops 3355443200 | bytes 8388608 | tf_op jit(solution)/shard_map/grad/pallas_call | solution.py:642
  498.9 10.4 %middle.3 = (f32[400,1024]{1,0:T(8,128)S(1)}, bf16[2,400,512]{2,1,0:T(8,128)(2,1)S(1)}, bf16[2,400,512]{2,1,0:T(8,128)(2,1)S(1)}, f32[8,1024]{1,0:T(8,128)S(1)}) custom-call(s32[1]{0:T(128)} %bitcast.113.place, bf16[2,400,2048]{2,1,0:T(8,128)(2,1)} %copy-done.30, bf16[16,128,1024]{2,1,0:T(8,128)(2,1)} %bitcast.41.here_ref.refs_1_, ...), custom_call_target="tpu_custom_call" | custom-call | flops 4194304000 | bytes 8388608 | tf_op jit(solution)/shard_map/middle/pallas_call | solution.py:488
  511.4 10.1 %collective-permute-done.50.from_across = bf16[2,144,1024]{2,1,0:T(8,128)(2,1)S(1)} collective-permute-done((bf16[2,144,1024]{2,1,0:T(8,128)(2,1)S(1)}, bf16[2,144,1024]{2,1,0:T(8,128)(2,1)S(1)}, u32[]{:S(2)}, u32[]{:S(2)}) %collective-permute-start.50) | collective-permute-done | bytes 589856 | tf_op jit(solution)/shard_map/ppermute | solution.py:50
  529.9 14.5 %attend_back.3 = bf16[4,200,2048]{2,1,0:T(8,128)(2,1)} custom-call(bf16[4,200,1536]{2,1,0:T(8,128)(2,1)S(1)} %bitcast.445, bf16[4,200,1536]{2,1,0:T(8,128)(2,1)S(1)} %bitcast.446, bf16[4,200,1536]{2,1,0:T(8,128)(2,1)S(1)} %bitcast.447, bf16[4,200,512]{2,1,0:T(8,128)(2,1)S(1)} %bitcast.463, bf16[4,200,512]{2,1,0:T(8,128)(2,1)S(1)} %bitcast.462), custom_call_target="tpu_custom_call" | custom-call | flops 1638400000 | bytes 5734400 | tf_op jit(solution)/shard_map/attend_back/pallas_call | solution.py:283
  548.6 8.8 %entry.3 = (bf16[400,1024]{1,0:T(8,128)(2,1)S(1)}, f32[8,1024]{1,0:T(8,128)S(1)}, f32[2,1,1536]{2,1,0:T(1,128)S(1)}) custom-call(bf16[2,400,2048]{2,1,0:T(8,128)(2,1)} %bitcast.470, bf16[16,160,1024]{2,1,0:T(8,128)(2,1)} %bitcast.469, bf16[16,160,1024]{2,1,0:T(8,128)(2,1)} %collective-permute-done.7.there_ref.refs_7_.w_there, ...), custom_call_target="tpu_custom_call" | custom-call | flops 2516582400 | bytes 6291456 | tf_op jit(solution)/shard_map/entry/pallas_call | solution.py:538
  567.5 20.2 %collective-permute-done.65 = bf16[4,128,1024]{2,1,0:T(8,128)(2,1)S(1)} collective-permute-done((bf16[4,128,1024]{2,1,0:T(8,128)(2,1)S(1)}, bf16[4,128,1024]{2,1,0:T(8,128)(2,1)S(1)}, u32[]{:S(2)}, u32[]{:S(2)}) %collective-permute-start.65) | collective-permute-done | bytes 1048608 | tf_op jit(solution)/shard_map/ppermute | solution.py:50
  597.9 8.7 %grad.11 = (bf16[2,144,1024]{2,1,0:T(8,128)(2,1)S(1)}, bf16[2,144,1024]{2,1,0:T(8,128)(2,1)S(1)}, bf16[4,144,1024]{2,1,0:T(8,128)(2,1)S(1)}, bf16[4,144,1024]{2,1,0:T(8,128)(2,1)S(1)}, bf16[4,144,1024]{2,1,0:T(8,128)(2,1)}) custom-call(s32[1]{0:T(128)} %bitcast.112.chip, bf16[400,1024]{1,0:T(8,128)(2,1)S(1)} %copy-done.19, bf16[400,1024]{1,0:T(8,128)(2,1)S(1)} %copy-done.21, ...), custom_call_target="tpu_custom_call" | custom-call | flops 3774873600 | bytes 9437184 | tf_op jit(solution)/shard_map/grad/pallas_call | solution.py:642
  609.1 13.0 %collective-permute-done.60.from_across = bf16[2,144,1024]{2,1,0:T(8,128)(2,1)S(1)} collective-permute-done((bf16[2,144,1024]{2,1,0:T(8,128)(2,1)S(1)}, bf16[2,144,1024]{2,1,0:T(8,128)(2,1)S(1)}, u32[]{:S(2)}, u32[]{:S(2)}) %collective-permute-start.60) | collective-permute-done | bytes 589856 | tf_op jit(solution)/shard_map/ppermute | solution.py:50
  626.7 6.7 output.3
  634.7 16.7 %collective-permute-done.67 = bf16[4,144,1024]{2,1,0:T(8,128)(2,1)S(1)} collective-permute-done((bf16[4,144,1024]{2,1,0:T(8,128)(2,1)S(1)}, bf16[4,144,1024]{2,1,0:T(8,128)(2,1)S(1)}, u32[]{:S(2)}, u32[]{:S(2)}) %collective-permute-start.67) | collective-permute-done | bytes 1179680 | tf_op jit(solution)/shard_map/ppermute | solution.py:50
  (642 shorter events, 342.6 us)
Async XLA Ops:
  7.2 54.4 %all-gather.13.cloned.1.call-start = ((), (), s32[]{:S(2)}) async-start(), calls=%async_computation.12 | async-start | bytes 1638400 | tf_op jit(solution)/shard_map/all_gather | solution.py:99
  26.1 64.6 %all-gather.15.cloned.1.call-start = ((), (), s32[]{:S(2)}) async-start(), calls=%async_computation.13 | async-start | bytes 1310720 | tf_op jit(solution)/shard_map/all_gather | solution.py:99
  27.1 103.4 %all-gather.17.cloned.1.call-start = ((), (), s32[]{:S(2)}) async-start(), calls=%async_computation.14 | async-start | bytes 1310720 | tf_op jit(solution)/shard_map/all_gather | solution.py:99
  93.7 88.2 %all-gather.19.cloned.1.call-start = ((), (), s32[]{:S(2)}) async-start(), calls=%async_computation.15 | async-start | bytes 1310720 | tf_op jit(solution)/shard_map/all_gather | solution.py:99
  96.6 34.4 %collective-permute-start.5 = (bf16[2,160,1024]{2,1,0:T(8,128)(2,1)}, bf16[2,160,1024]{2,1,0:T(8,128)(2,1)}, u32[]{:S(2)}, u32[]{:S(2)}) collective-permute-start(bf16[2,160,1024]{2,1,0:T(8,128)(2,1)} %slice.389), channel_id=1, source_target_pairs={{0,1},{1,0},{2,3},{3,2},{4,5},{5,4},{6,7},{7,6},{8,9},{9,8},{10,11... | collective-permute-start | bytes 1966088 | tf_op jit(solution)/shard_map/ppermute | solution.py:50
  135.0 56.6 %all-gather.21.cloned.1.call-start = ((), (), s32[]{:S(2)}) async-start(), calls=%async_computation.16 | async-start | bytes 1310720 | tf_op jit(solution)/shard_map/all_gather | solution.py:99
  135.6 85.5 %all-gather.23.cloned.1.call-start = ((), (), s32[]{:S(2)}) async-start(), calls=%async_computation.17 | async-start | bytes 1310720 | tf_op jit(solution)/shard_map/all_gather | solution.py:99
  136.2 391.4 %reduce-scatter.7.cloned.1.call-start = ((), (), s32[]{:S(2)}) async-start(), calls=%async_computation.6 | async-start | bytes 1310720 | tf_op jit(solution)/shard_map/reduce_scatter | solution.py:152
  138.4 39.8 %collective-permute-start.10 = (bf16[2,128,1024]{2,1,0:T(8,128)(2,1)}, bf16[2,128,1024]{2,1,0:T(8,128)(2,1)}, u32[]{:S(2)}, u32[]{:S(2)}) collective-permute-start(bf16[2,128,1024]{2,1,0:T(8,128)(2,1)} %slice.391), channel_id=1, source_target_pairs={{0,1},{1,0},{2,3},{3,2},{4,5},{5,4},{6,7},{7,6},{8,9},{9,8},{10,11... | collective-permute-start | bytes 1572872 | tf_op jit(solution)/shard_map/ppermute | solution.py:50
  138.9 39.2 %collective-permute-start.11 = (bf16[2,128,1024]{2,1,0:T(8,128)(2,1)}, bf16[2,128,1024]{2,1,0:T(8,128)(2,1)}, u32[]{:S(2)}, u32[]{:S(2)}) collective-permute-start(bf16[2,128,1024]{2,1,0:T(8,128)(2,1)} %slice.392), channel_id=1, source_target_pairs={{0,2},{2,0},{1,3},{3,1},{4,6},{6,4},{5,7},{7,5},{8,10},{10,8},{9,1... | collective-permute-start | bytes 1572872 | tf_op jit(solution)/shard_map/ppermute | solution.py:50
  191.6 38.0 %collective-permute-start.17 = (bf16[4,128,1024]{2,1,0:T(8,128)(2,1)}, bf16[4,128,1024]{2,1,0:T(8,128)(2,1)}, u32[]{:S(2)}, u32[]{:S(2)}) collective-permute-start(bf16[4,128,1024]{2,1,0:T(8,128)(2,1)} %bitcast.496), channel_id=1, source_target_pairs={{0,2},{2,0},{1,3},{3,1},{4,6},{6,4},{5,7},{7,5},{8,10},{10,8},{9,1... | collective-permute-start | bytes 3145736 | tf_op jit(solution)/shard_map/ppermute | solution.py:50
  193.1 38.0 %collective-permute-start.16 = (bf16[4,128,1024]{2,1,0:T(8,128)(2,1)}, bf16[4,128,1024]{2,1,0:T(8,128)(2,1)}, u32[]{:S(2)}, u32[]{:S(2)}) collective-permute-start(bf16[4,128,1024]{2,1,0:T(8,128)(2,1)} %bitcast.497), channel_id=1, source_target_pairs={{0,1},{1,0},{2,3},{3,2},{4,5},{5,4},{6,7},{7,6},{8,9},{9,8},{10,11... | collective-permute-start | bytes 3145736 | tf_op jit(solution)/shard_map/ppermute | solution.py:50
  204.7 41.6 %collective-permute-start.20 = (bf16[16,128,1024]{2,1,0:T(8,128)(2,1)}, bf16[16,128,1024]{2,1,0:T(8,128)(2,1)}, u32[]{:S(2)}, u32[]{:S(2)}) collective-permute-start(bf16[16,128,1024]{2,1,0:T(8,128)(2,1)} %bitcast.41.here_ref.refs_1_), channel_id=1, source_target_pairs={{0,16},{16,0},{1,17},{17,1},{2,18},{18,2},{3,19},{19,3},{4,20},{20... | collective-permute-start | bytes 12582920 | tf_op jit(solution)/shard_map/ppermute | solution.py:46
  208.3 73.0 %collective-permute-start.24 = (bf16[16,128,1024]{2,1,0:T(8,128)(2,1)}, bf16[16,128,1024]{2,1,0:T(8,128)(2,1)}, u32[]{:S(2)}, u32[]{:S(2)}) collective-permute-start(bf16[16,128,1024]{2,1,0:T(8,128)(2,1)} %bitcast.35.here_ref.refs_6_.w_here), channel_id=1, source_target_pairs={{0,16},{16,0},{1,17},{17,1},{2,18},{18,2},{3,19},{19,3},{4,20},{20... | collective-permute-start | bytes 12582920 | tf_op jit(solution)/shard_map/ppermute | solution.py:46
  208.8 37.5 %collective-permute-start.21 = (bf16[3,400,1024]{2,1,0:T(8,128)(2,1)}, bf16[3,400,1024]{2,1,0:T(8,128)(2,1)}, u32[]{:S(2)}, u32[]{:S(2)}) collective-permute-start(bf16[3,400,1024]{2,1,0:T(8,128)(2,1)} %pad_maximum_fusion), channel_id=1, source_target_pairs={{0,16},{16,0},{1,17},{17,1},{2,18},{18,2},{3,19},{19,3},{4,20},{20... | collective-permute-start | bytes 7372808 | tf_op jit(solution)/shard_map/ppermute | solution.py:46
  246.3 35.1 %collective-permute-start.25 = (bf16[16,128,1024]{2,1,0:T(8,128)(2,1)}, bf16[16,128,1024]{2,1,0:T(8,128)(2,1)}, u32[]{:S(2)}, u32[]{:S(2)}) collective-permute-start(bf16[16,128,1024]{2,1,0:T(8,128)(2,1)} %bitcast.72.w_here), channel_id=1, source_target_pairs={{0,16},{16,0},{1,17},{17,1},{2,18},{18,2},{3,19},{19,3},{4,20},{20... | collective-permute-start | bytes 12582920 | tf_op jit(solution)/shard_map/ppermute | solution.py:46
  275.9 34.9 %collective-permute-start.28 = (bf16[4,128,1024]{2,1,0:T(8,128)(2,1)}, bf16[4,128,1024]{2,1,0:T(8,128)(2,1)S(1)}, u32[]{:S(2)}, u32[]{:S(2)}) collective-permute-start(bf16[4,128,1024]{2,1,0:T(8,128)(2,1)} %bitcast.61), channel_id=1, source_target_pairs={{0,2},{2,0},{1,3},{3,1},{4,6},{6,4},{5,7},{7,5},{8,10},{10,8},{9,1... | collective-permute-start | bytes 3145736 | tf_op jit(solution)/shard_map/ppermute | solution.py:50
  276.5 34.4 %collective-permute-start.27 = (bf16[4,128,1024]{2,1,0:T(8,128)(2,1)}, bf16[4,128,1024]{2,1,0:T(8,128)(2,1)S(1)}, u32[]{:S(2)}, u32[]{:S(2)}) collective-permute-start(bf16[4,128,1024]{2,1,0:T(8,128)(2,1)} %bitcast.61), channel_id=1, source_target_pairs={{0,1},{1,0},{2,3},{3,2},{4,5},{5,4},{6,7},{7,6},{8,9},{9,8},{10,11... | collective-permute-start | bytes 3145736 | tf_op jit(solution)/shard_map/ppermute | solution.py:50
  281.3 39.0 %collective-permute-start.29 = (bf16[16,128,1024]{2,1,0:T(8,128)(2,1)}, bf16[16,128,1024]{2,1,0:T(8,128)(2,1)}, u32[]{:S(2)}, u32[]{:S(2)}) collective-permute-start(bf16[16,128,1024]{2,1,0:T(8,128)(2,1)} %bitcast.79.here_ref.refs_1_), channel_id=1, source_target_pairs={{0,16},{16,0},{1,17},{17,1},{2,18},{18,2},{3,19},{19,3},{4,20},{20... | collective-permute-start | bytes 12582920 | tf_op jit(solution)/shard_map/ppermute | solution.py:46
  385.3 45.8 %collective-permute-start.40 = (bf16[4,128,1024]{2,1,0:T(8,128)(2,1)}, bf16[4,128,1024]{2,1,0:T(8,128)(2,1)}, u32[]{:S(2)}, u32[]{:S(2)}) collective-permute-start(bf16[4,128,1024]{2,1,0:T(8,128)(2,1)} %get-tuple-element.804), channel_id=1, source_target_pairs={{0,1},{1,0},{2,3},{3,2},{4,5},{5,4},{6,7},{7,6},{8,9},{9,8},{10,11... | collective-permute-start | bytes 3145736 | tf_op jit(solution)/shard_map/ppermute | solution.py:50
  387.0 44.1 %collective-permute-start.41 = (bf16[4,128,1024]{2,1,0:T(8,128)(2,1)}, bf16[4,128,1024]{2,1,0:T(8,128)(2,1)}, u32[]{:S(2)}, u32[]{:S(2)}) collective-permute-start(bf16[4,128,1024]{2,1,0:T(8,128)(2,1)} %get-tuple-element.805), channel_id=1, source_target_pairs={{0,2},{2,0},{1,3},{3,1},{4,6},{6,4},{5,7},{7,5},{8,10},{10,8},{9,1... | collective-permute-start | bytes 3145736 | tf_op jit(solution)/shard_map/ppermute | solution.py:50
  460.3 102.7 %reduce-scatter.9.cloned.1.call-start = ((), (), s32[]{:S(2)}) async-start(), calls=%async_computation.7 | async-start | bytes 1310720 | tf_op jit(solution)/shard_map/reduce_scatter | solution.py:152
  465.1 191.6 %reduce-scatter.11.cloned.1.call-start = ((), (), s32[]{:S(2)}) async-start(), calls=%async_computation.8 | async-start | bytes 1310720 | tf_op jit(solution)/shard_map/reduce_scatter | solution.py:152
  484.1 60.4 %collective-permute-start.52 = (bf16[4,128,1024]{2,1,0:T(8,128)(2,1)}, bf16[4,128,1024]{2,1,0:T(8,128)(2,1)}, u32[]{:S(2)}, u32[]{:S(2)}) collective-permute-start(bf16[4,128,1024]{2,1,0:T(8,128)(2,1)} %get-tuple-element.920), channel_id=1, source_target_pairs={{0,1},{1,0},{2,3},{3,2},{4,5},{5,4},{6,7},{7,6},{8,9},{9,8},{10,11... | collective-permute-start | bytes 3145736 | tf_op jit(solution)/shard_map/ppermute | solution.py:50
  485.5 60.0 %collective-permute-start.53 = (bf16[4,128,1024]{2,1,0:T(8,128)(2,1)}, bf16[4,128,1024]{2,1,0:T(8,128)(2,1)}, u32[]{:S(2)}, u32[]{:S(2)}) collective-permute-start(bf16[4,128,1024]{2,1,0:T(8,128)(2,1)} %get-tuple-element.921), channel_id=1, source_target_pairs={{0,2},{2,0},{1,3},{3,1},{4,6},{6,4},{5,7},{7,5},{8,10},{10,8},{9,1... | collective-permute-start | bytes 3145736 | tf_op jit(solution)/shard_map/ppermute | solution.py:50
  486.7 34.9 %collective-permute-start.50 = (bf16[2,144,1024]{2,1,0:T(8,128)(2,1)S(1)}, bf16[2,144,1024]{2,1,0:T(8,128)(2,1)S(1)}, u32[]{:S(2)}, u32[]{:S(2)}) collective-permute-start(bf16[2,144,1024]{2,1,0:T(8,128)(2,1)S(1)} %get-tuple-element.895), channel_id=1, source_target_pairs={{0,1},{1,0},{2,3},{3,2},{4,5},{5,4},{6,7},{7,6},{8,9},{9,8},{10,11... | collective-permute-start | bytes 1769480 | tf_op jit(solution)/shard_map/ppermute | solution.py:50
  487.4 34.8 %collective-permute-start.51 = (bf16[2,144,1024]{2,1,0:T(8,128)(2,1)S(1)}, bf16[2,144,1024]{2,1,0:T(8,128)(2,1)S(1)}, u32[]{:S(2)}, u32[]{:S(2)}) collective-permute-start(bf16[2,144,1024]{2,1,0:T(8,128)(2,1)S(1)} %get-tuple-element.896), channel_id=1, source_target_pairs={{0,2},{2,0},{1,3},{3,1},{4,6},{6,4},{5,7},{7,5},{8,10},{10,8},{9,1... | collective-permute-start | bytes 1769480 | tf_op jit(solution)/shard_map/ppermute | solution.py:50
  524.4 34.1 %collective-permute-start.54 = (bf16[4,144,1024]{2,1,0:T(8,128)(2,1)}, bf16[4,144,1024]{2,1,0:T(8,128)(2,1)}, u32[]{:S(2)}, u32[]{:S(2)}) collective-permute-start(bf16[4,144,1024]{2,1,0:T(8,128)(2,1)} %get-tuple-element.940), channel_id=1, source_target_pairs={{0,1},{1,0},{2,3},{3,2},{4,5},{5,4},{6,7},{7,6},{8,9},{9,8},{10,11... | collective-permute-start | bytes 3538952 | tf_op jit(solution)/shard_map/ppermute | solution.py:50
  526.3 36.6 %collective-permute-start.56 = (bf16[2,128,1024]{2,1,0:T(8,128)(2,1)}, bf16[2,128,1024]{2,1,0:T(8,128)(2,1)}, u32[]{:S(2)}, u32[]{:S(2)}) collective-permute-start(bf16[2,128,1024]{2,1,0:T(8,128)(2,1)} %copy-done.66), channel_id=1, source_target_pairs={{0,1},{1,0},{2,3},{3,2},{4,5},{5,4},{6,7},{7,6},{8,9},{9,8},{10,11... | collective-permute-start | bytes 1572872 | tf_op jit(solution)/shard_map/ppermute | solution.py:50
  558.3 104.1 %reduce-scatter.15.cloned.1.call-start = ((), (), s32[]{:S(2)}) async-start(), calls=%async_computation.10 | async-start | bytes 1310720 | tf_op jit(solution)/shard_map/reduce_scatter | solution.py:152
  591.1 76.6 %reduce-scatter.13.cloned.1.call-start = ((), (), s32[]{:S(2)}) async-start(), calls=%async_computation.9 | async-start | bytes 1474560 | tf_op jit(solution)/shard_map/reduce_scatter | solution.py:152
  594.5 87.6 %reduce-scatter.17.cloned.1.call-start = ((), (), s32[]{:S(2)}) async-start(), calls=%async_computation.11 | async-start | bytes 1474560 | tf_op jit(solution)/shard_map/reduce_scatter | solution.py:152
  (163 other events, 1827.8 us)
Sparse Core Ops, SparseCore 0:
  26.3 35.3 all-gather.12
  63.8 26.9 all-gather.14
  93.8 26.4 all-gather.16
  135.2 26.9 all-gather.18
  164.2 27.4 all-gather.20
  193.6 27.4 all-gather.22
  460.4 25.6 reduce-scatter.6
  489.0 25.7 reduce-scatter.8
  558.4 25.8 reduce-scatter.10
  591.3 26.3 reduce-scatter.14
  620.0 27.8 reduce-scatter.12
  654.3 27.7 reduce-scatter.16

commit v5 on v4

--- a/solution.py
+++ b/solution.py
@@ -772,16 +772,16 @@
             lowered[4], ((0, SLABS - count_vectors), (0, width - lowered[4].shape[1]))
         )
         pairs[0] = (spread, spread)
-        names = list(pairs)
-        here = jnp.concatenate([choose(pairs[name])[0] for name in names], axis=0)
-        there = jnp.concatenate([choose(pairs[name])[1] for name in names], axis=0)
-        both = swap_halves(here, there, first)
-        start = 0
-        for name in names:
-            stop = start + pairs[name][0].shape[0]
-            for layer in range(2):
-                parts[layer][name] = both[layer][start:stop]
-            start = stop
+        for names in ((1, 0), (3, 2)):
+            here = jnp.concatenate([choose(pairs[name])[0] for name in names], axis=0)
+            there = jnp.concatenate([choose(pairs[name])[1] for name in names], axis=0)
+            both = swap_halves(here, there, first)
+            start = 0
+            for name in names:
+                stop = start + pairs[name][0].shape[0]
+                for layer in range(2):
+                    parts[layer][name] = both[layer][start:stop]
+                start = stop
     else:
         for name in pairs:
             parts[0][name], parts[1][name] = swap_halves(*choose(pairs[name]), first)

time: 748 us -> 743 us (level)
  waiting for transfers between devices: 212 us -> 200 us
    unnamed x225 -> x213, local copies, waits for them, and re-layouts: 37.9 us -> 36.4 us
  transfers between devices with their start and end apart: 88 -> 89, of which waited for: 39 -> 40; matrix products, arithmetic and copies ran while one was open for 19% -> 22% of each run, Pallas kernels for 29% -> 30%
where the time goes in v5:
time: 743 us; the launch traced here: 731 us
  Pallas kernels  217 us (29%)
  waiting for transfers between devices  200 us (27%)
  local copies, waits for them, and re-layouts  153 us (21%)
  other arithmetic  71.4 us (10%)
  starting transfers between devices  65.1 us (9%)
  between operations  25 us (3%)
    ppermute x50, waiting for transfers between devices, flip(): return lax.ppermute(x, axis, [(0, 1), (1, 0)])  122 us
    all_gather x6, waiting for transfers between devices, gather_flow(): column = lax.all_gather(part, Z, axis=0, tiled=False)  57.6 us
    ppermute x50, starting transfers between devices, flip(): return lax.ppermute(x, axis, [(0, 1), (1, 0)])  56.2 us
    pallas_call x6, Pallas kernels, weight_grad(): pl.pallas_call(functools.partial(grad_kernel, pairs, len(own), extra is n...  50.2 us
    pallas_call x6, Pallas kernels, project(): pl.pallas_call(functools.partial(project_kernel, smooth, count), grid=(2...  43.2 us
    unnamed x213, local copies, waits for them, and re-layouts  36.4 us
    dynamic_update_slice x18, local copies, waits for them, and re-layouts, place_blocks(): full = lax.dynamic_update_slice(full, jnp.expand_dims(block, axis), start)  31.8 us
    pallas_call x2, Pallas kernels, attend_back(): pl.pallas_call(attend_back_kernel, grid=(groups,), in_specs=[third_at(thi...  29 us
  transfers between devices with their start and end apart: 89, of which 40 were waited for; matrix products, arithmetic and copies ran while one was open for 22% of the time, Pallas kernels for 30%

profile of v5, /device:TPU:0, one launch (start us, length us, event | category | flops | bytes accessed | tf_op | source)
XLA Modules:
  0.0 731.4 jit_solution(6527313530222607529)
XLA Ops:
  29.0 28.9 %all-gather.13.cloned.1.call-done = bf16[640,1024]{1,0:T(8,128)(2,1)} async-done(((bf16[160,1024]{1,0:T(8,128)(2,1)}), bf16[640,1024]{1,0:T(8,128)(2,1)}) %all-gather.13.cloned.1.call-update) | async-done | bytes 1310736 | tf_op jit(solution)/shard_map/all_gather | solution.py:99
  60.9 26.2 %all-gather.15.cloned.1.call-done = bf16[512,1024]{1,0:T(8,128)(2,1)} async-done(((bf16[128,1024]{1,0:T(8,128)(2,1)}), bf16[512,1024]{1,0:T(8,128)(2,1)}) %all-gather.15.cloned.1.call-update) | async-done | bytes 1048592 | tf_op jit(solution)/shard_map/all_gather | solution.py:99
  102.0 11.4 %collective-permute-done.5 = bf16[4,128,1024]{2,1,0:T(8,128)(2,1)} collective-permute-done((bf16[4,128,1024]{2,1,0:T(8,128)(2,1)}, bf16[4,128,1024]{2,1,0:T(8,128)(2,1)}, u32[]{:S(2)}, u32[]{:S(2)}) %collective-permute-start.5) | collective-permute-done | bytes 1048608 | tf_op jit(solution)/shard_map/ppermute | solution.py:50
  141.3 7.2 project.6
  148.5 10.4 %collective-permute-done.10 = bf16[4,128,1024]{2,1,0:T(8,128)(2,1)} collective-permute-done((bf16[4,128,1024]{2,1,0:T(8,128)(2,1)}, bf16[4,128,1024]{2,1,0:T(8,128)(2,1)}, u32[]{:S(2)}, u32[]{:S(2)}) %collective-permute-start.10) | collective-permute-done | bytes 1048608 | tf_op jit(solution)/shard_map/ppermute | solution.py:50
  217.4 8.5 %collective-permute-done.18 = bf16[4,128,1024]{2,1,0:T(8,128)(2,1)} collective-permute-done((bf16[4,128,1024]{2,1,0:T(8,128)(2,1)}, bf16[4,128,1024]{2,1,0:T(8,128)(2,1)}, u32[]{:S(2)}, u32[]{:S(2)}) %collective-permute-start.18) | collective-permute-done | bytes 1048608 | tf_op jit(solution)/shard_map/ppermute | solution.py:50
  244.0 11.3 %project.8 = (bf16[2,400,2048]{2,1,0:T(8,128)(2,1)S(1)}, bf16[2,400,2048]{2,1,0:T(8,128)(2,1)}) custom-call(bf16[400,1024]{1,0:T(8,128)(2,1)S(1)} %add_convert_fusion.7.x_ref.refs_0_, bf16[16,128,1024]{2,1,0:T(8,128)(2,1)} %bitcast.41.here_ref.refs_1_, bf16[16,128,1024]{2,1,0:T(8,128)(2,1)} %collective-permute-done.21.there_ref.refs_2_, ...), custom_call_target="tpu_custom_call" | custom-call | flops 3355443200 | bytes 8388608 | tf_op jit(solution)/shard_map/project/pallas_call | solution.py:349
  260.7 12.2 %collective-permute-done.23 = bf16[2,128,1024]{2,1,0:T(8,128)(2,1)} collective-permute-done((bf16[2,128,1024]{2,1,0:T(8,128)(2,1)}, bf16[2,128,1024]{2,1,0:T(8,128)(2,1)}, u32[]{:S(2)}, u32[]{:S(2)}) %collective-permute-start.23) | collective-permute-done | bytes 524320 | tf_op jit(solution)/shard_map/ppermute | solution.py:50
  280.4 6.4 output.2.inputs
  287.8 7.1 project.9
  294.9 6.2 attend.3
  325.5 11.2 %project.11 = (bf16[2,400,2048]{2,1,0:T(8,128)(2,1)S(1)}, bf16[2,400,2048]{2,1,0:T(8,128)(2,1)}) custom-call(bf16[400,1024]{1,0:T(8,128)(2,1)S(1)} %copy-done.36, bf16[16,128,1024]{2,1,0:T(8,128)(2,1)} %bitcast.79.here_ref.refs_1_, bf16[16,128,1024]{2,1,0:T(8,128)(2,1)} %collective-permute-done.30.there_ref.refs_2_, f32[2,1,2048]{2,1,0:T(1,128)S(1)} %pad_maximum_fusion.16.b_ref), custom_call_target="tpu_custom_call" | custom-call | flops 3355443200 | bytes 8388608 | tf_op jit(solution)/shard_map/project/pallas_call | solution.py:349
  342.4 9.8 %active.2 = (bf16[2,400,2048]{2,1,0:T(8,128)(2,1)S(1)}, f32[2,1,2048]{2,1,0:T(1,128)S(1)}) custom-call(bf16[400,1024]{1,0:T(8,128)(2,1)S(1)} %get-tuple-element.746.up_ref.refs_1_.refs_5_, bf16[16,128,1024]{2,1,0:T(8,128)(2,1)} %bitcast.106.w_here, bf16[16,128,1024]{2,1,0:T(8,128)(2,1)} %collective-permute-done.34.w_there, ...), custom_call_target="tpu_custom_call" | custom-call | flops 3355443200 | bytes 12582912 | tf_op jit(solution)/shard_map/active/pallas_call | solution.py:415
  353.8 7.8 %grad.6 = (bf16[2,128,1024]{2,1,0:T(8,128)(2,1)}, bf16[2,128,1024]{2,1,0:T(8,128)(2,1)}, bf16[4,128,1024]{2,1,0:T(8,128)(2,1)S(1)}, bf16[4,128,1024]{2,1,0:T(8,128)(2,1)}, bf16[4,128,1024]{2,1,0:T(8,128)(2,1)}) custom-call(s32[1]{0:T(128)} %bitcast.112.chip, bf16[2,400,2048]{2,1,0:T(8,128)(2,1)} %copy-done.26, ...), custom_call_target="tpu_custom_call" | custom-call | flops 3355443200 | bytes 8388608 | tf_op jit(solution)/shard_map/grad/pallas_call | solution.py:642
  364.4 10.7 %middle.2 = (f32[400,1024]{1,0:T(8,128)S(1)}, bf16[2,400,512]{2,1,0:T(8,128)(2,1)S(1)}, bf16[2,400,512]{2,1,0:T(8,128)(2,1)S(1)}, f32[8,1024]{1,0:T(8,128)S(1)}) custom-call(s32[1]{0:T(128)} %bitcast.113.place, bf16[2,400,2048]{2,1,0:T(8,128)(2,1)} %copy-done.32, bf16[16,128,1024]{2,1,0:T(8,128)(2,1)} %bitcast.79.here_ref.refs_1_, ...), custom_call_target="tpu_custom_call" | custom-call | flops 4194304000 | bytes 8388608 | tf_op jit(solution)/shard_map/middle/pallas_call | solution.py:488
  384.3 8.7 %grad.7 = (bf16[2,128,1024]{2,1,0:T(8,128)(2,1)}, bf16[2,128,1024]{2,1,0:T(8,128)(2,1)}, bf16[4,128,1024]{2,1,0:T(8,128)(2,1)S(1)}, bf16[4,128,1024]{2,1,0:T(8,128)(2,1)}, bf16[4,128,1024]{2,1,0:T(8,128)(2,1)}) custom-call(s32[1]{0:T(128)} %bitcast.112.chip, bf16[400,1024]{1,0:T(8,128)(2,1)S(1)} %copy-done.37, bf16[2,400,2048]{2,1,0:T(8,128)(2,1)} %copy-done.32, ...), custom_call_target="tpu_custom_call" | custom-call | flops 3355443200 | bytes 8388608 | tf_op jit(solution)/shard_map/grad/pallas_call | solution.py:642
  394.0 14.5 %attend_back.2 = bf16[4,200,2048]{2,1,0:T(8,128)(2,1)} custom-call(bf16[4,200,1536]{2,1,0:T(8,128)(2,1)S(1)} %bitcast.451, bf16[4,200,1536]{2,1,0:T(8,128)(2,1)S(1)} %bitcast.452, bf16[4,200,1536]{2,1,0:T(8,128)(2,1)S(1)} %bitcast.453, bf16[4,200,512]{2,1,0:T(8,128)(2,1)S(1)} %bitcast.461, bf16[4,200,512]{2,1,0:T(8,128)(2,1)S(1)} %bitcast.460), custom_call_target="tpu_custom_call" | custom-call | flops 1638400000 | bytes 5734400 | tf_op jit(solution)/shard_map/attend_back/pallas_call | solution.py:283
  410.3 8.5 %entry.2 = (bf16[400,1024]{1,0:T(8,128)(2,1)S(1)}, f32[8,1024]{1,0:T(8,128)S(1)}, f32[2,1,1536]{2,1,0:T(1,128)S(1)}) custom-call(bf16[2,400,2048]{2,1,0:T(8,128)(2,1)} %bitcast.467, bf16[16,128,1024]{2,1,0:T(8,128)(2,1)} %bitcast.35.here_ref.refs_6_.w_here, bf16[16,128,1024]{2,1,0:T(8,128)(2,1)} %collective-permute-done.25.there_ref.refs_7_.w_there, ...), custom_call_target="tpu_custom_call" | custom-call | flops 2516582400 | bytes 6291456 | tf_op jit(solution)/shard_map/entry/pallas_call | solution.py:538
  431.9 9.6 %active.3 = (bf16[2,400,2048]{2,1,0:T(8,128)(2,1)S(1)}, f32[2,1,2048]{2,1,0:T(1,128)S(1)}) custom-call(bf16[400,1024]{1,0:T(8,128)(2,1)S(1)} %copy-done.13, bf16[16,128,1024]{2,1,0:T(8,128)(2,1)} %bitcast.72.w_here, bf16[16,128,1024]{2,1,0:T(8,128)(2,1)} %collective-permute-done.26.w_there, bf16[2,400,2048]{2,1,0:T(8,128)(2,1)} %get-tuple-element.815.slope_ref), custom_call_target="tpu_custom_call" | custom-call | flops 3355443200 | bytes 12582912 | tf_op jit(solution)/shard_map/active/pallas_call | solution.py:415
  443.3 7.8 %grad.8 = (bf16[2,128,1024]{2,1,0:T(8,128)(2,1)S(1)}, bf16[2,128,1024]{2,1,0:T(8,128)(2,1)S(1)}, bf16[4,128,1024]{2,1,0:T(8,128)(2,1)S(1)}, bf16[4,128,1024]{2,1,0:T(8,128)(2,1)}, bf16[4,128,1024]{2,1,0:T(8,128)(2,1)}) custom-call(s32[1]{0:T(128)} %bitcast.112.chip, bf16[2,400,2048]{2,1,0:T(8,128)(2,1)} %copy-done.28, bf16[400,1024]{1,0:T(8,128)(2,1)S(1)} %copy-done.13, ...), custom_call_target="tpu_custom_call" | custom-call | flops 3355443200 | bytes 8388608 | tf_op jit(solution)/shard_map/grad/pallas_call | solution.py:642
  468.7 8.7 %grad.9 = (bf16[2,144,1024]{2,1,0:T(8,128)(2,1)S(1)}, bf16[2,144,1024]{2,1,0:T(8,128)(2,1)S(1)}, bf16[4,144,1024]{2,1,0:T(8,128)(2,1)S(1)}, bf16[4,144,1024]{2,1,0:T(8,128)(2,1)}, bf16[4,144,1024]{2,1,0:T(8,128)(2,1)}) custom-call(s32[1]{0:T(128)} %bitcast.112.chip, bf16[400,1024]{1,0:T(8,128)(2,1)S(1)} %copy-done.23, bf16[400,1024]{1,0:T(8,128)(2,1)S(1)} %copy-done.25, ...), custom_call_target="tpu_custom_call" | custom-call | flops 3774873600 | bytes 9437184 | tf_op jit(solution)/shard_map/grad/pallas_call | solution.py:642
  485.0 8.4 %grad.10 = (bf16[2,128,1024]{2,1,0:T(8,128)(2,1)S(1)}, bf16[2,128,1024]{2,1,0:T(8,128)(2,1)}, bf16[4,128,1024]{2,1,0:T(8,128)(2,1)S(1)}, bf16[4,128,1024]{2,1,0:T(8,128)(2,1)S(1)}, bf16[4,128,1024]{2,1,0:T(8,128)(2,1)S(1)}) custom-call(s32[1]{0:T(128)} %bitcast.112.chip, bf16[400,1024]{1,0:T(8,128)(2,1)S(1)} %copy-done.34, bf16[2,400,2048]{2,1,0:T(8,128)(2,1)} %copy-done.30, ...), custom_call_target="tpu_custom_call" | custom-call | flops 3355443200 | bytes 8388608 | tf_op jit(solution)/shard_map/grad/pallas_call | solution.py:642
  496.1 10.4 %middle.3 = (f32[400,1024]{1,0:T(8,128)S(1)}, bf16[2,400,512]{2,1,0:T(8,128)(2,1)S(1)}, bf16[2,400,512]{2,1,0:T(8,128)(2,1)S(1)}, f32[8,1024]{1,0:T(8,128)S(1)}) custom-call(s32[1]{0:T(128)} %bitcast.113.place, bf16[2,400,2048]{2,1,0:T(8,128)(2,1)} %copy-done.30, bf16[16,128,1024]{2,1,0:T(8,128)(2,1)} %bitcast.41.here_ref.refs_1_, ...), custom_call_target="tpu_custom_call" | custom-call | flops 4194304000 | bytes 8388608 | tf_op jit(solution)/shard_map/middle/pallas_call | solution.py:488
  509.5 8.5 %collective-permute-done.51.from_across = bf16[2,144,1024]{2,1,0:T(8,128)(2,1)S(1)} collective-permute-done((bf16[2,144,1024]{2,1,0:T(8,128)(2,1)S(1)}, bf16[2,144,1024]{2,1,0:T(8,128)(2,1)S(1)}, u32[]{:S(2)}, u32[]{:S(2)}) %collective-permute-start.51) | collective-permute-done | bytes 589856 | tf_op jit(solution)/shard_map/ppermute | solution.py:50
  526.5 14.5 %attend_back.3 = bf16[4,200,2048]{2,1,0:T(8,128)(2,1)} custom-call(bf16[4,200,1536]{2,1,0:T(8,128)(2,1)S(1)} %bitcast.445, bf16[4,200,1536]{2,1,0:T(8,128)(2,1)S(1)} %bitcast.446, bf16[4,200,1536]{2,1,0:T(8,128)(2,1)S(1)} %bitcast.447, bf16[4,200,512]{2,1,0:T(8,128)(2,1)S(1)} %bitcast.463, bf16[4,200,512]{2,1,0:T(8,128)(2,1)S(1)} %bitcast.462), custom_call_target="tpu_custom_call" | custom-call | flops 1638400000 | bytes 5734400 | tf_op jit(solution)/shard_map/attend_back/pallas_call | solution.py:283
  545.2 8.8 %entry.3 = (bf16[400,1024]{1,0:T(8,128)(2,1)S(1)}, f32[8,1024]{1,0:T(8,128)S(1)}, f32[2,1,1536]{2,1,0:T(1,128)S(1)}) custom-call(bf16[2,400,2048]{2,1,0:T(8,128)(2,1)} %bitcast.464, bf16[16,160,1024]{2,1,0:T(8,128)(2,1)} %bitcast.21.here_ref.refs_6_.w_here, bf16[16,160,1024]{2,1,0:T(8,128)(2,1)} %collective-permute-done.8.there_ref.refs_7_.w_there, ...), custom_call_target="tpu_custom_call" | custom-call | flops 2516582400 | bytes 6291456 | tf_op jit(solution)/shard_map/entry/pallas_call | solution.py:538
  562.6 20.1 %collective-permute-done.66 = bf16[4,128,1024]{2,1,0:T(8,128)(2,1)S(1)} collective-permute-done((bf16[4,128,1024]{2,1,0:T(8,128)(2,1)S(1)}, bf16[4,128,1024]{2,1,0:T(8,128)(2,1)S(1)}, u32[]{:S(2)}, u32[]{:S(2)}) %collective-permute-start.66) | collective-permute-done | bytes 1048608 | tf_op jit(solution)/shard_map/ppermute | solution.py:50
  591.8 8.7 %grad.11 = (bf16[2,144,1024]{2,1,0:T(8,128)(2,1)S(1)}, bf16[2,144,1024]{2,1,0:T(8,128)(2,1)S(1)}, bf16[4,144,1024]{2,1,0:T(8,128)(2,1)S(1)}, bf16[4,144,1024]{2,1,0:T(8,128)(2,1)S(1)}, bf16[4,144,1024]{2,1,0:T(8,128)(2,1)}) custom-call(s32[1]{0:T(128)} %bitcast.112.chip, bf16[400,1024]{1,0:T(8,128)(2,1)S(1)} %copy-done.19, bf16[400,1024]{1,0:T(8,128)(2,1)S(1)} %copy-done.21, ...), custom_call_target="tpu_custom_call" | custom-call | flops 3774873600 | bytes 9437184 | tf_op jit(solution)/shard_map/grad/pallas_call | solution.py:642
  602.7 13.2 %collective-permute-done.61.from_across = bf16[2,144,1024]{2,1,0:T(8,128)(2,1)S(1)} collective-permute-done((bf16[2,144,1024]{2,1,0:T(8,128)(2,1)S(1)}, bf16[2,144,1024]{2,1,0:T(8,128)(2,1)S(1)}, u32[]{:S(2)}, u32[]{:S(2)}) %collective-permute-start.61) | collective-permute-done | bytes 589856 | tf_op jit(solution)/shard_map/ppermute | solution.py:50
  620.5 6.7 output.3
  628.6 16.6 %collective-permute-done.68 = bf16[4,144,1024]{2,1,0:T(8,128)(2,1)S(1)} collective-permute-done((bf16[4,144,1024]{2,1,0:T(8,128)(2,1)S(1)}, bf16[4,144,1024]{2,1,0:T(8,128)(2,1)S(1)}, u32[]{:S(2)}, u32[]{:S(2)}) %collective-permute-start.68) | collective-permute-done | bytes 1179680 | tf_op jit(solution)/shard_map/ppermute | solution.py:50
  668.8 7.0 reduce-scatter.17.cloned.1.call-done
  (634 shorter events, 350.1 us)
Async XLA Ops:
  7.2 50.7 %all-gather.13.cloned.1.call-start = ((), (), s32[]{:S(2)}) async-start(), calls=%async_computation.12 | async-start | bytes 1638400 | tf_op jit(solution)/shard_map/all_gather | solution.py:99
  22.7 64.4 %all-gather.15.cloned.1.call-start = ((), (), s32[]{:S(2)}) async-start(), calls=%async_computation.13 | async-start | bytes 1310720 | tf_op jit(solution)/shard_map/all_gather | solution.py:99
  29.0 97.8 %all-gather.17.cloned.1.call-start = ((), (), s32[]{:S(2)}) async-start(), calls=%async_computation.14 | async-start | bytes 1310720 | tf_op jit(solution)/shard_map/all_gather | solution.py:99
  90.0 88.3 %all-gather.19.cloned.1.call-start = ((), (), s32[]{:S(2)}) async-start(), calls=%async_computation.15 | async-start | bytes 1310720 | tf_op jit(solution)/shard_map/all_gather | solution.py:99
  92.9 34.4 %collective-permute-start.6 = (bf16[2,160,1024]{2,1,0:T(8,128)(2,1)}, bf16[2,160,1024]{2,1,0:T(8,128)(2,1)}, u32[]{:S(2)}, u32[]{:S(2)}) collective-permute-start(bf16[2,160,1024]{2,1,0:T(8,128)(2,1)} %slice.384), channel_id=1, source_target_pairs={{0,1},{1,0},{2,3},{3,2},{4,5},{5,4},{6,7},{7,6},{8,9},{9,8},{10,11... | collective-permute-start | bytes 1966088 | tf_op jit(solution)/shard_map/ppermute | solution.py:50
  131.4 56.6 %all-gather.21.cloned.1.call-start = ((), (), s32[]{:S(2)}) async-start(), calls=%async_computation.16 | async-start | bytes 1310720 | tf_op jit(solution)/shard_map/all_gather | solution.py:99
  132.0 85.4 %all-gather.23.cloned.1.call-start = ((), (), s32[]{:S(2)}) async-start(), calls=%async_computation.17 | async-start | bytes 1310720 | tf_op jit(solution)/shard_map/all_gather | solution.py:99
  132.5 391.7 %reduce-scatter.7.cloned.1.call-start = ((), (), s32[]{:S(2)}) async-start(), calls=%async_computation.6 | async-start | bytes 1310720 | tf_op jit(solution)/shard_map/reduce_scatter | solution.py:152
  134.6 39.9 %collective-permute-start.11 = (bf16[2,128,1024]{2,1,0:T(8,128)(2,1)}, bf16[2,128,1024]{2,1,0:T(8,128)(2,1)}, u32[]{:S(2)}, u32[]{:S(2)}) collective-permute-start(bf16[2,128,1024]{2,1,0:T(8,128)(2,1)} %slice.386), channel_id=1, source_target_pairs={{0,1},{1,0},{2,3},{3,2},{4,5},{5,4},{6,7},{7,6},{8,9},{9,8},{10,11... | collective-permute-start | bytes 1572872 | tf_op jit(solution)/shard_map/ppermute | solution.py:50
  135.2 39.3 %collective-permute-start.12 = (bf16[2,128,1024]{2,1,0:T(8,128)(2,1)}, bf16[2,128,1024]{2,1,0:T(8,128)(2,1)}, u32[]{:S(2)}, u32[]{:S(2)}) collective-permute-start(bf16[2,128,1024]{2,1,0:T(8,128)(2,1)} %slice.387), channel_id=1, source_target_pairs={{0,2},{2,0},{1,3},{3,1},{4,6},{6,4},{5,7},{7,5},{8,10},{10,8},{9,1... | collective-permute-start | bytes 1572872 | tf_op jit(solution)/shard_map/ppermute | solution.py:50
  187.9 38.0 %collective-permute-start.18 = (bf16[4,128,1024]{2,1,0:T(8,128)(2,1)}, bf16[4,128,1024]{2,1,0:T(8,128)(2,1)}, u32[]{:S(2)}, u32[]{:S(2)}) collective-permute-start(bf16[4,128,1024]{2,1,0:T(8,128)(2,1)} %bitcast.490), channel_id=1, source_target_pairs={{0,2},{2,0},{1,3},{3,1},{4,6},{6,4},{5,7},{7,5},{8,10},{10,8},{9,1... | collective-permute-start | bytes 3145736 | tf_op jit(solution)/shard_map/ppermute | solution.py:50
  189.4 38.0 %collective-permute-start.17 = (bf16[4,128,1024]{2,1,0:T(8,128)(2,1)}, bf16[4,128,1024]{2,1,0:T(8,128)(2,1)}, u32[]{:S(2)}, u32[]{:S(2)}) collective-permute-start(bf16[4,128,1024]{2,1,0:T(8,128)(2,1)} %bitcast.491), channel_id=1, source_target_pairs={{0,1},{1,0},{2,3},{3,2},{4,5},{5,4},{6,7},{7,6},{8,9},{9,8},{10,11... | collective-permute-start | bytes 3145736 | tf_op jit(solution)/shard_map/ppermute | solution.py:50
  201.0 41.6 %collective-permute-start.21 = (bf16[16,128,1024]{2,1,0:T(8,128)(2,1)}, bf16[16,128,1024]{2,1,0:T(8,128)(2,1)}, u32[]{:S(2)}, u32[]{:S(2)}) collective-permute-start(bf16[16,128,1024]{2,1,0:T(8,128)(2,1)} %bitcast.41.here_ref.refs_1_), channel_id=1, source_target_pairs={{0,16},{16,0},{1,17},{17,1},{2,18},{18,2},{3,19},{19,3},{4,20},{20... | collective-permute-start | bytes 12582920 | tf_op jit(solution)/shard_map/ppermute | solution.py:46
  204.7 73.8 %collective-permute-start.25 = (bf16[16,128,1024]{2,1,0:T(8,128)(2,1)}, bf16[16,128,1024]{2,1,0:T(8,128)(2,1)}, u32[]{:S(2)}, u32[]{:S(2)}) collective-permute-start(bf16[16,128,1024]{2,1,0:T(8,128)(2,1)} %bitcast.35.here_ref.refs_6_.w_here), channel_id=1, source_target_pairs={{0,16},{16,0},{1,17},{17,1},{2,18},{18,2},{3,19},{19,3},{4,20},{20... | collective-permute-start | bytes 12582920 | tf_op jit(solution)/shard_map/ppermute | solution.py:46
  205.1 37.5 %collective-permute-start.22 = (bf16[3,400,1024]{2,1,0:T(8,128)(2,1)}, bf16[3,400,1024]{2,1,0:T(8,128)(2,1)}, u32[]{:S(2)}, u32[]{:S(2)}) collective-permute-start(bf16[3,400,1024]{2,1,0:T(8,128)(2,1)} %pad_maximum_fusion), channel_id=1, source_target_pairs={{0,16},{16,0},{1,17},{17,1},{2,18},{18,2},{3,19},{19,3},{4,20},{20... | collective-permute-start | bytes 7372808 | tf_op jit(solution)/shard_map/ppermute | solution.py:46
  242.6 35.9 %collective-permute-start.26 = (bf16[16,128,1024]{2,1,0:T(8,128)(2,1)}, bf16[16,128,1024]{2,1,0:T(8,128)(2,1)}, u32[]{:S(2)}, u32[]{:S(2)}) collective-permute-start(bf16[16,128,1024]{2,1,0:T(8,128)(2,1)} %bitcast.72.w_here), channel_id=1, source_target_pairs={{0,16},{16,0},{1,17},{17,1},{2,18},{18,2},{3,19},{19,3},{4,20},{20... | collective-permute-start | bytes 12582920 | tf_op jit(solution)/shard_map/ppermute | solution.py:46
  273.0 34.6 %collective-permute-start.29 = (bf16[4,128,1024]{2,1,0:T(8,128)(2,1)}, bf16[4,128,1024]{2,1,0:T(8,128)(2,1)S(1)}, u32[]{:S(2)}, u32[]{:S(2)}) collective-permute-start(bf16[4,128,1024]{2,1,0:T(8,128)(2,1)} %bitcast.61), channel_id=1, source_target_pairs={{0,2},{2,0},{1,3},{3,1},{4,6},{6,4},{5,7},{7,5},{8,10},{10,8},{9,1... | collective-permute-start | bytes 3145736 | tf_op jit(solution)/shard_map/ppermute | solution.py:50
  273.5 34.0 %collective-permute-start.28 = (bf16[4,128,1024]{2,1,0:T(8,128)(2,1)}, bf16[4,128,1024]{2,1,0:T(8,128)(2,1)S(1)}, u32[]{:S(2)}, u32[]{:S(2)}) collective-permute-start(bf16[4,128,1024]{2,1,0:T(8,128)(2,1)} %bitcast.61), channel_id=1, source_target_pairs={{0,1},{1,0},{2,3},{3,2},{4,5},{5,4},{6,7},{7,6},{8,9},{9,8},{10,11... | collective-permute-start | bytes 3145736 | tf_op jit(solution)/shard_map/ppermute | solution.py:50
  278.5 38.6 %collective-permute-start.30 = (bf16[16,128,1024]{2,1,0:T(8,128)(2,1)}, bf16[16,128,1024]{2,1,0:T(8,128)(2,1)}, u32[]{:S(2)}, u32[]{:S(2)}) collective-permute-start(bf16[16,128,1024]{2,1,0:T(8,128)(2,1)} %bitcast.79.here_ref.refs_1_), channel_id=1, source_target_pairs={{0,16},{16,0},{1,17},{17,1},{2,18},{18,2},{3,19},{19,3},{4,20},{20... | collective-permute-start | bytes 12582920 | tf_op jit(solution)/shard_map/ppermute | solution.py:46
  382.0 45.7 %collective-permute-start.41 = (bf16[4,128,1024]{2,1,0:T(8,128)(2,1)}, bf16[4,128,1024]{2,1,0:T(8,128)(2,1)}, u32[]{:S(2)}, u32[]{:S(2)}) collective-permute-start(bf16[4,128,1024]{2,1,0:T(8,128)(2,1)} %get-tuple-element.804), channel_id=1, source_target_pairs={{0,1},{1,0},{2,3},{3,2},{4,5},{5,4},{6,7},{7,6},{8,9},{9,8},{10,11... | collective-permute-start | bytes 3145736 | tf_op jit(solution)/shard_map/ppermute | solution.py:50
  383.7 43.9 %collective-permute-start.42 = (bf16[4,128,1024]{2,1,0:T(8,128)(2,1)}, bf16[4,128,1024]{2,1,0:T(8,128)(2,1)}, u32[]{:S(2)}, u32[]{:S(2)}) collective-permute-start(bf16[4,128,1024]{2,1,0:T(8,128)(2,1)} %get-tuple-element.805), channel_id=1, source_target_pairs={{0,2},{2,0},{1,3},{3,1},{4,6},{6,4},{5,7},{7,5},{8,10},{10,8},{9,1... | collective-permute-start | bytes 3145736 | tf_op jit(solution)/shard_map/ppermute | solution.py:50
  456.8 102.2 %reduce-scatter.9.cloned.1.call-start = ((), (), s32[]{:S(2)}) async-start(), calls=%async_computation.7 | async-start | bytes 1310720 | tf_op jit(solution)/shard_map/reduce_scatter | solution.py:152
  461.6 187.6 %reduce-scatter.11.cloned.1.call-start = ((), (), s32[]{:S(2)}) async-start(), calls=%async_computation.8 | async-start | bytes 1310720 | tf_op jit(solution)/shard_map/reduce_scatter | solution.py:152
  480.7 60.3 %collective-permute-start.53 = (bf16[4,128,1024]{2,1,0:T(8,128)(2,1)}, bf16[4,128,1024]{2,1,0:T(8,128)(2,1)}, u32[]{:S(2)}, u32[]{:S(2)}) collective-permute-start(bf16[4,128,1024]{2,1,0:T(8,128)(2,1)} %get-tuple-element.920), channel_id=1, source_target_pairs={{0,1},{1,0},{2,3},{3,2},{4,5},{5,4},{6,7},{7,6},{8,9},{9,8},{10,11... | collective-permute-start | bytes 3145736 | tf_op jit(solution)/shard_map/ppermute | solution.py:50
  482.0 60.0 %collective-permute-start.54 = (bf16[4,128,1024]{2,1,0:T(8,128)(2,1)}, bf16[4,128,1024]{2,1,0:T(8,128)(2,1)}, u32[]{:S(2)}, u32[]{:S(2)}) collective-permute-start(bf16[4,128,1024]{2,1,0:T(8,128)(2,1)} %get-tuple-element.921), channel_id=1, source_target_pairs={{0,2},{2,0},{1,3},{3,1},{4,6},{6,4},{5,7},{7,5},{8,10},{10,8},{9,1... | collective-permute-start | bytes 3145736 | tf_op jit(solution)/shard_map/ppermute | solution.py:50
  483.2 34.8 %collective-permute-start.51 = (bf16[2,144,1024]{2,1,0:T(8,128)(2,1)S(1)}, bf16[2,144,1024]{2,1,0:T(8,128)(2,1)S(1)}, u32[]{:S(2)}, u32[]{:S(2)}) collective-permute-start(bf16[2,144,1024]{2,1,0:T(8,128)(2,1)S(1)} %get-tuple-element.895), channel_id=1, source_target_pairs={{0,1},{1,0},{2,3},{3,2},{4,5},{5,4},{6,7},{7,6},{8,9},{9,8},{10,11... | collective-permute-start | bytes 1769480 | tf_op jit(solution)/shard_map/ppermute | solution.py:50
  484.0 34.8 %collective-permute-start.52 = (bf16[2,144,1024]{2,1,0:T(8,128)(2,1)S(1)}, bf16[2,144,1024]{2,1,0:T(8,128)(2,1)S(1)}, u32[]{:S(2)}, u32[]{:S(2)}) collective-permute-start(bf16[2,144,1024]{2,1,0:T(8,128)(2,1)S(1)} %get-tuple-element.896), channel_id=1, source_target_pairs={{0,2},{2,0},{1,3},{3,1},{4,6},{6,4},{5,7},{7,5},{8,10},{10,8},{9,1... | collective-permute-start | bytes 1769480 | tf_op jit(solution)/shard_map/ppermute | solution.py:50
  521.0 34.1 %collective-permute-start.55 = (bf16[4,144,1024]{2,1,0:T(8,128)(2,1)}, bf16[4,144,1024]{2,1,0:T(8,128)(2,1)}, u32[]{:S(2)}, u32[]{:S(2)}) collective-permute-start(bf16[4,144,1024]{2,1,0:T(8,128)(2,1)} %get-tuple-element.940), channel_id=1, source_target_pairs={{0,1},{1,0},{2,3},{3,2},{4,5},{5,4},{6,7},{7,6},{8,9},{9,8},{10,11... | collective-permute-start | bytes 3538952 | tf_op jit(solution)/shard_map/ppermute | solution.py:50
  522.9 36.2 %collective-permute-start.57 = (bf16[2,128,1024]{2,1,0:T(8,128)(2,1)}, bf16[2,128,1024]{2,1,0:T(8,128)(2,1)}, u32[]{:S(2)}, u32[]{:S(2)}) collective-permute-start(bf16[2,128,1024]{2,1,0:T(8,128)(2,1)} %copy-done.66), channel_id=1, source_target_pairs={{0,1},{1,0},{2,3},{3,2},{4,5},{5,4},{6,7},{7,6},{8,9},{9,8},{10,11... | collective-permute-start | bytes 1572872 | tf_op jit(solution)/shard_map/ppermute | solution.py:50
  554.9 100.2 %reduce-scatter.15.cloned.1.call-start = ((), (), s32[]{:S(2)}) async-start(), calls=%async_computation.10 | async-start | bytes 1310720 | tf_op jit(solution)/shard_map/reduce_scatter | solution.py:152
  584.9 75.5 %reduce-scatter.13.cloned.1.call-start = ((), (), s32[]{:S(2)}) async-start(), calls=%async_computation.9 | async-start | bytes 1474560 | tf_op jit(solution)/shard_map/reduce_scatter | solution.py:152
  588.3 87.5 %reduce-scatter.17.cloned.1.call-start = ((), (), s32[]{:S(2)}) async-start(), calls=%async_computation.11 | async-start | bytes 1474560 | tf_op jit(solution)/shard_map/reduce_scatter | solution.py:152
  (158 other events, 1832.9 us)
Sparse Core Ops, SparseCore 0:
  22.8 35.0 all-gather.12
  60.1 26.9 all-gather.14
  90.1 26.4 all-gather.16
  131.5 26.9 all-gather.18
  160.5 27.4 all-gather.20
  189.9 27.4 all-gather.22
  456.9 25.7 reduce-scatter.6
  485.6 25.8 reduce-scatter.8
  555.0 25.7 reduce-scatter.10
  585.0 26.1 reduce-scatter.14
  613.5 27.8 reduce-scatter.12
  647.9 27.9 reduce-scatter.16
